TPU v7x, 32 devices: a whole 2x2x4 slice. The times are simulated.
32 devices in a mesh: fsdp: 8 (over z, y), tp: 4 (over x, core).
Axes of the slice: x: 2, y: 2, z: 4, core: 2. Of those that a mesh axis runs over, the one named last changes fastest.
Arguments:
- tokens: bfloat16 [8192, 2048], P(('fsdp', 'tp')), may hold values from -6 to 6
- out_grad: bfloat16 [8192, 2048], P(('fsdp', 'tp')), may hold values from -6 to 6
- lengths: int32 [8], P('fsdp'), may hold values from 256 to 1024, as said below
- w_query: float32 [2048, 2048], P('fsdp', 'tp'), may hold values from -0.125 to 0.125
- w_key: float32 [2048, 1024], P('fsdp', 'tp'), may hold values from -0.125 to 0.125
- w_value: float32 [2048, 1024], P('fsdp', 'tp'), may hold values from -0.125 to 0.125
- w_out: float32 [2048, 2048], P('fsdp', 'tp'), may hold values from -3 to 3
- w_gate: float32 [2048, 8192], P('fsdp', 'tp'), may hold values from -0.125 to 0.125
- w_up: float32 [2048, 8192], P('fsdp', 'tp'), may hold values from -0.125 to 0.125
- w_down: float32 [2048, 8192], P('fsdp', 'tp'), may hold values from -0.0625 to 0.0625
- norm_attn: float32 [2048], replicated, may hold values from 0.5 to 1.5
- norm_mlp: float32 [2048], replicated, may hold values from 0.5 to 1.5
- moment_query: float32 [2048, 2048], P('fsdp', 'tp'), may hold values from -7.6293945e-05 to 7.6293945e-05
- moment_key: float32 [2048, 1024], P('fsdp', 'tp'), may hold values from -7.6293945e-05 to 7.6293945e-05
- moment_value: float32 [2048, 1024], P('fsdp', 'tp'), may hold values from -7.6293945e-05 to 7.6293945e-05
- moment_out: float32 [2048, 2048], P('fsdp', 'tp'), may hold values from -1.5258789e-05 to 1.5258789e-05
- moment_gate: float32 [2048, 8192], P('fsdp', 'tp'), may hold values from -7.6293945e-05 to 7.6293945e-05
- moment_up: float32 [2048, 8192], P('fsdp', 'tp'), may hold values from -7.6293945e-05 to 7.6293945e-05
- moment_down: float32 [2048, 8192], P('fsdp', 'tp'), may hold values from -7.6293945e-05 to 7.6293945e-05
- moment_norm_attn: float32 [2048], replicated, may hold values from -7.6293945e-05 to 7.6293945e-05
- moment_norm_mlp: float32 [2048], replicated, may hold values from -7.6293945e-05 to 7.6293945e-05
- square_query: float32 [2048, 2048], P('fsdp', 'tp'), may hold values from 1.5893538e-10 to 1.5893538e-09
- square_key: float32 [2048, 1024], P('fsdp', 'tp'), may hold values from 1.5893538e-10 to 1.5893538e-09
- square_value: float32 [2048, 1024], P('fsdp', 'tp'), may hold values from 1.5893538e-10 to 1.5893538e-09
- square_out: float32 [2048, 2048], P('fsdp', 'tp'), may hold values from 4.768061e-12 to 4.7680613e-11
- square_gate: float32 [2048, 8192], P('fsdp', 'tp'), may hold values from 1.5893538e-10 to 1.5893538e-09
- square_up: float32 [2048, 8192], P('fsdp', 'tp'), may hold values from 1.5893538e-10 to 1.5893538e-09
- square_down: float32 [2048, 8192], P('fsdp', 'tp'), may hold values from 1.5893538e-10 to 1.5893538e-09
- square_norm_attn: float32 [2048], replicated, may hold values from 1.5893538e-10 to 1.5893538e-09
- square_norm_mlp: float32 [2048], replicated, may hold values from 1.5893538e-10 to 1.5893538e-09
Outputs:
- block_out: bfloat16 [8192, 2048], P(('fsdp', 'tp'))
- input_grad: float32 [8192, 2048], P(('fsdp', 'tp'))
- grad_query: float32 [2048, 2048], P('fsdp', 'tp')
- grad_key: float32 [2048, 1024], P('fsdp', 'tp')
- grad_value: float32 [2048, 1024], P('fsdp', 'tp')
- grad_out_proj: float32 [2048, 2048], P('fsdp', 'tp')
- grad_gate: float32 [2048, 8192], P('fsdp', 'tp')
- grad_up: float32 [2048, 8192], P('fsdp', 'tp')
- grad_down: float32 [2048, 8192], P('fsdp', 'tp')
- grad_norm_attn: float32 [2048], replicated
- grad_norm_mlp: float32 [2048], replicated
- new_moment_query: float32 [2048, 2048], P('fsdp', 'tp')
- new_moment_key: float32 [2048, 1024], P('fsdp', 'tp')
- new_moment_value: float32 [2048, 1024], P('fsdp', 'tp')
- new_moment_out: float32 [2048, 2048], P('fsdp', 'tp')
- new_moment_gate: float32 [2048, 8192], P('fsdp', 'tp')
- new_moment_up: float32 [2048, 8192], P('fsdp', 'tp')
- new_moment_down: float32 [2048, 8192], P('fsdp', 'tp')
- new_moment_norm_attn: float32 [2048], replicated
- new_moment_norm_mlp: float32 [2048], replicated
- new_square_query: float32 [2048, 2048], P('fsdp', 'tp')
- new_square_key: float32 [2048, 1024], P('fsdp', 'tp')
- new_square_value: float32 [2048, 1024], P('fsdp', 'tp')
- new_square_out: float32 [2048, 2048], P('fsdp', 'tp')
- new_square_gate: float32 [2048, 8192], P('fsdp', 'tp')
- new_square_up: float32 [2048, 8192], P('fsdp', 'tp')
- new_square_down: float32 [2048, 8192], P('fsdp', 'tp')
- new_square_norm_attn: float32 [2048], replicated
- new_square_norm_mlp: float32 [2048], replicated
- update_query: float32 [2048, 2048], P('fsdp', 'tp')
- update_key: float32 [2048, 1024], P('fsdp', 'tp')
- update_value: float32 [2048, 1024], P('fsdp', 'tp')
- update_out: float32 [2048, 2048], P('fsdp', 'tp')
- update_gate: float32 [2048, 8192], P('fsdp', 'tp')
- update_up: float32 [2048, 8192], P('fsdp', 'tp')
- update_down: float32 [2048, 8192], P('fsdp', 'tp')
- update_norm_attn: float32 [2048], replicated
- update_norm_mlp: float32 [2048], replicated
- clip_norm: float32 [], replicated
Inputs may be any that keep to these rules, and one draw needn't show every extreme that they name: `lengths`: some slot holds a sequence of 1024 tokens and some slot one of a quarter of 1024.
All inputs are finite; a program needn't handle non-finite values.
Results may differ from a plain program's by a relative error of at most 0.02.
The roundings to bfloat16 on the way count: a program that leaves them out, or rounds other values in their place, can miss the bound.
Values may be sent and summed in bfloat16 or wider, within the bound.
No kernel may reach another device: no remote copies, remote signals or barrier semaphores. Data moves between devices by JAX's collectives and lax.ppermute only.
A program may use at most 168 MiB of HBM per device.

v0:
```python
import jax
import jax.numpy as jnp
from jax import lax
from jax.sharding import PartitionSpec as P

HD = 256
STEP = 10


EPS_NORM = 1e-05
THETA = 1000042.0
LEARN_RATE = 0.02
BETA_ONE = 0.9
BETA_TWO = 0.95
ADAM_EPS = 1e-08
WEIGHT_DECAY = 0.1
MAX_NORM = 1.0
MASKED = -1000000000.0


def rms_scale(values, norm_gain):
    return (
        values * lax.rsqrt(jnp.mean(values * values, axis=-1, keepdims=True) + EPS_NORM) * norm_gain
    )


def norm_back(values, norm_gain, incoming):
    row_scale = lax.rsqrt(jnp.mean(values * values, axis=-1, keepdims=True) + EPS_NORM)
    weighted = incoming * norm_gain
    grad_values = row_scale * weighted - values * row_scale**3 * jnp.mean(
        weighted * values, axis=-1, keepdims=True
    )
    return (grad_values, jnp.sum(incoming * values * row_scale, axis=0))


def rotary_tables(count, head_dim):
    positions = jnp.arange(count).astype(jnp.float32)
    inverse = THETA ** (-2.0 * jnp.arange(head_dim // 2).astype(jnp.float32) / head_dim)
    angles = positions[:, None] * inverse[None, :]
    return (jnp.cos(angles)[:, None, :], jnp.sin(angles)[:, None, :])


def rotary(values, cosine_table, sine_table):
    half_width = values.shape[-1] // 2
    first_half = values[..., :half_width]
    second_half = values[..., half_width:]
    return jnp.concatenate(
        [
            first_half * cosine_table - second_half * sine_table,
            second_half * cosine_table + first_half * sine_table,
        ],
        axis=-1,
    )


def dot_rows(left, right):
    return lax.dot_general(
        left, right, (((0,), (0,)), ((), ())), preferred_element_type=jnp.float32
    )


def dot_last(left, right):
    return lax.dot_general(
        left, right, (((1,), (1,)), ((), ())), preferred_element_type=jnp.float32
    )


def block_mask(first_row, block_rows, slot_rows, length):
    query_pos = first_row + jnp.arange(block_rows)
    key_pos = jnp.arange(slot_rows)
    return (key_pos[None, :] <= query_pos[:, None]) & (key_pos[None, :] < length)


def attend(query_rot, key_rot, value_bf, length, block_rows, heads_kv):
    slot_rows = query_rot.shape[0]
    head_dim = query_rot.shape[-1]
    group_size = query_rot.shape[1] // heads_kv
    score_scale = head_dim ** (-0.5)

    def one_block(block_index):
        first_row = block_index * block_rows
        query_blk = lax.dynamic_slice_in_dim(query_rot, first_row, block_rows, 0).reshape(
            block_rows, heads_kv, group_size, head_dim
        )
        raw_scores = jnp.einsum(
            "qkgd,skd->kgqs", query_blk, key_rot, preferred_element_type=jnp.float32
        )
        allowed = block_mask(first_row, block_rows, slot_rows, length)
        scores = jnp.where(allowed, raw_scores * score_scale, MASKED)
        row_peak = jnp.max(scores, axis=-1, keepdims=True)
        exponent = jnp.exp(scores - row_peak)
        row_total = jnp.sum(exponent, axis=-1, keepdims=True)
        attn_probs = (exponent / row_total).astype(jnp.bfloat16)
        attended = jnp.einsum(
            "kgqs,skd->qkgd", attn_probs, value_bf, preferred_element_type=jnp.float32
        )
        return (
            attended.reshape(block_rows, heads_kv * group_size * head_dim),
            (row_peak + jnp.log(row_total))[..., 0],
        )

    attended, log_sums = lax.map(one_block, jnp.arange(slot_rows // block_rows))
    return (attended.reshape(slot_rows, -1), log_sums)


def attend_back(
    query_rot, key_rot, value_bf, attended_grad, log_sums, length, block_rows, heads_kv
):
    slot_rows = query_rot.shape[0]
    head_dim = query_rot.shape[-1]
    group_size = query_rot.shape[1] // heads_kv
    score_scale = head_dim ** (-0.5)

    def one_block(carried, block_index):
        key_grad, value_grad = carried
        first_row = block_index * block_rows
        query_blk = lax.dynamic_slice_in_dim(query_rot, first_row, block_rows, 0).reshape(
            block_rows, heads_kv, group_size, head_dim
        )
        grad_blk = lax.dynamic_slice_in_dim(attended_grad, first_row, block_rows, 0).reshape(
            block_rows, heads_kv, group_size, head_dim
        )
        raw_scores = jnp.einsum(
            "qkgd,skd->kgqs", query_blk, key_rot, preferred_element_type=jnp.float32
        )
        allowed = block_mask(first_row, block_rows, slot_rows, length)
        scores = jnp.where(allowed, raw_scores * score_scale, MASKED)
        attn_probs = jnp.exp(scores - log_sums[block_index][..., None])
        prob_grad = jnp.einsum(
            "qkgd,skd->kgqs", grad_blk, value_bf, preferred_element_type=jnp.float32
        )
        row_delta = jnp.sum(attn_probs * prob_grad, axis=-1, keepdims=True)
        score_grad = (attn_probs * (prob_grad - row_delta) * score_scale).astype(jnp.bfloat16)
        query_grad = jnp.einsum(
            "kgqs,skd->qkgd", score_grad, key_rot, preferred_element_type=jnp.float32
        )
        key_grad = key_grad + jnp.einsum(
            "kgqs,qkgd->skd", score_grad, query_blk, preferred_element_type=jnp.float32
        )
        value_grad = value_grad + jnp.einsum(
            "kgqs,qkgd->skd",
            attn_probs.astype(jnp.bfloat16),
            grad_blk,
            preferred_element_type=jnp.float32,
        )
        return (
            (key_grad, value_grad),
            query_grad.reshape(block_rows, heads_kv * group_size, head_dim),
        )

    zero_grads = jnp.zeros(key_rot.shape, jnp.float32)
    (key_grad, value_grad), query_grad = lax.scan(
        one_block, (zero_grads, zero_grads), jnp.arange(slot_rows // block_rows)
    )
    return (query_grad.reshape(slot_rows, heads_kv * group_size, head_dim), key_grad, value_grad)


def adam_step(master, gradient, moment, square, factor):
    clipped = gradient * factor
    new_moment = BETA_ONE * moment + (1.0 - BETA_ONE) * clipped
    new_square = BETA_TWO * square + (1.0 - BETA_TWO) * clipped * clipped
    moment_hat = new_moment / (1.0 - BETA_ONE**STEP)
    square_hat = new_square / (1.0 - BETA_TWO**STEP)
    update = -LEARN_RATE * (moment_hat / (jnp.sqrt(square_hat) + ADAM_EPS) + WEIGHT_DECAY * master)
    return (new_moment, new_square, update)


def on_device(
    tokens,
    out_grad,
    lengths,
    w_query,
    w_key,
    w_value,
    w_out,
    w_gate,
    w_up,
    w_down,
    norm_attn,
    norm_mlp,
    moment_query,
    moment_key,
    moment_value,
    moment_out,
    moment_gate,
    moment_up,
    moment_down,
    moment_norm_attn,
    moment_norm_mlp,
    square_query,
    square_key,
    square_value,
    square_out,
    square_gate,
    square_up,
    square_down,
    square_norm_attn,
    square_norm_mlp,
):
    rows_dev = tokens.shape[0]
    tp_ways = lax.axis_size("tp")
    slot_rows = rows_dev * tp_ways
    block_rows = min(512, slot_rows)
    heads_kv = w_key.shape[1] // HD
    length = lengths[0]
    row_pos = lax.axis_index("tp") * rows_dev + jnp.arange(rows_dev)
    row_valid = (row_pos < length).astype(jnp.float32)
    cosine_table, sine_table = rotary_tables(slot_rows, HD)
    low_query = w_query.astype(jnp.bfloat16)
    low_key = w_key.astype(jnp.bfloat16)
    low_value = w_value.astype(jnp.bfloat16)
    low_out = w_out.astype(jnp.bfloat16)
    low_gate = w_gate.astype(jnp.bfloat16)
    low_up = w_up.astype(jnp.bfloat16)
    low_down = w_down.astype(jnp.bfloat16)
    resid_in = tokens.astype(jnp.float32)
    normed_attn = rms_scale(resid_in, norm_attn).astype(jnp.bfloat16)
    attn_input = lax.all_gather(normed_attn, "tp", axis=0, tiled=True)
    full_query, full_key, full_value, full_out = (
        lax.all_gather(low_query, "fsdp", axis=0, tiled=True),
        lax.all_gather(low_key, "fsdp", axis=0, tiled=True),
        lax.all_gather(low_value, "fsdp", axis=0, tiled=True),
        lax.all_gather(low_out, "fsdp", axis=0, tiled=True),
    )
    query_lin = jnp.dot(attn_input, full_query, preferred_element_type=jnp.float32).reshape(
        slot_rows, -1, HD
    )
    key_lin = jnp.dot(attn_input, full_key, preferred_element_type=jnp.float32).reshape(
        slot_rows, heads_kv, HD
    )
    value_bf = (
        jnp.dot(attn_input, full_value, preferred_element_type=jnp.float32)
        .astype(jnp.bfloat16)
        .reshape(slot_rows, heads_kv, HD)
    )
    query_rot = rotary(query_lin, cosine_table, sine_table).astype(jnp.bfloat16)
    key_rot = rotary(key_lin, cosine_table, sine_table).astype(jnp.bfloat16)
    attended, log_sums = attend(query_rot, key_rot, value_bf, length, block_rows, heads_kv)
    attn_bf = attended.astype(jnp.bfloat16)
    attn_rows = lax.psum_scatter(dot_last(attn_bf, full_out), "tp", scatter_dimension=0, tiled=True)
    middle = resid_in + attn_rows
    normed_mlp = rms_scale(middle, norm_mlp).astype(jnp.bfloat16)
    mlp_input = lax.all_gather(normed_mlp, "tp", axis=0, tiled=True)
    full_gate, full_up, full_down = (
        lax.all_gather(low_gate, "fsdp", axis=0, tiled=True),
        lax.all_gather(low_up, "fsdp", axis=0, tiled=True),
        lax.all_gather(low_down, "fsdp", axis=0, tiled=True),
    )
    gate_lin = jnp.dot(mlp_input, full_gate, preferred_element_type=jnp.float32)
    up_lin = jnp.dot(mlp_input, full_up, preferred_element_type=jnp.float32)
    gate_sig = jax.nn.sigmoid(gate_lin)
    hidden_bf = (gate_lin * gate_sig * up_lin).astype(jnp.bfloat16)
    mlp_rows = lax.psum_scatter(
        dot_last(hidden_bf, full_down).astype(jnp.bfloat16), "tp", scatter_dimension=0, tiled=True
    ).astype(jnp.float32)
    block_out = (middle + mlp_rows).astype(jnp.bfloat16)
    full_query, full_key, full_value, full_out, full_gate, full_up, full_down = (
        lax.all_gather(low_query, "fsdp", axis=0, tiled=True),
        lax.all_gather(low_key, "fsdp", axis=0, tiled=True),
        lax.all_gather(low_value, "fsdp", axis=0, tiled=True),
        lax.all_gather(low_out, "fsdp", axis=0, tiled=True),
        lax.all_gather(low_gate, "fsdp", axis=0, tiled=True),
        lax.all_gather(low_up, "fsdp", axis=0, tiled=True),
        lax.all_gather(low_down, "fsdp", axis=0, tiled=True),
    )
    cotangent = out_grad.astype(jnp.float32) * row_valid[:, None]
    mlp_grad_in = lax.all_gather(cotangent.astype(jnp.bfloat16), "tp", axis=0, tiled=True)
    hidden_grad = jnp.dot(mlp_grad_in, full_down, preferred_element_type=jnp.float32)
    grad_down = dot_rows(mlp_grad_in, hidden_bf)
    gate_grad = (hidden_grad * up_lin * gate_sig * (1.0 + gate_lin * (1.0 - gate_sig))).astype(
        jnp.bfloat16
    )
    up_grad = (hidden_grad * gate_lin * gate_sig).astype(jnp.bfloat16)
    grad_gate = dot_rows(mlp_input, gate_grad)
    grad_up = dot_rows(mlp_input, up_grad)
    normed_mlp_grad = lax.psum_scatter(
        dot_last(gate_grad, full_gate) + dot_last(up_grad, full_up),
        "tp",
        scatter_dimension=0,
        tiled=True,
    )
    middle_back, gain_mlp_part = norm_back(middle, norm_mlp, normed_mlp_grad)
    middle_grad = cotangent + middle_back
    attn_grad_in = lax.all_gather(middle_grad.astype(jnp.bfloat16), "tp", axis=0, tiled=True)
    attended_grad = jnp.dot(attn_grad_in, full_out, preferred_element_type=jnp.float32).astype(
        jnp.bfloat16
    )
    grad_proj = dot_rows(attn_grad_in, attn_bf)
    query_grad_rot, key_grad_rot, value_grad = attend_back(
        query_rot, key_rot, value_bf, attended_grad, log_sums, length, block_rows, heads_kv
    )
    query_grad = (
        rotary(query_grad_rot, cosine_table, -sine_table)
        .astype(jnp.bfloat16)
        .reshape(slot_rows, -1)
    )
    key_grad = (
        rotary(key_grad_rot, cosine_table, -sine_table).astype(jnp.bfloat16).reshape(slot_rows, -1)
    )
    value_grad_bf = value_grad.astype(jnp.bfloat16).reshape(slot_rows, -1)
    grad_query = dot_rows(attn_input, query_grad)
    grad_key = dot_rows(attn_input, key_grad)
    grad_value = dot_rows(attn_input, value_grad_bf)
    normed_attn_grad = lax.psum_scatter(
        dot_last(query_grad, full_query)
        + dot_last(key_grad, full_key)
        + dot_last(value_grad_bf, full_value),
        "tp",
        scatter_dimension=0,
        tiled=True,
    )
    input_back, gain_attn_part = norm_back(resid_in, norm_attn, normed_attn_grad)
    input_grad = middle_grad + input_back
    shard_grads = (
        lax.psum_scatter(grad_query, "fsdp", scatter_dimension=0, tiled=True),
        lax.psum_scatter(grad_key, "fsdp", scatter_dimension=0, tiled=True),
        lax.psum_scatter(grad_value, "fsdp", scatter_dimension=0, tiled=True),
        lax.psum_scatter(grad_proj, "fsdp", scatter_dimension=0, tiled=True),
        lax.psum_scatter(grad_gate, "fsdp", scatter_dimension=0, tiled=True),
        lax.psum_scatter(grad_up, "fsdp", scatter_dimension=0, tiled=True),
        lax.psum_scatter(grad_down, "fsdp", scatter_dimension=0, tiled=True),
    )
    square_part = jnp.zeros((), jnp.float32)
    for shard_grad in shard_grads:
        square_part = square_part + jnp.sum(shard_grad * shard_grad)
    gain_attn_grad, gain_mlp_grad, square_total = lax.psum(
        (gain_attn_part, gain_mlp_part, square_part), ("fsdp", "tp")
    )
    clip_norm = jnp.sqrt(
        square_total
        + jnp.sum(gain_attn_grad * gain_attn_grad)
        + jnp.sum(gain_mlp_grad * gain_mlp_grad)
    )
    factor = jnp.minimum(1.0, MAX_NORM / (clip_norm + 1e-06))
    every_grad = tuple(shard_grads) + (gain_attn_grad, gain_mlp_grad)
    params = (w_query, w_key, w_value, w_out, w_gate, w_up, w_down, norm_attn, norm_mlp)
    moments = (
        moment_query,
        moment_key,
        moment_value,
        moment_out,
        moment_gate,
        moment_up,
        moment_down,
        moment_norm_attn,
        moment_norm_mlp,
    )
    squares = (
        square_query,
        square_key,
        square_value,
        square_out,
        square_gate,
        square_up,
        square_down,
        square_norm_attn,
        square_norm_mlp,
    )
    results = [
        adam_step(params[number], every_grad[number], moments[number], squares[number], factor)
        for number in range(9)
    ]
    return (
        block_out,
        input_grad,
        every_grad[0],
        every_grad[1],
        every_grad[2],
        every_grad[3],
        every_grad[4],
        every_grad[5],
        every_grad[6],
        every_grad[7],
        every_grad[8],
        results[0][0],
        results[1][0],
        results[2][0],
        results[3][0],
        results[4][0],
        results[5][0],
        results[6][0],
        results[7][0],
        results[8][0],
        results[0][1],
        results[1][1],
        results[2][1],
        results[3][1],
        results[4][1],
        results[5][1],
        results[6][1],
        results[7][1],
        results[8][1],
        results[0][2],
        results[1][2],
        results[2][2],
        results[3][2],
        results[4][2],
        results[5][2],
        results[6][2],
        results[7][2],
        results[8][2],
        clip_norm,
    )


def solution(mesh):
    return jax.shard_map(
        on_device,
        mesh=mesh,
        in_specs=(
            P(("fsdp", "tp"), None),
            P(("fsdp", "tp"), None),
            P("fsdp"),
            P("fsdp", "tp"),
            P("fsdp", "tp"),
            P("fsdp", "tp"),
            P("fsdp", "tp"),
            P("fsdp", "tp"),
            P("fsdp", "tp"),
            P("fsdp", "tp"),
            P(),
            P(),
            P("fsdp", "tp"),
            P("fsdp", "tp"),
            P("fsdp", "tp"),
            P("fsdp", "tp"),
            P("fsdp", "tp"),
            P("fsdp", "tp"),
            P("fsdp", "tp"),
            P(),
            P(),
            P("fsdp", "tp"),
            P("fsdp", "tp"),
            P("fsdp", "tp"),
            P("fsdp", "tp"),
            P("fsdp", "tp"),
            P("fsdp", "tp"),
            P("fsdp", "tp"),
            P(),
            P(),
        ),
        out_specs=(
            P(("fsdp", "tp"), None),
            P(("fsdp", "tp"), None),
            P("fsdp", "tp"),
            P("fsdp", "tp"),
            P("fsdp", "tp"),
            P("fsdp", "tp"),
            P("fsdp", "tp"),
            P("fsdp", "tp"),
            P("fsdp", "tp"),
            P(),
            P(),
            P("fsdp", "tp"),
            P("fsdp", "tp"),
            P("fsdp", "tp"),
            P("fsdp", "tp"),
            P("fsdp", "tp"),
            P("fsdp", "tp"),
            P("fsdp", "tp"),
            P(),
            P(),
            P("fsdp", "tp"),
            P("fsdp", "tp"),
            P("fsdp", "tp"),
            P("fsdp", "tp"),
            P("fsdp", "tp"),
            P("fsdp", "tp"),
            P("fsdp", "tp"),
            P(),
            P(),
            P("fsdp", "tp"),
            P("fsdp", "tp"),
            P("fsdp", "tp"),
            P("fsdp", "tp"),
            P("fsdp", "tp"),
            P("fsdp", "tp"),
            P("fsdp", "tp"),
            P(),
            P(),
            P(),
        ),
        check_vma=False,
    )
```

profile of v0, /device:TPU:0, one launch (start us, length us, event | category | flops | bytes accessed | tf_op | source)
XLA Modules:
  0.0 2366.7 jit_solution(11106957944922076026)
XLA Ops:
  15.1 3.1 fusion.92
  18.2 44.6 %all-gather.14.cloned.1.call-done = bf16[2048,512]{1,0:T(8,128)(2,1)} async-done(((bf16[256,512]{1,0:T(8,128)(2,1)}), bf16[2048,512]{1,0:T(8,128)(2,1)}) %all-gather.14.cloned.1.call-update) | async-done | bytes 2097168 | tf_op jit(solution)/shard_map/all_gather | solution.py:220
  62.8 35.1 %all-gather.12.cloned.1.call-done = bf16[1024,2048]{1,0:T(8,128)(2,1)} async-done(((bf16[256,2048]{1,0:T(8,128)(2,1)}), bf16[1024,2048]{1,0:T(8,128)(2,1)}) %all-gather.12.cloned.1.call-update) | async-done | bytes 4194320 | tf_op jit(solution)/shard_map/all_gather | solution.py:218
  97.9 5.2 fusion.108
  106.3 2.5 copy.95
  108.8 32.0 %all-gather.16.cloned.1.call-done = bf16[2048,256]{1,0:T(8,128)(2,1)} async-done(((bf16[256,256]{1,0:T(8,128)(2,1)}), bf16[2048,256]{1,0:T(8,128)(2,1)}) %all-gather.16.cloned.1.call-update) | async-done | bytes 1048592 | tf_op jit(solution)/shard_map/all_gather | solution.py:221
  140.8 3.8 convolution_bitcast_fusion.2
  148.0 34.4 %all-gather.18.cloned.1.call-done = bf16[2048,256]{1,0:T(8,128)(2,1)} async-done(((bf16[256,256]{1,0:T(8,128)(2,1)}), bf16[2048,256]{1,0:T(8,128)(2,1)}) %all-gather.18.cloned.1.call-update) | async-done | bytes 1048592 | tf_op jit(solution)/shard_map/all_gather | solution.py:222
  182.4 3.7 fusion.61
  189.9 17.2 while.27
  207.1 25.9 %all-gather.20.cloned.1.call-done = bf16[2048,512]{1,0:T(8,128)(2,1)} async-done(((bf16[256,512]{1,0:T(8,128)(2,1)}), bf16[2048,512]{1,0:T(8,128)(2,1)}) %all-gather.20.cloned.1.call-update) | async-done | bytes 2097168 | tf_op jit(solution)/shard_map/all_gather | solution.py:223
  233.0 7.6 fusion.109
  243.3 67.6 %reduce-scatter.12.cloned.1.call-done = f32[256,2048]{1,0:T(8,128)} async-done(((f32[1024,2048]{1,0:T(8,128)}), f32[256,2048]{1,0:T(8,128)}) %reduce-scatter.12.cloned.1.call-update) | async-done | bytes 2097168 | tf_op jit(solution)/shard_map/reduce_scatter | solution.py:240
  314.2 2.8 convert_element_type.194
  319.0 2.7 convert_element_type.196
  321.8 117.0 %all-gather.24.cloned.1.call-done = bf16[2048,2048]{1,0:T(8,128)(2,1)} async-done(((bf16[256,2048]{1,0:T(8,128)(2,1)}), bf16[2048,2048]{1,0:T(8,128)(2,1)}) %all-gather.24.cloned.1.call-update) | async-done | bytes 8388624 | tf_op jit(solution)/shard_map/all_gather | solution.py:245
  438.8 34.9 %all-gather.22.cloned.1.call-done = bf16[1024,2048]{1,0:T(8,128)(2,1)} async-done(((bf16[256,2048]{1,0:T(8,128)(2,1)}), bf16[1024,2048]{1,0:T(8,128)(2,1)}) %all-gather.22.cloned.1.call-update) | async-done | bytes 4194320 | tf_op jit(solution)/shard_map/all_gather | solution.py:243
  473.7 14.5 fusion.110
  488.3 113.4 %all-gather.26.cloned.1.call-done = bf16[2048,2048]{1,0:T(8,128)(2,1)} async-done(((bf16[256,2048]{1,0:T(8,128)(2,1)}), bf16[2048,2048]{1,0:T(8,128)(2,1)}) %all-gather.26.cloned.1.call-update) | async-done | bytes 8388624 | tf_op jit(solution)/shard_map/all_gather | solution.py:246
  601.6 14.6 fusion.111
  616.2 20.2 all-gather.30.cloned.1.call-done
  636.4 127.9 %all-gather.28.cloned.1.call-done = bf16[2048,2048]{1,0:T(8,128)(2,1)} async-done(((bf16[256,2048]{1,0:T(8,128)(2,1)}), bf16[2048,2048]{1,0:T(8,128)(2,1)}) %all-gather.28.cloned.1.call-update) | async-done | bytes 8388624 | tf_op jit(solution)/shard_map/all_gather | solution.py:247
  764.3 21.2 multiply_convert_fusion
  785.5 16.7 fusion.112
  802.2 13.0 convolution_add_fusion
  815.3 13.9 convolution_convert_fusion
  829.3 56.0 %reduce-scatter.16.cloned.1.call-done = f32[256,2048]{1,0:T(8,128)} async-done(((f32[1024,2048]{1,0:T(8,128)}), f32[256,2048]{1,0:T(8,128)}) %reduce-scatter.16.cloned.1.call-update) | async-done | bytes 2097168 | tf_op jit(solution)/shard_map/reduce_scatter | solution.py:276
  885.3 2.7 multiply_reduce_fusion.3
  888.1 44.4 %reduce-scatter.14.cloned.1.call-done = bf16[256,2048]{1,0:T(8,128)(2,1)} async-done(((bf16[1024,2048]{1,0:T(8,128)(2,1)}), bf16[256,2048]{1,0:T(8,128)(2,1)}) %reduce-scatter.14.cloned.1.call-update) | async-done | bytes 1048592 | tf_op jit(solution)/shard_map/reduce_scatter | solution.py:253
  932.4 4.7 fusion.106
  937.4 34.4 %all-gather.32.cloned.1.call-done = bf16[1024,2048]{1,0:T(8,128)(2,1)} async-done(((bf16[256,2048]{1,0:T(8,128)(2,1)}), bf16[1024,2048]{1,0:T(8,128)(2,1)}) %all-gather.32.cloned.1.call-update) | async-done | bytes 4194320 | tf_op jit(solution)/shard_map/all_gather | solution.py:284
  971.8 5.2 convolution_convert_fusion.1
  977.1 46.9 %while.28 = (s32[]{:T(128)}, f32[1024,1,256]{0,2,1:T(8,128)}, f32[1024,1,256]{0,2,1:T(8,128)}, f32[2,512,2,256]{3,1,0,2:T(8,128)}, s32[2]{0:T(128)S(1)}, /*index...) while((s32[]{:T(128)}, f32[1024,1,256]{0,2,1:T(8,128)}, ...), condition=%wide.region_12.13_spmd.clone, body=%wide.region_10.12_spmd.clone.sunk | while | flops 2703229440 | bytes 88640424 | solution.py:152
  978.4 3.9 fusion.198
  985.7 4.4 fusion.200
  991.5 2.7 fusion.204
  994.3 2.9 fusion.202
  1001.0 3.9 fusion.198
  1008.3 4.4 fusion.200
  1014.1 2.7 fusion.204
  1016.9 3.2 fusion.202
  1020.1 3.8 fusion.203
  1024.0 3.7 fusion.91
  1028.4 4.8 fusion.84
  1034.5 4.9 fusion.81
  1043.0 6.6 fusion.114
  1050.8 6.6 fusion.115
  1057.5 15.4 fusion.116
  1073.3 15.4 fusion.117
  1088.8 15.3 fusion.118
  1110.2 4.6 add_add_fusion
  1116.5 56.5 %reduce-scatter.24.cloned.1.call-done = f32[256,256]{1,0:T(8,128)} async-done(((f32[2048,256]{1,0:T(8,128)}), f32[256,256]{1,0:T(8,128)}) %reduce-scatter.24.cloned.1.call-update) | async-done | bytes 262160 | tf_op jit(solution)/shard_map/reduce_scatter | solution.py:317
  1174.6 89.9 %reduce-scatter.20.cloned.1.call-done = f32[256,512]{1,0:T(8,128)} async-done(((f32[2048,512]{1,0:T(8,128)}), f32[256,512]{1,0:T(8,128)}) %reduce-scatter.20.cloned.1.call-update) | async-done | bytes 524304 | tf_op jit(solution)/shard_map/reduce_scatter | solution.py:315
  1268.2 88.2 %reduce-scatter.26.cloned.1.call-done = f32[256,512]{1,0:T(8,128)} async-done(((f32[2048,512]{1,0:T(8,128)}), f32[256,512]{1,0:T(8,128)}) %reduce-scatter.26.cloned.1.call-update) | async-done | bytes 524304 | tf_op jit(solution)/shard_map/reduce_scatter | solution.py:318
  1358.8 284.8 %reduce-scatter.28.cloned.1.call-done = f32[256,2048]{1,0:T(8,128)} async-done(((f32[2048,2048]{1,0:T(8,128)}), f32[256,2048]{1,0:T(8,128)}) %reduce-scatter.28.cloned.1.call-update) | async-done | bytes 2097168 | tf_op jit(solution)/shard_map/reduce_scatter | solution.py:319
  1643.7 2.7 multiply_reduce_fusion.2
  1647.1 282.5 %reduce-scatter.30.cloned.1.call-done = f32[256,2048]{1,0:T(8,128)} async-done(((f32[2048,2048]{1,0:T(8,128)}), f32[256,2048]{1,0:T(8,128)}) %reduce-scatter.30.cloned.1.call-update) | async-done | bytes 2097168 | tf_op jit(solution)/shard_map/reduce_scatter | solution.py:320
  1929.6 2.7 multiply_reduce_fusion.1
  1933.0 283.3 %reduce-scatter.32.cloned.1.call-done = f32[256,2048]{1,0:T(8,128)} async-done(((f32[2048,2048]{1,0:T(8,128)}), f32[256,2048]{1,0:T(8,128)}) %reduce-scatter.32.cloned.1.call-update) | async-done | bytes 2097168 | tf_op jit(solution)/shard_map/reduce_scatter | solution.py:321
  2216.3 2.7 multiply_reduce_fusion
  2219.8 69.8 %reduce-scatter.18.cloned.1.call-done = f32[256,2048]{1,0:T(8,128)} async-done(((f32[1024,2048]{1,0:T(8,128)}), f32[256,2048]{1,0:T(8,128)}) %reduce-scatter.18.cloned.1.call-update) | async-done | bytes 2097168 | tf_op jit(solution)/shard_map/reduce_scatter | solution.py:304
  2291.8 40.0 %all-reduce = (f32[2048]{0:T(1024)S(1)}, f32[2048]{0:T(1024)S(1)}, f32[]{:T(128)}) all-reduce(f32[2048]{0:T(1024)S(1)} %get-tuple-element.222, f32[2048]{0:T(1024)S(1)} %copy-done.57, f32[]{:T(128)S(6)} %add.315), channel_id=1, replica_groups=mesh['fsdp'=8,'tp'=4] {'fsdp','tp'}, use_global_device_ids=true, to_apply=%region_23.24 | all-reduce | flops 4097 | bytes 32776 | tf_op jit(solution)/shard_map/psum | solution.py:326
  2335.8 7.0 add_multiply_fusion.2
  2347.8 5.8 add_multiply_fusion
  (286 shorter events, 84.7 us)
Async XLA Ops:
  7.2 55.6 %all-gather.14.cloned.1.call-start = ((), (), s32[]{:S(2)}) async-start(), calls=%async_computation.12 | async-start | bytes 2359296 | tf_op jit(solution)/shard_map/all_gather | solution.py:220
  9.2 88.8 %all-gather.12.cloned.1.call-start = ((), (), s32[]{:S(2)}) async-start(), calls=%async_computation.11 | async-start | bytes 5242880 | tf_op jit(solution)/shard_map/all_gather | solution.py:218
  12.7 128.2 %all-gather.16.cloned.1.call-start = ((), (), s32[]{:S(2)}) async-start(), calls=%async_computation.13 | async-start | bytes 1179648 | tf_op jit(solution)/shard_map/all_gather | solution.py:221
  13.4 168.9 %all-gather.18.cloned.1.call-start = ((), (), s32[]{:S(2)}) async-start(), calls=%async_computation.14 | async-start | bytes 1179648 | tf_op jit(solution)/shard_map/all_gather | solution.py:222
  14.2 218.8 %all-gather.20.cloned.1.call-start = ((), (), s32[]{:S(2)}) async-start(), calls=%async_computation.15 | async-start | bytes 2359296 | tf_op jit(solution)/shard_map/all_gather | solution.py:223
  15.0 295.9 %reduce-scatter.12.cloned.1.call-start = ((), (), s32[]{:S(2)}) async-start(), calls=%async_computation.16 | async-start | bytes 10485760 | tf_op jit(solution)/shard_map/reduce_scatter | solution.py:240
  15.1 129.5 %copy-start.53 = (f32[1024]{0:T(1024)}, f32[1024]{0:T(1024)S(1)}, u32[]{:S(2)}) copy-start(f32[1024]{0:T(1024)S(1)} %iota_convert_fusion) | copy-start | bytes 12292
  15.1 129.5 %copy-start.66 = (f32[128]{0:T(128)}, f32[128]{0:T(128)S(1)}, u32[]{:S(2)}) copy-start(f32[128]{0:T(128)S(1)} %multiply_power_fusion) | copy-start | bytes 1540
  18.2 168.9 %copy-start.17 = (f32[1024,128]{1,0:T(8,128)}, f32[1024,128]{1,0:T(8,128)S(1)}, u32[]{:S(2)}) copy-start(f32[1024,128]{1,0:T(8,128)S(1)} %get-tuple-element.316) | copy-start | bytes 1572868
  207.1 33.5 %copy-start.55 = (f32[2,1,2,512]{3,2,1,0:T(2,128)}, f32[2,1,2,512]{3,2,1,0:T(2,128)S(1)}, u32[]{:S(2)}) copy-start(f32[2,1,2,512]{3,2,1,0:T(2,128)S(1)} %get-tuple-element.501) | copy-start | bytes 24580
  240.6 198.3 %all-gather.24.cloned.1.call-start = ((), (), s32[]{:S(2)}) async-start(), calls=%async_computation.18 | async-start | bytes 9437184 | tf_op jit(solution)/shard_map/all_gather | solution.py:245
  243.3 69.6 %copy-start.51 = (f32[2048]{0:T(1024)S(1)}, f32[2048]{0:T(1024)}, u32[]{:S(2)}) copy-start(f32[2048]{0:T(1024)} %param.45) | copy-start | bytes 24580
  243.3 230.4 %all-gather.22.cloned.1.call-start = ((), (), s32[]{:S(2)}) async-start(), calls=%async_computation.17 | async-start | bytes 5242880 | tf_op jit(solution)/shard_map/all_gather | solution.py:243
  314.2 287.5 %all-gather.26.cloned.1.call-start = ((), (), s32[]{:S(2)}) async-start(), calls=%async_computation.19 | async-start | bytes 9437184 | tf_op jit(solution)/shard_map/all_gather | solution.py:246
  317.0 319.4 %all-gather.30.cloned.1.call-start = ((), (), s32[]{:S(2)}) async-start(), calls=%async_computation.22 | async-start | bytes 5242880 | tf_op jit(solution)/shard_map/all_gather | solution.py:267
  319.0 445.3 %all-gather.28.cloned.1.call-start = ((), (), s32[]{:S(2)}) async-start(), calls=%async_computation.20 | async-start | bytes 9437184 | tf_op jit(solution)/shard_map/all_gather | solution.py:247
  321.8 563.5 %reduce-scatter.16.cloned.1.call-start = ((), (), s32[]{:S(2)}) async-start(), calls=%async_computation.23 | async-start | bytes 10485760 | tf_op jit(solution)/shard_map/reduce_scatter | solution.py:276
  785.5 16.7 copy-start.72
  785.5 16.7 copy-start.69
  815.3 117.1 %reduce-scatter.14.cloned.1.call-start = ((), (), s32[]{:S(2)}) async-start(), calls=%async_computation.21 | async-start | bytes 5242880 | tf_op jit(solution)/shard_map/reduce_scatter | solution.py:253
  829.3 142.5 %all-gather.32.cloned.1.call-start = ((), (), s32[]{:S(2)}) async-start(), calls=%async_computation.24 | async-start | bytes 5242880 | tf_op jit(solution)/shard_map/all_gather | solution.py:284
  937.2 177.7 %reduce-scatter.22.cloned.1.call-start = ((), (), s32[]{:S(2)}) async-start(), calls=%async_computation.27 | async-start | bytes 2359296 | tf_op jit(solution)/shard_map/reduce_scatter | solution.py:316
  937.4 39.6 %copy-start.5 = (bf16[1024,1,256]{2,0,1:T(8,128)(2,1)S(1)}, bf16[1024,1,256]{2,0,1:T(8,128)(2,1)}, u32[]{:S(2)}) copy-start(bf16[1024,1,256]{2,0,1:T(8,128)(2,1)} %copy-done.4) | copy-start | bytes 1572868
  937.4 39.6 %copy-start.56 = (f32[2,1,2,512]{3,2,1,0:T(2,128)S(1)}, f32[2,1,2,512]{3,2,1,0:T(2,128)}, u32[]{:S(2)}) copy-start(f32[2,1,2,512]{3,2,1,0:T(2,128)} %copy-done.55) | copy-start | bytes 24580
  977.0 46.9 %copy-start.54 = (f32[1024]{0:T(1024)S(1)}, f32[1024]{0:T(1024)}, u32[]{:S(2)}) copy-start(f32[1024]{0:T(1024)} %copy-done.53) | copy-start | bytes 12292
  977.0 46.9 %copy-start.67 = (f32[128]{0:T(128)S(1)}, f32[128]{0:T(128)}, u32[]{:S(2)}) copy-start(f32[128]{0:T(128)} %copy-done.66) | copy-start | bytes 1540
  977.1 5.3 copy-start.15
  999.7 5.3 copy-start.15
  1033.3 139.7 %reduce-scatter.24.cloned.1.call-start = ((), (), s32[]{:S(2)}) async-start(), calls=%async_computation.28 | async-start | bytes 2359296 | tf_op jit(solution)/shard_map/reduce_scatter | solution.py:317
  1039.3 225.1 %reduce-scatter.20.cloned.1.call-start = ((), (), s32[]{:S(2)}) async-start(), calls=%async_computation.26 | async-start | bytes 4718592 | tf_op jit(solution)/shard_map/reduce_scatter | solution.py:315
  1049.6 306.8 %reduce-scatter.26.cloned.1.call-start = ((), (), s32[]{:S(2)}) async-start(), calls=%async_computation.29 | async-start | bytes 4718592 | tf_op jit(solution)/shard_map/reduce_scatter | solution.py:318
  1057.4 586.2 %reduce-scatter.28.cloned.1.call-start = ((), (), s32[]{:S(2)}) async-start(), calls=%async_computation.30 | async-start | bytes 18874368 | tf_op jit(solution)/shard_map/reduce_scatter | solution.py:319
  1072.9 856.7 %reduce-scatter.30.cloned.1.call-start = ((), (), s32[]{:S(2)}) async-start(), calls=%async_computation.31 | async-start | bytes 18874368 | tf_op jit(solution)/shard_map/reduce_scatter | solution.py:320
  1088.8 1127.5 %reduce-scatter.32.cloned.1.call-start = ((), (), s32[]{:S(2)}) async-start(), calls=%async_computation.32 | async-start | bytes 18874368 | tf_op jit(solution)/shard_map/reduce_scatter | solution.py:321
  1104.2 1185.5 %reduce-scatter.18.cloned.1.call-start = ((), (), s32[]{:S(2)}) async-start(), calls=%async_computation.25 | async-start | bytes 10485760 | tf_op jit(solution)/shard_map/reduce_scatter | solution.py:304
  1647.0 642.6 %copy-start.3 = (bf16[256,2048]{1,0:T(8,128)(2,1)S(1)}, bf16[256,2048]{1,0:T(8,128)(2,1)}, u32[]{:S(2)}) copy-start(bf16[256,2048]{1,0:T(8,128)(2,1)} %param.34) | copy-start | bytes 3145732
  1647.1 642.6 %copy-start.50 = (f32[2048]{0:T(1024)S(1)}, f32[2048]{0:T(1024)}, u32[]{:S(2)}) copy-start(f32[2048]{0:T(1024)} %param.44) | copy-start | bytes 24580
  1647.1 642.6 %copy-start.61 = (f32[256]{0:T(256)S(1)}, f32[256]{0:T(256)}, u32[]{:S(2)}) copy-start(f32[256]{0:T(256)} %copy-done.60) | copy-start | bytes 3076
  2219.0 72.8 %copy-start.57 = (f32[2048]{0:T(1024)S(1)}, f32[2048]{0:T(1024)}, u32[]{:S(2)}) copy-start(f32[2048]{0:T(1024)} %get-tuple-element.220) | copy-start | bytes 24580
  2219.0 116.0 %copy-start.52 = (f32[2048]{0:T(1024)S(1)}, f32[2048]{0:T(1024)}, u32[]{:S(2)}) copy-start(f32[2048]{0:T(1024)} %param.45) | copy-start | bytes 24580
  2219.0 116.0 %copy-start.62 = (f32[2048]{0:T(1024)S(1)}, f32[2048]{0:T(1024)}, u32[]{:S(2)}) copy-start(f32[2048]{0:T(1024)} %param.63) | copy-start | bytes 24580
  2219.0 116.0 %copy-start.63 = (f32[2048]{0:T(1024)S(1)}, f32[2048]{0:T(1024)}, u32[]{:S(2)}) copy-start(f32[2048]{0:T(1024)} %param.54) | copy-start | bytes 24580
  2219.0 116.0 %copy-start.64 = (f32[2048]{0:T(1024)S(1)}, f32[2048]{0:T(1024)}, u32[]{:S(2)}) copy-start(f32[2048]{0:T(1024)} %param.62) | copy-start | bytes 24580
  2219.0 116.0 %copy-start.65 = (f32[2048]{0:T(1024)S(1)}, f32[2048]{0:T(1024)}, u32[]{:S(2)}) copy-start(f32[2048]{0:T(1024)} %param.53) | copy-start | bytes 24580
  2219.0 116.7 %copy-start.10 = (f32[256,2048]{1,0:T(8,128)S(1)}, f32[256,2048]{1,0:T(8,128)}, u32[]{:S(2)}) copy-start(f32[256,2048]{1,0:T(8,128)} %param.41) | copy-start | bytes 6291460
  2331.8 11.0 copy-start.58
  2331.8 11.0 copy-start.59
  2335.7 7.1 copy-start.7
  2335.7 7.1 copy-start.8
  2335.7 7.1 copy-start.68
  2335.7 9.0 copy-start.14
  2335.7 9.0 copy-start.27
  2335.8 9.0 copy-start.28
  2335.8 9.0 copy-start.29
  2335.8 10.0 copy-start.30
  2347.7 5.9 copy-start.34
  2347.7 5.9 copy-start.36
  2347.7 5.9 copy-start.37
  2347.8 5.9 copy-start.38
  2347.8 5.9 copy-start.45
  2347.8 5.9 copy-start.46
  2347.8 5.9 copy-start.47
  2347.8 5.9 copy-start.48
  2347.8 7.4 copy-start.44
  (36 other events, 95.1 us)
Sparse Core Ops, SparseCore 0:
  10.8 51.9 all-gather.13
  64.9 32.9 all-gather.11
  100.6 40.1 all-gather.15
  143.4 38.9 all-gather.17
  184.9 48.0 all-gather.19
  240.7 70.1 reduce-scatter.11
  313.9 124.9 all-gather.23
  441.0 32.6 all-gather.21
  476.7 124.9 all-gather.25
  603.7 32.6 all-gather.29
  639.3 124.9 all-gather.27
  815.4 69.8 reduce-scatter.15
  887.8 44.5 reduce-scatter.13
  937.3 34.4 all-gather.31
  1033.4 67.9 reduce-scatter.21
  1106.3 66.5 reduce-scatter.23
  1177.4 87.0 reduce-scatter.19
  1268.5 87.7 reduce-scatter.25
  1361.2 282.3 reduce-scatter.27
  1647.9 281.6 reduce-scatter.29
  1934.4 281.7 reduce-scatter.31
  2218.8 70.7 reduce-scatter.17
where the time goes:
time: 2380 us; the launch traced here: 2370 us
  waiting for transfers between devices  1940 us (82%)
  matrix products  240 us (10%)
  other arithmetic  86.4 us (4%)
  blocking collectives  40 us (2%)
  local copies, waits for them, and re-layouts  24.1 us (1%)
  between operations  24 us (1%)
    reduce_scatter x1, waiting for transfers between devices, on_device(): lax.psum_scatter(grad_gate, 'fsdp', scatter_dimension=0, tiled=True)  285 us
    reduce_scatter x1, waiting for transfers between devices, on_device(): lax.psum_scatter(grad_down, 'fsdp', scatter_dimension=0, tiled=True)  283 us
    reduce_scatter x1, waiting for transfers between devices, on_device(): lax.psum_scatter(grad_up, 'fsdp', scatter_dimension=0, tiled=True)  283 us
    all_gather x1, waiting for transfers between devices, on_device(): lax.all_gather(low_down, 'fsdp', axis=0, tiled=True)  128 us
    all_gather x1, waiting for transfers between devices, on_device(): lax.all_gather(low_gate, 'fsdp', axis=0, tiled=True)  117 us
    all_gather x1, waiting for transfers between devices, on_device(): lax.all_gather(low_up, 'fsdp', axis=0, tiled=True)  113 us
    reduce_scatter x1, waiting for transfers between devices, on_device(): lax.psum_scatter(grad_query, 'fsdp', scatter_dimension=0, tiled=True)  89.9 us
    reduce_scatter x1, waiting for transfers between devices, on_device(): lax.psum_scatter(grad_proj, 'fsdp', scatter_dimension=0, tiled=True)  88.2 us
  transfers between devices with their start and end apart: 22, of which 21 were waited for; matrix products, arithmetic and copies ran while one was open for 8% of the time, Pallas kernels for 0%

commit v1 on v0

--- a/solution.py
+++ b/solution.py
@@ -163,6 +163,122 @@
     square_hat = new_square / (1.0 - BETA_TWO**STEP)
     update = -LEARN_RATE * (moment_hat / (jnp.sqrt(square_hat) + ADAM_EPS) + WEIGHT_DECAY * master)
     return (new_moment, new_square, update)
+
+
+AXES = ("fsdp", "tp")
+PAIR = 2
+
+
+def swap(value, fsdp_mask, tp_mask, odd_masks=None):
+    fsdp_ways, tp_ways = lax.axis_size("fsdp"), lax.axis_size("tp")
+    pairs = []
+    for row in range(fsdp_ways):
+        for col in range(tp_ways):
+            masks = (fsdp_mask, tp_mask)
+            if odd_masks is not None and col & 1:
+                masks = odd_masks
+            pairs.append((row * tp_ways + col, (row ^ masks[0]) * tp_ways + (col ^ masks[1])))
+    return lax.ppermute(value, AXES, pairs)
+
+
+def bits_below(ways):
+    return [1 << power for power in reversed(range(ways.bit_length() - 1))]
+
+
+def gather_chunks(first, bits):
+    chunks = dict(first)
+    for bit in bits:
+        arrived = {mask ^ bit: swap(chunk, bit, 0) for mask, chunk in chunks.items()}
+        chunks.update(arrived)
+    return chunks
+
+
+def assemble(chunks):
+    me = lax.axis_index("fsdp")
+    rows, cols = chunks[0].shape
+    whole = jnp.zeros((rows * len(chunks), cols), chunks[0].dtype)
+    for mask, chunk in chunks.items():
+        whole = lax.dynamic_update_slice_in_dim(whole, chunk, (me ^ mask) * rows, 0)
+    return whole
+
+
+def scatter_chunks(whole, bits, rows):
+    me = lax.axis_index("fsdp")
+    ways = whole.shape[0] // rows
+    parts = {
+        mask: lax.dynamic_slice_in_dim(whole, (me ^ mask) * rows, rows, 0) for mask in range(ways)
+    }
+    for bit in bits:
+        kept = {}
+        for mask, part in parts.items():
+            if not mask & bit:
+                got = swap(parts[mask ^ bit].astype(jnp.bfloat16), bit, 0)
+                kept[mask] = part.astype(jnp.float32) + got.astype(jnp.float32)
+        parts = kept
+    return parts
+
+
+def gather_slot(block):
+    other = swap(block, 0, 2)
+    near = swap(block, 0, 1)
+    far = swap(other, 0, 1)
+    me = lax.axis_index("tp")
+    rows = block.shape[0]
+    whole = jnp.zeros((rows * 4, block.shape[1]), block.dtype)
+    for mask, chunk in ((0, block), (2, other), (1, near), (3, far)):
+        whole = lax.dynamic_update_slice_in_dim(whole, chunk, (me ^ mask) * rows, 0)
+    return whole
+
+
+def scatter_slot(whole):
+    me = lax.axis_index("tp")
+    rows = whole.shape[0] // 4
+    parts = [lax.dynamic_slice_in_dim(whole, (me ^ mask) * rows, rows, 0) for mask in range(4)]
+    far = parts[2] + swap(parts[3].astype(jnp.bfloat16), 0, 1).astype(jnp.float32)
+    own = parts[0] + swap(parts[1].astype(jnp.bfloat16), 0, 1).astype(jnp.float32)
+    return own + swap(far.astype(jnp.bfloat16), 0, 2).astype(jnp.float32)
+
+
+def swap_one(value):
+    return swap(value, 0, 2, (PAIR, 0))
+
+
+def swap_two(value):
+    return swap(value, PAIR, 0, (0, 2))
+
+
+def gather_group(block):
+    first = swap_one(block)
+    second = swap_two(block)
+    both = swap_two(first)
+    mine = [block, first, second, both]
+    return jnp.concatenate(mine + [swap(each, 0, 1) for each in mine], axis=0)
+
+
+def scatter_group(whole):
+    rows = whole.shape[0] // 8
+    parts = [whole[rows * number : rows * (number + 1)] for number in range(8)]
+    sums = [
+        parts[number].astype(jnp.float32)
+        + swap(parts[number + 4].astype(jnp.bfloat16), 0, 1).astype(jnp.float32)
+        for number in (3, 2, 1, 0)
+    ][::-1]
+    first = sums[1] + swap_two(sums[3].astype(jnp.bfloat16)).astype(jnp.float32)
+    own = sums[0] + swap_two(sums[2].astype(jnp.bfloat16)).astype(jnp.float32)
+    return own + swap_one(first.astype(jnp.bfloat16)).astype(jnp.float32)
+
+
+def sum_everywhere(value):
+    for bit in bits_below(lax.axis_size("tp"))[::-1]:
+        value = value + swap(value, 0, bit)
+    for bit in bits_below(lax.axis_size("fsdp")):
+        value = value + swap(value, bit, 0)
+    return value
+
+
+def half_columns(value, which):
+    width = value.shape[1] // 2
+    return lax.dynamic_slice_in_dim(value, which * width, width, 1)
 
 
 def on_device(
@@ -199,133 +315,112 @@
 ):
     rows_dev = tokens.shape[0]
     tp_ways = lax.axis_size("tp")
+    fsdp_ways = lax.axis_size("fsdp")
+    all_bits = bits_below(fsdp_ways)
+    far_bits = [bit for bit in all_bits if bit != PAIR]
+    pair_side = (lax.axis_index("fsdp") // PAIR) % 2
     slot_rows = rows_dev * tp_ways
     block_rows = min(512, slot_rows)
     heads_kv = w_key.shape[1] // HD
+    weight_rows = w_query.shape[0]
     length = lengths[0]
     row_pos = lax.axis_index("tp") * rows_dev + jnp.arange(rows_dev)
     row_valid = (row_pos < length).astype(jnp.float32)
     cosine_table, sine_table = rotary_tables(slot_rows, HD)
-    low_query = w_query.astype(jnp.bfloat16)
-    low_key = w_key.astype(jnp.bfloat16)
-    low_value = w_value.astype(jnp.bfloat16)
-    low_out = w_out.astype(jnp.bfloat16)
-    low_gate = w_gate.astype(jnp.bfloat16)
-    low_up = w_up.astype(jnp.bfloat16)
-    low_down = w_down.astype(jnp.bfloat16)
     resid_in = tokens.astype(jnp.float32)
     normed_attn = rms_scale(resid_in, norm_attn).astype(jnp.bfloat16)
-    attn_input = lax.all_gather(normed_attn, "tp", axis=0, tiled=True)
-    full_query, full_key, full_value, full_out = (
-        lax.all_gather(low_query, "fsdp", axis=0, tiled=True),
-        lax.all_gather(low_key, "fsdp", axis=0, tiled=True),
-        lax.all_gather(low_value, "fsdp", axis=0, tiled=True),
-        lax.all_gather(low_out, "fsdp", axis=0, tiled=True),
-    )
-    query_lin = jnp.dot(attn_input, full_query, preferred_element_type=jnp.float32).reshape(
-        slot_rows, -1, HD
-    )
-    key_lin = jnp.dot(attn_input, full_key, preferred_element_type=jnp.float32).reshape(
-        slot_rows, heads_kv, HD
-    )
+    low_qkv = jnp.concatenate([w_query, w_key, w_value], axis=1).astype(jnp.bfloat16)
+    low_out = w_out.astype(jnp.bfloat16)
+    full_qkv = assemble(gather_chunks({0: low_qkv}, all_bits))
+    attn_input = gather_slot(normed_attn)
+    full_out = assemble(gather_chunks({0: low_out}, all_bits))
+
+    def gather_wide(weight):
+        kept = half_columns(weight, pair_side).astype(jnp.bfloat16)
+        sent = half_columns(weight, 1 - pair_side).astype(jnp.bfloat16)
+        return assemble(gather_chunks({0: kept, PAIR: swap(sent, PAIR, 0)}, far_bits))
+
+    def scatter_wide(gradient):
+        parts = scatter_chunks(gradient, far_bits[::-1], weight_rows)
+        got = swap(parts[PAIR].astype(jnp.bfloat16), PAIR, 0).astype(jnp.float32)
+        return jnp.where(
+            pair_side == 0,
+            jnp.concatenate([parts[0], got], axis=1),
+            jnp.concatenate([got, parts[0]], axis=1),
+        )
+
+    full_gate = gather_wide(w_gate)
+    full_up = gather_wide(w_up)
+    full_down = gather_wide(w_down)
+    cotangent = out_grad.astype(jnp.float32) * row_valid[:, None]
+    mlp_grad_in = gather_group(cotangent.astype(jnp.bfloat16))
+
+    width_query, width_key = w_query.shape[1], w_key.shape[1]
+    qkv_lin = jnp.dot(attn_input, full_qkv, preferred_element_type=jnp.float32)
+    query_lin = qkv_lin[:, :width_query].reshape(slot_rows, -1, HD)
+    key_lin = qkv_lin[:, width_query : width_query + width_key].reshape(slot_rows, heads_kv, HD)
     value_bf = (
-        jnp.dot(attn_input, full_value, preferred_element_type=jnp.float32)
-        .astype(jnp.bfloat16)
-        .reshape(slot_rows, heads_kv, HD)
+        qkv_lin[:, width_query + width_key :].astype(jnp.bfloat16).reshape(slot_rows, heads_kv, HD)
     )
     query_rot = rotary(query_lin, cosine_table, sine_table).astype(jnp.bfloat16)
     key_rot = rotary(key_lin, cosine_table, sine_table).astype(jnp.bfloat16)
     attended, log_sums = attend(query_rot, key_rot, value_bf, length, block_rows, heads_kv)
     attn_bf = attended.astype(jnp.bfloat16)
-    attn_rows = lax.psum_scatter(dot_last(attn_bf, full_out), "tp", scatter_dimension=0, tiled=True)
-    middle = resid_in + attn_rows
+    middle = resid_in + scatter_slot(dot_last(attn_bf, full_out))
     normed_mlp = rms_scale(middle, norm_mlp).astype(jnp.bfloat16)
-    mlp_input = lax.all_gather(normed_mlp, "tp", axis=0, tiled=True)
-    full_gate, full_up, full_down = (
-        lax.all_gather(low_gate, "fsdp", axis=0, tiled=True),
-        lax.all_gather(low_up, "fsdp", axis=0, tiled=True),
-        lax.all_gather(low_down, "fsdp", axis=0, tiled=True),
-    )
+    mlp_input = gather_group(normed_mlp)
     gate_lin = jnp.dot(mlp_input, full_gate, preferred_element_type=jnp.float32)
     up_lin = jnp.dot(mlp_input, full_up, preferred_element_type=jnp.float32)
     gate_sig = jax.nn.sigmoid(gate_lin)
     hidden_bf = (gate_lin * gate_sig * up_lin).astype(jnp.bfloat16)
-    mlp_rows = lax.psum_scatter(
-        dot_last(hidden_bf, full_down).astype(jnp.bfloat16), "tp", scatter_dimension=0, tiled=True
-    ).astype(jnp.float32)
-    block_out = (middle + mlp_rows).astype(jnp.bfloat16)
-    full_query, full_key, full_value, full_out, full_gate, full_up, full_down = (
-        lax.all_gather(low_query, "fsdp", axis=0, tiled=True),
-        lax.all_gather(low_key, "fsdp", axis=0, tiled=True),
-        lax.all_gather(low_value, "fsdp", axis=0, tiled=True),
-        lax.all_gather(low_out, "fsdp", axis=0, tiled=True),
-        lax.all_gather(low_gate, "fsdp", axis=0, tiled=True),
-        lax.all_gather(low_up, "fsdp", axis=0, tiled=True),
-        lax.all_gather(low_down, "fsdp", axis=0, tiled=True),
-    )
-    cotangent = out_grad.astype(jnp.float32) * row_valid[:, None]
-    mlp_grad_in = lax.all_gather(cotangent.astype(jnp.bfloat16), "tp", axis=0, tiled=True)
+    grad_down = dot_rows(mlp_grad_in, hidden_bf)
+    shard_down = scatter_wide(grad_down.astype(jnp.bfloat16))
     hidden_grad = jnp.dot(mlp_grad_in, full_down, preferred_element_type=jnp.float32)
-    grad_down = dot_rows(mlp_grad_in, hidden_bf)
     gate_grad = (hidden_grad * up_lin * gate_sig * (1.0 + gate_lin * (1.0 - gate_sig))).astype(
         jnp.bfloat16
     )
     up_grad = (hidden_grad * gate_lin * gate_sig).astype(jnp.bfloat16)
-    grad_gate = dot_rows(mlp_input, gate_grad)
-    grad_up = dot_rows(mlp_input, up_grad)
-    normed_mlp_grad = lax.psum_scatter(
-        dot_last(gate_grad, full_gate) + dot_last(up_grad, full_up),
-        "tp",
-        scatter_dimension=0,
-        tiled=True,
-    )
+    normed_mlp_grad = scatter_group(dot_last(gate_grad, full_gate) + dot_last(up_grad, full_up))
+    shard_gate = scatter_wide(dot_rows(mlp_input, gate_grad).astype(jnp.bfloat16))
+    shard_up = scatter_wide(dot_rows(mlp_input, up_grad).astype(jnp.bfloat16))
     middle_back, gain_mlp_part = norm_back(middle, norm_mlp, normed_mlp_grad)
     middle_grad = cotangent + middle_back
-    attn_grad_in = lax.all_gather(middle_grad.astype(jnp.bfloat16), "tp", axis=0, tiled=True)
+    attn_grad_in = gather_slot(middle_grad.astype(jnp.bfloat16))
     attended_grad = jnp.dot(attn_grad_in, full_out, preferred_element_type=jnp.float32).astype(
         jnp.bfloat16
     )
-    grad_proj = dot_rows(attn_grad_in, attn_bf)
     query_grad_rot, key_grad_rot, value_grad = attend_back(
         query_rot, key_rot, value_bf, attended_grad, log_sums, length, block_rows, heads_kv
     )
-    query_grad = (
-        rotary(query_grad_rot, cosine_table, -sine_table)
-        .astype(jnp.bfloat16)
-        .reshape(slot_rows, -1)
-    )
-    key_grad = (
-        rotary(key_grad_rot, cosine_table, -sine_table).astype(jnp.bfloat16).reshape(slot_rows, -1)
-    )
-    value_grad_bf = value_grad.astype(jnp.bfloat16).reshape(slot_rows, -1)
-    grad_query = dot_rows(attn_input, query_grad)
-    grad_key = dot_rows(attn_input, key_grad)
-    grad_value = dot_rows(attn_input, value_grad_bf)
-    normed_attn_grad = lax.psum_scatter(
-        dot_last(query_grad, full_query)
-        + dot_last(key_grad, full_key)
-        + dot_last(value_grad_bf, full_value),
-        "tp",
-        scatter_dimension=0,
-        tiled=True,
-    )
+    query_grad = rotary(query_grad_rot, cosine_table, -sine_table).reshape(slot_rows, -1)
+    key_grad = rotary(key_grad_rot, cosine_table, -sine_table).reshape(slot_rows, -1)
+    qkv_grad = jnp.concatenate(
+        [query_grad, key_grad, value_grad.reshape(slot_rows, -1)], axis=1
+    ).astype(jnp.bfloat16)
+    shard_qkv = scatter_chunks(dot_rows(attn_input, qkv_grad), all_bits[::-1], weight_rows)[0]
+    shard_out = scatter_chunks(dot_rows(attn_grad_in, attn_bf), all_bits[::-1], weight_rows)[0]
+    normed_attn_grad = scatter_slot(dot_last(qkv_grad, full_qkv))
     input_back, gain_attn_part = norm_back(resid_in, norm_attn, normed_attn_grad)
     input_grad = middle_grad + input_back
+    block_out = (middle + scatter_group(dot_last(hidden_bf, full_down))).astype(jnp.bfloat16)
     shard_grads = (
-        lax.psum_scatter(grad_query, "fsdp", scatter_dimension=0, tiled=True),
-        lax.psum_scatter(grad_key, "fsdp", scatter_dimension=0, tiled=True),
-        lax.psum_scatter(grad_value, "fsdp", scatter_dimension=0, tiled=True),
-        lax.psum_scatter(grad_proj, "fsdp", scatter_dimension=0, tiled=True),
-        lax.psum_scatter(grad_gate, "fsdp", scatter_dimension=0, tiled=True),
-        lax.psum_scatter(grad_up, "fsdp", scatter_dimension=0, tiled=True),
-        lax.psum_scatter(grad_down, "fsdp", scatter_dimension=0, tiled=True),
+        shard_qkv[:, :width_query],
+        shard_qkv[:, width_query : width_query + width_key],
+        shard_qkv[:, width_query + width_key :],
+        shard_out,
+        shard_gate,
+        shard_up,
+        shard_down,
     )
     square_part = jnp.zeros((), jnp.float32)
     for shard_grad in shard_grads:
         square_part = square_part + jnp.sum(shard_grad * shard_grad)
-    gain_attn_grad, gain_mlp_grad, square_total = lax.psum(
-        (gain_attn_part, gain_mlp_part, square_part), ("fsdp", "tp")
-    )
+    summed = sum_everywhere(
+        jnp.concatenate([gain_attn_part, gain_mlp_part, jnp.broadcast_to(square_part, (128,))])
+    )
+    gain_attn_grad = summed[: norm_attn.shape[0]]
+    gain_mlp_grad = summed[norm_attn.shape[0] : -128]
+    square_total = summed[-1]
     clip_norm = jnp.sqrt(
         square_total
         + jnp.sum(gain_attn_grad * gain_attn_grad)

time: 2380 us -> 1070 us (0.45)
  waiting for transfers between devices: 1940 us -> 426 us
  starting transfers between devices: 1.88 us -> 148 us
  local copies, waits for them, and re-layouts: 24.1 us -> 150 us
  blocking collectives: 40 us -> 0 us
  matrix products: 240 us -> 203 us
  other arithmetic: 86.4 us -> 117 us
    reduce_scatter x11 -> x0, waiting for transfers between devices: 1320 us -> none  [the longest x1 285 us: on_device(): lax.psum_scatter(grad_gate, 'fsdp', scatter_dimension=0, tiled=True)]
    all_gather x11 -> x0, waiting for transfers between devices: 620 us -> none  [the longest x1 128 us: on_device(): lax.all_gather(low_down, 'fsdp', axis=0, tiled=True)]
    ppermute x0 -> x115, waiting for transfers between devices: none -> 426 us  [swap(): return lax.ppermute(value, AXES, pairs)]
    ppermute x0 -> x115, starting transfers between devices: none -> 148 us  [swap(): return lax.ppermute(value, AXES, pairs)]
    unnamed x138 -> x242, local copies, waits for them, and re-layouts: 14.9 us -> 83.3 us
    psum x1 -> x0, blocking collectives: 40 us -> none  [on_device(): lax.psum((gain_attn_part, gain_mlp_part, square_part), ('fsdp', 'tp'))]
    dynamic_update_slice x0 -> x44, local copies, waits for them, and re-layouts: none -> 31.1 us  [the longest x38 30.4 us: assemble(): whole = lax.dynamic_update_slice_in_dim(whole, chunk, (me ^ mask) * rows, 0)]
    dot_general x7 -> x5, matrix products: 68.9 us -> 43.9 us  [dot_rows(): lax.dot_general(left, right, (((0,), (0,)), ((), ())), preferred_element_...]
  transfers between devices with their start and end apart: 22 -> 115, of which waited for: 21 -> 52; matrix products, arithmetic and copies ran while one was open for 8% -> 26% of each run, Pallas kernels for 0% -> 0%
where the time goes in v1:
time: 1070 us; the launch traced here: 1060 us
  waiting for transfers between devices  426 us (40%)
  matrix products  203 us (19%)
  local copies, waits for them, and re-layouts  150 us (14%)
  starting transfers between devices  148 us (14%)
  other arithmetic  117 us (11%)
  between operations  10.9 us (1%)
    ppermute x115, waiting for transfers between devices, swap(): return lax.ppermute(value, AXES, pairs)  426 us
    ppermute x115, starting transfers between devices, swap(): return lax.ppermute(value, AXES, pairs)  148 us
    unnamed x242, local copies, waits for them, and re-layouts  83.3 us
    dot_general x5, matrix products, dot_last(): lax.dot_general(left, right, (((1,), (1,)), ((), ())), preferred_element_...  62 us
    dot_general x5, matrix products, dot_rows(): lax.dot_general(left, right, (((0,), (0,)), ((), ())), preferred_element_...  43.9 us
    dynamic_update_slice x38, local copies, waits for them, and re-layouts, assemble(): whole = lax.dynamic_update_slice_in_dim(whole, chunk, (me ^ mask) * rows, 0)  30.4 us
    mul x5, other arithmetic, adam_step(): -LEARN_RATE  22.9 us
    dot_general x1, matrix products, on_device(): gate_lin = jnp.dot(mlp_input, full_gate, preferred_element_type=jnp.float32)  21.9 us
  transfers between devices with their start and end apart: 115, of which 52 were waited for; matrix products, arithmetic and copies ran while one was open for 26% of the time, Pallas kernels for 0%

profile of v1, /device:TPU:0, one launch (start us, length us, event | category | flops | bytes accessed | tf_op | source)
XLA Modules:
  0.0 1062.5 jit_solution(17117058604726334180)
XLA Ops:
  38.3 5.8 collective-permute-done.10
  55.2 11.0 %collective-permute-done.41 = bf16[256,1024]{1,0:T(8,128)(2,1)} collective-permute-done((bf16[256,1024]{1,0:T(8,128)(2,1)}, bf16[256,1024]{1,0:T(8,128)(2,1)}, u32[]{:S(2)}, u32[]{:S(2)}) %collective-permute-start.41) | collective-permute-done | bytes 524320 | tf_op jit(solution)/shard_map/ppermute | solution.py:181
  73.4 15.2 %collective-permute-done.34 = bf16[256,1024]{1,0:T(8,128)(2,1)S(1)} collective-permute-done((bf16[256,1024]{1,0:T(8,128)(2,1)}, bf16[256,1024]{1,0:T(8,128)(2,1)S(1)}, u32[]{:S(2)}, u32[]{:S(2)}) %collective-permute-start.34) | collective-permute-done | bytes 524320 | tf_op jit(solution)/shard_map/ppermute | solution.py:181
  95.5 15.6 %collective-permute-done.27 = bf16[256,1024]{1,0:T(8,128)(2,1)S(1)} collective-permute-done((bf16[256,1024]{1,0:T(8,128)(2,1)}, bf16[256,1024]{1,0:T(8,128)(2,1)S(1)}, u32[]{:S(2)}, u32[]{:S(2)}) %collective-permute-start.27) | collective-permute-done | bytes 524320 | tf_op jit(solution)/shard_map/ppermute | solution.py:181
  128.8 5.6 collective-permute-done.16
  139.0 6.7 collective-permute-done.7
  147.2 9.7 collective-permute-done.8
  161.7 26.8 %collective-permute-done.9 = bf16[256,1024]{1,0:T(8,128)(2,1)S(1)} collective-permute-done((bf16[256,1024]{1,0:T(8,128)(2,1)S(1)}, bf16[256,1024]{1,0:T(8,128)(2,1)S(1)}, u32[]{:S(2)}, u32[]{:S(2)}) %collective-permute-start.9) | collective-permute-done | bytes 524320 | tf_op jit(solution)/shard_map/ppermute | solution.py:181
  190.8 4.6 fusion.122
  208.6 17.2 %while.27 = (s32[]{:T(128)}, bf16[2,512,512]{2,1,0:T(8,128)(2,1)}, f32[2,1,2,512]{3,2,1,0:T(2,128)S(1)}, s32[2]{0:T(128)S(1)}, s32[]{:T(128)}, /*index=5*/bf16[1...) while((s32[]{:T(128)}, bf16[2,512,512]{2,1,0:T(8,128)(2,1)}, ...), condition=%wide.region_4.5_spmd, body=%wide.region_1.4_spmd.sunk | while | flops 1087373824 | bytes 18913484 | solution.py:102
  225.9 4.5 fusion.123
  236.4 16.7 %collective-permute-done.36 = bf16[256,1024]{1,0:T(8,128)(2,1)S(1)} collective-permute-done((bf16[256,1024]{1,0:T(8,128)(2,1)S(1)}, bf16[256,1024]{1,0:T(8,128)(2,1)S(1)}, u32[]{:S(2)}, u32[]{:S(2)}) %collective-permute-start.36) | collective-permute-done | bytes 524320 | tf_op jit(solution)/shard_map/ppermute | solution.py:181
  261.1 6.7 collective-permute-done.39
  269.4 9.7 collective-permute-done.30
  282.6 7.8 collective-permute-done.31
  293.4 8.1 collective-permute-done.32
  303.8 9.0 collective-permute-done.47
  316.3 7.8 collective-permute-done.40
  324.1 10.2 collective-permute-done.33
  344.8 14.0 %collective-permute-done.20 = bf16[256,2048]{1,0:T(8,128)(2,1)S(1)} collective-permute-done((bf16[256,2048]{1,0:T(8,128)(2,1)S(1)}, bf16[256,2048]{1,0:T(8,128)(2,1)S(1)}, u32[]{:S(2)}, u32[]{:S(2)}) %collective-permute-start.20) | collective-permute-done | bytes 1048608 | tf_op jit(solution)/shard_map/ppermute | solution.py:181
  358.8 13.6 %fusion.125 = f32[2048,1024]{1,0:T(8,128)} fusion(bf16[2048,2048]{1,0:T(8,128)(2,1)} %constant_dynamic-update-slice_fusion.9, bf16[2048,1024]{1,0:T(8,128)(2,1)S(1)} %constant_dynamic-update-slice_fusion.21), kind=kOutput, calls=%fused_computation.338 | convolution fusion | flops 8589934592 | bytes 20971520 | tf_op jit(solution)/shard_map/dot_general | solution.py:378
  380.6 11.0 %fusion.124 = f32[2048,1024]{1,0:T(8,128)} fusion(bf16[2048,2048]{1,0:T(8,128)(2,1)S(1)} %constant_dynamic-update-slice_fusion.1, bf16[2048,1024]{1,0:T(8,128)(2,1)S(1)} %constant_dynamic-update-slice_fusion.29), kind=kOutput, calls=%fused_computation.337 | convolution fusion | flops 8589934592 | bytes 20971520 | tf_op jit(solution)/shard_map/dot_general | solution.py:373
  391.6 21.9 %multiply_convert_fusion.1 = (bf16[2048,1024]{1,0:T(8,128)(2,1)}, bf16[2048,1024]{1,0:T(8,128)(2,1)}, bf16[2048,1024]{1,0:T(8,128)(2,1)}) fusion(f32[2048,1024]{1,0:T(8,128)} %fusion.125, f32[2048,1024]{1,0:T(8,128)} %fusion.124, bf16[2048,2048]{1,0:T(8,128)(2,1)} %copy-done.76, bf16[2048,1024]{1,0:T(8,128)(2,1)} %constant_dynamic-update-slice_fusion.37), kind=kOutput, calls=%fused_computation.62 | convolution fusion | flops 8623489024 | bytes 41943040 | tf_op jit(solution)/shard_map/dot_general | solution.py:372
  413.5 15.6 %fusion.126 = f32[2048,2048]{1,0:T(8,128)} fusion(bf16[2048,1024]{1,0:T(8,128)(2,1)} %get-tuple-element.414, bf16[2048,1024]{1,0:T(8,128)(2,1)} %copy-done.31), kind=kOutput, calls=%fused_computation.339 | convolution fusion | flops 8589934592 | bytes 25165824 | tf_op jit(solution)/shard_map/dot_general | solution.py:63
  429.1 11.2 %convolution_convert_fusion.1 = bf16[2048,1024]{0,1:T(8,128)(2,1)} fusion(bf16[2048,2048]{1,0:T(8,128)(2,1)S(1)} %copy-done.77, bf16[2048,1024]{1,0:T(8,128)(2,1)S(1)} %copy-done.102), kind=kOutput, calls=%fused_computation.73 | convolution fusion | flops 8592031744 | bytes 16777216 | tf_op jit(solution)/shard_map/dot_general | solution.py:57
  440.3 16.1 %fusion.121 = (bf16[2048,2048]{1,0:T(8,128)(2,1)}, f32[2048,2048]{1,0:T(8,128)}) fusion(bf16[2048,1024]{1,0:T(8,128)(2,1)} %get-tuple-element.413, bf16[2048,1024]{1,0:T(8,128)(2,1)S(1)} %constant_dynamic-update-slice_fusion.21), kind=kOutput, calls=%fused_computation.334 | convolution fusion | flops 8594128896 | bytes 33554432 | tf_op jit(solution)/shard_map/dot_general | solution.py:63
  456.4 14.1 %convolution_convert_fusion = bf16[2048,1024]{0,1:T(8,128)(2,1)} fusion(bf16[2048,2048]{1,0:T(8,128)(2,1)} %constant_dynamic-update-slice_fusion.9, bf16[2048,1024]{1,0:T(8,128)(2,1)} %get-tuple-element.413), kind=kOutput, calls=%fused_computation.72 | convolution fusion | flops 8592031744 | bytes 16777216 | tf_op jit(solution)/shard_map/dot_general | solution.py:57
  470.5 11.6 %convolution_convert_fusion.2 = bf16[2048,1024]{0,1:T(8,128)(2,1)} fusion(bf16[2048,2048]{1,0:T(8,128)(2,1)S(1)} %copy-done.77, bf16[2048,1024]{1,0:T(8,128)(2,1)S(1)} %copy-done.101), kind=kOutput, calls=%fused_computation.74 | convolution fusion | flops 8592031744 | bytes 16777216 | tf_op jit(solution)/shard_map/dot_general | solution.py:57
  482.0 19.1 %fusion.120 = (bf16[2048,2048]{1,0:T(8,128)(2,1)}, f32[2048,2048]{1,0:T(8,128)}) fusion(f32[2048,2048]{1,0:T(8,128)} %fusion.126, bf16[2048,1024]{1,0:T(8,128)(2,1)} %get-tuple-element.412, bf16[2048,1024]{1,0:T(8,128)(2,1)} %constant_dynamic-update-slice_fusion.37), kind=kOutput, calls=%fused_computation.333 | convolution fusion | flops 8598323200 | bytes 50331648 | tf_op jit(solution)/shard_map/dot_general | solution.py:63
  501.1 4.2 fusion.117
  522.5 4.5 collective-permute-done.93
  527.0 11.3 %collective-permute-done.92 = bf16[256,1024]{0,1:T(8,128)(2,1)} collective-permute-done((bf16[256,1024]{0,1:T(8,128)(2,1)}, bf16[256,1024]{0,1:T(8,128)(2,1)}, u32[]{:S(2)}, u32[]{:S(2)}) %collective-permute-start.92) | collective-permute-done | bytes 524320 | tf_op jit(solution)/shard_map/ppermute | solution.py:181
  539.8 9.8 collective-permute-done.90
  555.2 5.6 collective-permute-done.100
  560.8 11.2 %collective-permute-done.99 = bf16[256,1024]{0,1:T(8,128)(2,1)} collective-permute-done((bf16[256,1024]{0,1:T(8,128)(2,1)}, bf16[256,1024]{0,1:T(8,128)(2,1)}, u32[]{:S(2)}, u32[]{:S(2)}) %collective-permute-start.99) | collective-permute-done | bytes 524320 | tf_op jit(solution)/shard_map/ppermute | solution.py:181
  572.0 10.7 %collective-permute-done.97 = bf16[256,1024]{0,1:T(8,128)(2,1)} collective-permute-done((bf16[256,1024]{0,1:T(8,128)(2,1)}, bf16[256,1024]{0,1:T(8,128)(2,1)}, u32[]{:S(2)}, u32[]{:S(2)}) %collective-permute-start.97) | collective-permute-done | bytes 524320 | tf_op jit(solution)/shard_map/ppermute | solution.py:181
  589.9 9.0 collective-permute-done.107
  601.1 23.9 %collective-permute-done.94 = bf16[256,1024]{0,1:T(8,128)(2,1)S(1)} collective-permute-done((bf16[256,1024]{0,1:T(8,128)(2,1)S(1)}, bf16[256,1024]{0,1:T(8,128)(2,1)S(1)}, u32[]{:S(2)}, u32[]{:S(2)}) %collective-permute-start.94) | collective-permute-done | bytes 524320 | tf_op jit(solution)/shard_map/ppermute | solution.py:181
  626.6 8.1 collective-permute-done.101
  642.0 7.9 collective-permute-start.104
  649.9 12.9 %collective-permute-done.50 = bf16[256,2048]{1,0:T(8,128)(2,1)S(1)} collective-permute-done((bf16[256,2048]{1,0:T(8,128)(2,1)S(1)}, bf16[256,2048]{1,0:T(8,128)(2,1)S(1)}, u32[]{:S(2)}, u32[]{:S(2)}) %collective-permute-start.50) | collective-permute-done | bytes 1048608 | tf_op jit(solution)/shard_map/ppermute | solution.py:181
  667.3 5.4 multiply_reduce_fusion.3
  686.0 8.8 collective-permute-start.89
  697.5 13.6 %collective-permute-start.96 = (bf16[256,1024]{0,1:T(8,128)(2,1)}, bf16[256,1024]{0,1:T(8,128)(2,1)}, u32[]{:S(2)}, u32[]{:S(2)}) collective-permute-start(bf16[256,1024]{0,1:T(8,128)(2,1)} %get-tuple-element.446), channel_id=1, source_target_pairs={{0,4},{1,5},{2,6},{3,7},{4,0},{5,1},{6,2},{7,3},{8,12},{9,13},{10,... | collective-permute-start | bytes 1572872 | tf_op jit(solution)/shard_map/ppermute | solution.py:181
  711.1 7.6 collective-permute-done.109
  725.2 4.5 collective-permute-start.70
  736.4 19.7 %collective-permute-done.98 = bf16[256,1024]{0,1:T(8,128)(2,1)} collective-permute-done((bf16[256,1024]{0,1:T(8,128)(2,1)}, bf16[256,1024]{0,1:T(8,128)(2,1)}, u32[]{:S(2)}, u32[]{:S(2)}) %collective-permute-start.98) | collective-permute-done | bytes 524320 | tf_op jit(solution)/shard_map/ppermute | solution.py:181
  762.3 4.9 convolution_convert_fusion.3
  767.2 49.9 %while.28 = (s32[]{:T(128)}, f32[1024,1,256]{0,2,1:T(8,128)}, f32[1024,1,256]{0,2,1:T(8,128)}, f32[2,512,2,256]{3,1,0,2:T(8,128)}, s32[2]{0:T(128)S(1)}, /*index...) while((s32[]{:T(128)}, f32[1024,1,256]{0,2,1:T(8,128)}, ...), condition=%wide.region_9.10_spmd.clone, body=%wide.region_7.9_spmd.clone.sunk | while | flops 2703229440 | bytes 94931344 | solution.py:152
  776.8 4.6 fusion.199
  800.9 4.6 fusion.199
  824.5 6.7 fusion.76
  831.3 4.7 fusion.75
  837.9 5.4 collective-permute-start.76
  845.9 10.1 collective-permute-done.76
  858.0 9.2 collective-permute-done.79
  884.3 10.3 collective-permute-done.85
  900.6 13.0 %collective-permute-done.82 = bf16[256,512]{1,0:T(8,128)(2,1)S(1)} collective-permute-done((bf16[256,512]{1,0:T(8,128)(2,1)S(1)}, bf16[256,512]{1,0:T(8,128)(2,1)S(1)}, u32[]{:S(2)}, u32[]{:S(2)}) %collective-permute-start.82) | collective-permute-done | bytes 262176 | tf_op jit(solution)/shard_map/ppermute | solution.py:181
  917.8 19.8 %collective-permute-done.88 = bf16[256,512]{1,0:T(8,128)(2,1)S(1)} collective-permute-done((bf16[256,512]{1,0:T(8,128)(2,1)S(1)}, bf16[256,512]{1,0:T(8,128)(2,1)S(1)}, u32[]{:S(2)}, u32[]{:S(2)}) %collective-permute-start.88) | collective-permute-done | bytes 262176 | tf_op jit(solution)/shard_map/ppermute | solution.py:181
  943.1 5.7 collective-permute-done.81
  956.5 6.5 collective-permute-done.74
  962.9 4.4 fusion.59
  1014.7 6.5 add_multiply_fusion.2
  1024.2 10.2 add_multiply_fusion
  (637 shorter events, 410.0 us)
Async XLA Ops:
  5.2 44.7 %collective-permute-start.3 = (bf16[256,1024]{1,0:T(8,128)(2,1)}, bf16[256,1024]{1,0:T(8,128)(2,1)}, u32[]{:S(2)}, u32[]{:S(2)}) collective-permute-start(bf16[256,1024]{1,0:T(8,128)(2,1)} %get-tuple-element.475), channel_id=1, source_target_pairs={{0,16},{1,17},{2,18},{3,19},{4,20},{5,21},{6,22},{7,23},{8,24},{9,... | collective-permute-start | bytes 1572872 | tf_op jit(solution)/shard_map/ppermute | solution.py:181
  9.2 41.4 %collective-permute-start.4 = (bf16[256,1024]{1,0:T(8,128)(2,1)}, bf16[256,1024]{1,0:T(8,128)(2,1)}, u32[]{:S(2)}, u32[]{:S(2)}) collective-permute-start(bf16[256,1024]{1,0:T(8,128)(2,1)} %get-tuple-element.475), channel_id=1, source_target_pairs={{0,8},{1,9},{2,10},{3,11},{4,12},{5,13},{6,14},{7,15},{8,0},{9,1},... | collective-permute-start | bytes 1572872 | tf_op jit(solution)/shard_map/ppermute | solution.py:181
  14.2 29.9 %collective-permute-start.10 = (bf16[256,512]{1,0:T(8,128)(2,1)}, bf16[256,512]{1,0:T(8,128)(2,1)}, u32[]{:S(2)}, u32[]{:S(2)}) collective-permute-start(bf16[256,512]{1,0:T(8,128)(2,1)} %get-tuple-element.403), channel_id=1, source_target_pairs={{0,16},{1,17},{2,18},{3,19},{4,20},{5,21},{6,22},{7,23},{8,24},{9,... | collective-permute-start | bytes 786440 | tf_op jit(solution)/shard_map/ppermute | solution.py:181
  14.7 31.1 %collective-permute-start.11 = (bf16[256,512]{1,0:T(8,128)(2,1)}, bf16[256,512]{1,0:T(8,128)(2,1)S(1)}, u32[]{:S(2)}, u32[]{:S(2)}) collective-permute-start(bf16[256,512]{1,0:T(8,128)(2,1)} %get-tuple-element.403), channel_id=1, source_target_pairs={{0,8},{1,9},{2,10},{3,11},{4,12},{5,13},{6,14},{7,15},{8,0},{9,1},... | collective-permute-start | bytes 786440 | tf_op jit(solution)/shard_map/ppermute | solution.py:181
  19.9 46.3 %collective-permute-start.41 = (bf16[256,1024]{1,0:T(8,128)(2,1)}, bf16[256,1024]{1,0:T(8,128)(2,1)}, u32[]{:S(2)}, u32[]{:S(2)}) collective-permute-start(bf16[256,1024]{1,0:T(8,128)(2,1)} %get-tuple-element.464), channel_id=1, source_target_pairs={{0,8},{1,9},{2,10},{3,11},{4,12},{5,13},{6,14},{7,15},{8,0},{9,1},... | collective-permute-start | bytes 1572872 | tf_op jit(solution)/shard_map/ppermute | solution.py:181
  44.1 27.4 %collective-permute-start.42 = (bf16[256,1024]{1,0:T(8,128)(2,1)}, bf16[256,1024]{1,0:T(8,128)(2,1)}, u32[]{:S(2)}, u32[]{:S(2)}) collective-permute-start(bf16[256,1024]{1,0:T(8,128)(2,1)} %get-tuple-element.393), channel_id=1, source_target_pairs={{0,16},{1,17},{2,18},{3,19},{4,20},{5,21},{6,22},{7,23},{8,24},{9,... | collective-permute-start | bytes 1572872 | tf_op jit(solution)/shard_map/ppermute | solution.py:181
  45.8 42.8 %collective-permute-start.34 = (bf16[256,1024]{1,0:T(8,128)(2,1)}, bf16[256,1024]{1,0:T(8,128)(2,1)S(1)}, u32[]{:S(2)}, u32[]{:S(2)}) collective-permute-start(bf16[256,1024]{1,0:T(8,128)(2,1)} %get-tuple-element.466), channel_id=1, source_target_pairs={{0,8},{1,9},{2,10},{3,11},{4,12},{5,13},{6,14},{7,15},{8,0},{9,1},... | collective-permute-start | bytes 1572872 | tf_op jit(solution)/shard_map/ppermute | solution.py:181
  49.9 44.0 %collective-permute-start.35 = (bf16[256,1024]{1,0:T(8,128)(2,1)}, bf16[256,1024]{1,0:T(8,128)(2,1)S(1)}, u32[]{:S(2)}, u32[]{:S(2)}) collective-permute-start(bf16[256,1024]{1,0:T(8,128)(2,1)} %get-tuple-element.397), channel_id=1, source_target_pairs={{0,16},{1,17},{2,18},{3,19},{4,20},{5,21},{6,22},{7,23},{8,24},{9,... | collective-permute-start | bytes 1572872 | tf_op jit(solution)/shard_map/ppermute | solution.py:181
  50.6 60.4 %collective-permute-start.27 = (bf16[256,1024]{1,0:T(8,128)(2,1)}, bf16[256,1024]{1,0:T(8,128)(2,1)S(1)}, u32[]{:S(2)}, u32[]{:S(2)}) collective-permute-start(bf16[256,1024]{1,0:T(8,128)(2,1)} %get-tuple-element.465), channel_id=1, source_target_pairs={{0,8},{1,9},{2,10},{3,11},{4,12},{5,13},{6,14},{7,15},{8,0},{9,1},... | collective-permute-start | bytes 1572872 | tf_op jit(solution)/shard_map/ppermute | solution.py:181
  66.2 53.4 %collective-permute-start.6 = (bf16[256,1024]{1,0:T(8,128)(2,1)}, bf16[256,1024]{1,0:T(8,128)(2,1)S(1)}, u32[]{:S(2)}, u32[]{:S(2)}) collective-permute-start(bf16[256,1024]{1,0:T(8,128)(2,1)} %get-tuple-element.475), channel_id=1, source_target_pairs={{0,4},{1,5},{2,6},{3,7},{4,0},{5,1},{6,2},{7,3},{8,12},{9,13},{10,... | collective-permute-start | bytes 1572872 | tf_op jit(solution)/shard_map/ppermute | solution.py:181
  71.5 49.6 %collective-permute-start.28 = (bf16[256,1024]{1,0:T(8,128)(2,1)S(1)}, bf16[256,1024]{1,0:T(8,128)(2,1)S(1)}, u32[]{:S(2)}, u32[]{:S(2)}) collective-permute-start(bf16[256,1024]{1,0:T(8,128)(2,1)S(1)} %get-tuple-element.395), channel_id=1, source_target_pairs={{0,16},{1,17},{2,18},{3,19},{4,20},{5,21},{6,22},{7,23},{8,24},{9,... | collective-permute-start | bytes 1572872 | tf_op jit(solution)/shard_map/ppermute | solution.py:181
  111.0 27.8 %collective-permute-start = (bf16[256,2048]{1,0:T(8,128)(2,1)S(1)}, bf16[256,2048]{1,0:T(8,128)(2,1)S(1)}, u32[]{:S(2)}, u32[]{:S(2)}) collective-permute-start(bf16[256,2048]{1,0:T(8,128)(2,1)S(1)} %get-tuple-element.405), channel_id=1, source_target_pairs={{0,2},{1,3},{2,0},{3,1},{4,6},{5,7},{6,4},{7,5},{8,10},{9,11},{10,... | collective-permute-start | bytes 3145736 | tf_op jit(solution)/shard_map/ppermute | solution.py:181
  128.8 31.2 %collective-permute-start.1 = (bf16[256,2048]{1,0:T(8,128)(2,1)S(1)}, bf16[256,2048]{1,0:T(8,128)(2,1)S(1)}, u32[]{:S(2)}, u32[]{:S(2)}) collective-permute-start(bf16[256,2048]{1,0:T(8,128)(2,1)S(1)} %get-tuple-element.405), channel_id=1, source_target_pairs={{0,1},{1,0},{2,3},{3,2},{4,5},{5,4},{6,7},{7,6},{8,9},{9,8},{10,11... | collective-permute-start | bytes 3145736 | tf_op jit(solution)/shard_map/ppermute | solution.py:181
  138.9 51.2 %collective-permute-start.2 = (bf16[256,2048]{1,0:T(8,128)(2,1)S(1)}, bf16[256,2048]{1,0:T(8,128)(2,1)S(1)}, u32[]{:S(2)}, u32[]{:S(2)}) collective-permute-start(bf16[256,2048]{1,0:T(8,128)(2,1)S(1)} %collective-permute-done), channel_id=1, source_target_pairs={{0,1},{1,0},{2,3},{3,2},{4,5},{5,4},{6,7},{7,6},{8,9},{9,8},{10,11... | collective-permute-start | bytes 3145736 | tf_op jit(solution)/shard_map/ppermute | solution.py:181
  145.7 84.8 %collective-permute-start.44 = (bf16[256,1024]{1,0:T(8,128)(2,1)}, bf16[256,1024]{1,0:T(8,128)(2,1)}, u32[]{:S(2)}, u32[]{:S(2)}) collective-permute-start(bf16[256,1024]{1,0:T(8,128)(2,1)} %get-tuple-element.393), channel_id=1, source_target_pairs={{0,4},{1,5},{2,6},{3,7},{4,0},{5,1},{6,2},{7,3},{8,12},{9,13},{10,... | collective-permute-start | bytes 1572872 | tf_op jit(solution)/shard_map/ppermute | solution.py:181
  156.9 97.7 %collective-permute-start.37 = (bf16[256,1024]{1,0:T(8,128)(2,1)}, bf16[256,1024]{1,0:T(8,128)(2,1)}, u32[]{:S(2)}, u32[]{:S(2)}) collective-permute-start(bf16[256,1024]{1,0:T(8,128)(2,1)} %get-tuple-element.397), channel_id=1, source_target_pairs={{0,4},{1,5},{2,6},{3,7},{4,0},{5,1},{6,2},{7,3},{8,12},{9,13},{10,... | collective-permute-start | bytes 1572872 | tf_op jit(solution)/shard_map/ppermute | solution.py:181
  158.5 30.0 %collective-permute-start.9 = (bf16[256,1024]{1,0:T(8,128)(2,1)S(1)}, bf16[256,1024]{1,0:T(8,128)(2,1)S(1)}, u32[]{:S(2)}, u32[]{:S(2)}) collective-permute-start(bf16[256,1024]{1,0:T(8,128)(2,1)S(1)} %collective-permute-done.5), channel_id=1, source_target_pairs={{0,4},{1,5},{2,6},{3,7},{4,0},{5,1},{6,2},{7,3},{8,12},{9,13},{10,... | collective-permute-start | bytes 1572872 | tf_op jit(solution)/shard_map/ppermute | solution.py:181
  160.0 96.4 %collective-permute-start.55 = (bf16[256,2048]{1,0:T(8,128)(2,1)}, bf16[256,2048]{1,0:T(8,128)(2,1)}, u32[]{:S(2)}, u32[]{:S(2)}) collective-permute-start(bf16[256,2048]{1,0:T(8,128)(2,1)} %get-tuple-element.391), channel_id=1, source_target_pairs={{0,2},{1,9},{2,0},{3,11},{4,6},{5,13},{6,4},{7,15},{8,10},{9,1},{1... | collective-permute-start | bytes 3145736 | tf_op jit(solution)/shard_map/ppermute | solution.py:181
  188.5 42.5 %collective-permute-start.45 = (bf16[256,1024]{1,0:T(8,128)(2,1)}, bf16[256,1024]{1,0:T(8,128)(2,1)}, u32[]{:S(2)}, u32[]{:S(2)}) collective-permute-start(bf16[256,1024]{1,0:T(8,128)(2,1)} %collective-permute-done.41), channel_id=1, source_target_pairs={{0,4},{1,5},{2,6},{3,7},{4,0},{5,1},{6,2},{7,3},{8,12},{9,13},{10,... | collective-permute-start | bytes 1572872 | tf_op jit(solution)/shard_map/ppermute | solution.py:181
  190.1 42.8 %collective-permute-start.46 = (bf16[256,1024]{1,0:T(8,128)(2,1)}, bf16[256,1024]{1,0:T(8,128)(2,1)}, u32[]{:S(2)}, u32[]{:S(2)}) collective-permute-start(bf16[256,1024]{1,0:T(8,128)(2,1)} %collective-permute-done.42), channel_id=1, source_target_pairs={{0,4},{1,5},{2,6},{3,7},{4,0},{5,1},{6,2},{7,3},{8,12},{9,13},{10,... | collective-permute-start | bytes 1572872 | tf_op jit(solution)/shard_map/ppermute | solution.py:181
  232.9 47.7 %collective-permute-start.18 = (bf16[256,2048]{1,0:T(8,128)(2,1)S(1)}, bf16[256,2048]{1,0:T(8,128)(2,1)S(1)}, u32[]{:S(2)}, u32[]{:S(2)}) collective-permute-start(bf16[256,2048]{1,0:T(8,128)(2,1)S(1)} %get-tuple-element.434), channel_id=1, source_target_pairs={{0,1},{1,0},{2,3},{3,2},{4,5},{5,4},{6,7},{7,6},{8,9},{9,8},{10,11... | collective-permute-start | bytes 3145736 | tf_op jit(solution)/shard_map/ppermute | solution.py:181
  254.6 26.9 %collective-permute-start.56 = (bf16[256,2048]{1,0:T(8,128)(2,1)}, bf16[256,2048]{1,0:T(8,128)(2,1)S(1)}, u32[]{:S(2)}, u32[]{:S(2)}) collective-permute-start(bf16[256,2048]{1,0:T(8,128)(2,1)} %get-tuple-element.391), channel_id=1, source_target_pairs={{0,8},{1,3},{2,10},{3,1},{4,12},{5,7},{6,14},{7,5},{8,0},{9,11},{1... | collective-permute-start | bytes 3145736 | tf_op jit(solution)/shard_map/ppermute | solution.py:181
  280.6 32.2 %collective-permute-start.47 = (bf16[256,1024]{1,0:T(8,128)(2,1)S(1)}, bf16[256,1024]{1,0:T(8,128)(2,1)S(1)}, u32[]{:S(2)}, u32[]{:S(2)}) collective-permute-start(bf16[256,1024]{1,0:T(8,128)(2,1)S(1)} %copy-done.66), channel_id=1, source_target_pairs={{0,4},{1,5},{2,6},{3,7},{4,0},{5,1},{6,2},{7,3},{8,12},{9,13},{10,... | collective-permute-start | bytes 1572872 | tf_op jit(solution)/shard_map/ppermute | solution.py:181
  281.5 53.7 %collective-permute-start.57 = (bf16[256,2048]{1,0:T(8,128)(2,1)}, bf16[256,2048]{1,0:T(8,128)(2,1)S(1)}, u32[]{:S(2)}, u32[]{:S(2)}) collective-permute-start(bf16[256,2048]{1,0:T(8,128)(2,1)} %collective-permute-done.55), channel_id=1, source_target_pairs={{0,8},{1,3},{2,10},{3,1},{4,12},{5,7},{6,14},{7,5},{8,0},{9,11},{1... | collective-permute-start | bytes 3145736 | tf_op jit(solution)/shard_map/ppermute | solution.py:181
  282.6 53.1 %collective-permute-start.17 = (bf16[256,2048]{1,0:T(8,128)(2,1)S(1)}, bf16[256,2048]{1,0:T(8,128)(2,1)S(1)}, u32[]{:S(2)}, u32[]{:S(2)}) collective-permute-start(bf16[256,2048]{1,0:T(8,128)(2,1)S(1)} %get-tuple-element.433), channel_id=1, source_target_pairs={{0,1},{1,0},{2,3},{3,2},{4,5},{5,4},{6,7},{7,6},{8,9},{9,8},{10,11... | collective-permute-start | bytes 3145736 | tf_op jit(solution)/shard_map/ppermute | solution.py:181
  290.3 45.4 %collective-permute-start.19 = (bf16[256,2048]{1,0:T(8,128)(2,1)S(1)}, bf16[256,2048]{1,0:T(8,128)(2,1)S(1)}, u32[]{:S(2)}, u32[]{:S(2)}) collective-permute-start(bf16[256,2048]{1,0:T(8,128)(2,1)S(1)} %add_convert_fusion.1), channel_id=1, source_target_pairs={{0,2},{1,3},{2,0},{3,1},{4,6},{5,7},{6,4},{7,5},{8,10},{9,11},{10,... | collective-permute-start | bytes 3145736 | tf_op jit(solution)/shard_map/ppermute | solution.py:181
  344.6 27.7 %collective-permute-start.21 = (bf16[256,2048]{1,0:T(8,128)(2,1)S(1)}, bf16[256,2048]{1,0:T(8,128)(2,1)S(1)}, u32[]{:S(2)}, u32[]{:S(2)}) collective-permute-start(bf16[256,2048]{1,0:T(8,128)(2,1)S(1)} %get-tuple-element.399), channel_id=1, source_target_pairs={{0,8},{1,3},{2,10},{3,1},{4,12},{5,7},{6,14},{7,5},{8,0},{9,11},{1... | collective-permute-start | bytes 3145736 | tf_op jit(solution)/shard_map/ppermute | solution.py:181
  344.6 30.4 %collective-permute-start.23 = (bf16[256,2048]{1,0:T(8,128)(2,1)S(1)}, bf16[256,2048]{1,0:T(8,128)(2,1)S(1)}, u32[]{:S(2)}, u32[]{:S(2)}) collective-permute-start(bf16[256,2048]{1,0:T(8,128)(2,1)S(1)} %get-tuple-element.399), channel_id=1, source_target_pairs={{0,1},{1,0},{2,3},{3,2},{4,5},{5,4},{6,7},{7,6},{8,9},{9,8},{10,11... | collective-permute-start | bytes 3145736 | tf_op jit(solution)/shard_map/ppermute | solution.py:181
  510.1 40.9 %collective-permute-start.49 = (bf16[256,2048]{1,0:T(8,128)(2,1)}, bf16[256,2048]{1,0:T(8,128)(2,1)S(1)}, u32[]{:S(2)}, u32[]{:S(2)}) collective-permute-start(bf16[256,2048]{1,0:T(8,128)(2,1)} %get-tuple-element.432), channel_id=1, source_target_pairs={{0,1},{1,0},{2,3},{3,2},{4,5},{5,4},{6,7},{7,6},{8,9},{9,8},{10,11... | collective-permute-start | bytes 3145736 | tf_op jit(solution)/shard_map/ppermute | solution.py:181
  510.4 41.1 %collective-permute-start.52 = (bf16[256,2048]{1,0:T(8,128)(2,1)S(1)}, bf16[256,2048]{1,0:T(8,128)(2,1)S(1)}, u32[]{:S(2)}, u32[]{:S(2)}) collective-permute-start(bf16[256,2048]{1,0:T(8,128)(2,1)S(1)} %get-tuple-element.430), channel_id=1, source_target_pairs={{0,1},{1,0},{2,3},{3,2},{4,5},{5,4},{6,7},{7,6},{8,9},{9,8},{10,11... | collective-permute-start | bytes 3145736 | tf_op jit(solution)/shard_map/ppermute | solution.py:181
  516.9 32.6 %collective-permute-start.90 = (bf16[256,1024]{0,1:T(8,128)(2,1)}, bf16[256,1024]{0,1:T(8,128)(2,1)}, u32[]{:S(2)}, u32[]{:S(2)}) collective-permute-start(bf16[256,1024]{0,1:T(8,128)(2,1)} %get-tuple-element.451), channel_id=1, source_target_pairs={{0,4},{1,5},{2,6},{3,7},{4,0},{5,1},{6,2},{7,3},{8,12},{9,13},{10,... | collective-permute-start | bytes 1572872 | tf_op jit(solution)/shard_map/ppermute | solution.py:181
  527.0 58.7 %collective-permute-start.65 = (bf16[256,2048]{1,0:T(8,128)(2,1)S(1)}, bf16[256,2048]{1,0:T(8,128)(2,1)S(1)}, u32[]{:S(2)}, u32[]{:S(2)}) collective-permute-start(bf16[256,2048]{1,0:T(8,128)(2,1)S(1)} %get-tuple-element.427), channel_id=1, source_target_pairs={{0,1},{1,0},{2,3},{3,2},{4,5},{5,4},{6,7},{7,6},{8,9},{9,8},{10,11... | collective-permute-start | bytes 3145736 | tf_op jit(solution)/shard_map/ppermute | solution.py:181
  551.0 31.7 %collective-permute-start.97 = (bf16[256,1024]{0,1:T(8,128)(2,1)}, bf16[256,1024]{0,1:T(8,128)(2,1)}, u32[]{:S(2)}, u32[]{:S(2)}) collective-permute-start(bf16[256,1024]{0,1:T(8,128)(2,1)} %get-tuple-element.445), channel_id=1, source_target_pairs={{0,4},{1,5},{2,6},{3,7},{4,0},{5,1},{6,2},{7,3},{8,12},{9,13},{10,... | collective-permute-start | bytes 1572872 | tf_op jit(solution)/shard_map/ppermute | solution.py:181
  551.6 35.7 %collective-permute-start.67 = (bf16[256,2048]{1,0:T(8,128)(2,1)S(1)}, bf16[256,2048]{1,0:T(8,128)(2,1)S(1)}, u32[]{:S(2)}, u32[]{:S(2)}) collective-permute-start(bf16[256,2048]{1,0:T(8,128)(2,1)S(1)} %get-tuple-element.411), channel_id=1, source_target_pairs={{0,8},{1,3},{2,10},{3,1},{4,12},{5,7},{6,14},{7,5},{8,0},{9,11},{1... | collective-permute-start | bytes 3145736 | tf_op jit(solution)/shard_map/ppermute | solution.py:181
  560.8 38.2 %collective-permute-start.62 = (bf16[256,2048]{1,0:T(8,128)(2,1)S(1)}, bf16[256,2048]{1,0:T(8,128)(2,1)S(1)}, u32[]{:S(2)}, u32[]{:S(2)}) collective-permute-start(bf16[256,2048]{1,0:T(8,128)(2,1)S(1)} %get-tuple-element.425), channel_id=1, source_target_pairs={{0,1},{1,0},{2,3},{3,2},{4,5},{5,4},{6,7},{7,6},{8,9},{9,8},{10,11... | collective-permute-start | bytes 3145736 | tf_op jit(solution)/shard_map/ppermute | solution.py:181
  572.0 28.7 %collective-permute-start.51 = (bf16[256,2048]{1,0:T(8,128)(2,1)S(1)}, bf16[256,2048]{1,0:T(8,128)(2,1)S(1)}, u32[]{:S(2)}, u32[]{:S(2)}) collective-permute-start(bf16[256,2048]{1,0:T(8,128)(2,1)S(1)} %get-tuple-element.431), channel_id=1, source_target_pairs={{0,1},{1,0},{2,3},{3,2},{4,5},{5,4},{6,7},{7,6},{8,9},{9,8},{10,11... | collective-permute-start | bytes 3145736 | tf_op jit(solution)/shard_map/ppermute | solution.py:181
  582.7 42.3 %collective-permute-start.53 = (bf16[256,2048]{1,0:T(8,128)(2,1)}, bf16[256,2048]{1,0:T(8,128)(2,1)S(1)}, u32[]{:S(2)}, u32[]{:S(2)}) collective-permute-start(bf16[256,2048]{1,0:T(8,128)(2,1)} %get-tuple-element.416), channel_id=1, source_target_pairs={{0,8},{1,3},{2,10},{3,1},{4,12},{5,7},{6,14},{7,5},{8,0},{9,11},{1... | collective-permute-start | bytes 3145736 | tf_op jit(solution)/shard_map/ppermute | solution.py:181
  587.2 37.7 %collective-permute-start.94 = (bf16[256,1024]{0,1:T(8,128)(2,1)S(1)}, bf16[256,1024]{0,1:T(8,128)(2,1)S(1)}, u32[]{:S(2)}, u32[]{:S(2)}) collective-permute-start(bf16[256,1024]{0,1:T(8,128)(2,1)S(1)} %add_convert_fusion.9), channel_id=1, source_target_pairs={{0,16},{1,17},{2,18},{3,19},{4,20},{5,21},{6,22},{7,23},{8,24},{9,... | collective-permute-start | bytes 1572872 | tf_op jit(solution)/shard_map/ppermute | solution.py:181
  598.9 42.6 %collective-permute-start.48 = (bf16[256,2048]{1,0:T(8,128)(2,1)}, bf16[256,2048]{1,0:T(8,128)(2,1)S(1)}, u32[]{:S(2)}, u32[]{:S(2)}) collective-permute-start(bf16[256,2048]{1,0:T(8,128)(2,1)} %get-tuple-element.429), channel_id=1, source_target_pairs={{0,1},{1,0},{2,3},{3,2},{4,5},{5,4},{6,7},{7,6},{8,9},{9,8},{10,11... | collective-permute-start | bytes 3145736 | tf_op jit(solution)/shard_map/ppermute | solution.py:181
  598.9 35.8 %collective-permute-start.101 = (bf16[256,1024]{0,1:T(8,128)(2,1)S(1)}, bf16[256,1024]{0,1:T(8,128)(2,1)S(1)}, u32[]{:S(2)}, u32[]{:S(2)}) collective-permute-start(bf16[256,1024]{0,1:T(8,128)(2,1)S(1)} %add_convert_fusion.6), channel_id=1, source_target_pairs={{0,16},{1,17},{2,18},{3,19},{4,20},{5,21},{6,22},{7,23},{8,24},{9,... | collective-permute-start | bytes 1572872 | tf_op jit(solution)/shard_map/ppermute | solution.py:181
  600.7 41.4 %collective-permute-start.64 = (bf16[256,2048]{1,0:T(8,128)(2,1)}, bf16[256,2048]{1,0:T(8,128)(2,1)S(1)}, u32[]{:S(2)}, u32[]{:S(2)}) collective-permute-start(bf16[256,2048]{1,0:T(8,128)(2,1)} %get-tuple-element.410), channel_id=1, source_target_pairs={{0,8},{1,3},{2,10},{3,1},{4,12},{5,7},{6,14},{7,5},{8,0},{9,11},{1... | collective-permute-start | bytes 3145736 | tf_op jit(solution)/shard_map/ppermute | solution.py:181
  625.0 37.8 %collective-permute-start.50 = (bf16[256,2048]{1,0:T(8,128)(2,1)S(1)}, bf16[256,2048]{1,0:T(8,128)(2,1)S(1)}, u32[]{:S(2)}, u32[]{:S(2)}) collective-permute-start(bf16[256,2048]{1,0:T(8,128)(2,1)S(1)} %copy-done.55), channel_id=1, source_target_pairs={{0,8},{1,3},{2,10},{3,1},{4,12},{5,7},{6,14},{7,5},{8,0},{9,11},{1... | collective-permute-start | bytes 3145736 | tf_op jit(solution)/shard_map/ppermute | solution.py:181
  625.0 39.3 %collective-permute-start.68 = (bf16[256,2048]{1,0:T(8,128)(2,1)S(1)}, bf16[256,2048]{1,0:T(8,128)(2,1)S(1)}, u32[]{:S(2)}, u32[]{:S(2)}) collective-permute-start(bf16[256,2048]{1,0:T(8,128)(2,1)S(1)} %fusion.62), channel_id=1, source_target_pairs={{0,2},{1,9},{2,0},{3,11},{4,6},{5,13},{6,4},{7,15},{8,10},{9,1},{1... | collective-permute-start | bytes 3145736 | tf_op jit(solution)/shard_map/ppermute | solution.py:181
  634.7 30.2 %collective-permute-start.54 = (bf16[256,2048]{1,0:T(8,128)(2,1)S(1)}, bf16[256,2048]{1,0:T(8,128)(2,1)S(1)}, u32[]{:S(2)}, u32[]{:S(2)}) collective-permute-start(bf16[256,2048]{1,0:T(8,128)(2,1)S(1)} %fusion.68), channel_id=1, source_target_pairs={{0,2},{1,9},{2,0},{3,11},{4,6},{5,13},{6,4},{7,15},{8,10},{9,1},{1... | collective-permute-start | bytes 3145736 | tf_op jit(solution)/shard_map/ppermute | solution.py:181
  641.5 36.6 %collective-permute-start.106 = (bf16[256,1024]{0,1:T(8,128)(2,1)}, bf16[256,1024]{0,1:T(8,128)(2,1)}, u32[]{:S(2)}, u32[]{:S(2)}) collective-permute-start(bf16[256,1024]{0,1:T(8,128)(2,1)} %get-tuple-element.437), channel_id=1, source_target_pairs={{0,4},{1,5},{2,6},{3,7},{4,0},{5,1},{6,2},{7,3},{8,12},{9,13},{10,... | collective-permute-start | bytes 1572872 | tf_op jit(solution)/shard_map/ppermute | solution.py:181
  642.0 37.6 %collective-permute-start.104 = (bf16[256,1024]{0,1:T(8,128)(2,1)}, bf16[256,1024]{0,1:T(8,128)(2,1)}, u32[]{:S(2)}, u32[]{:S(2)}) collective-permute-start(bf16[256,1024]{0,1:T(8,128)(2,1)} %get-tuple-element.439), channel_id=1, source_target_pairs={{0,4},{1,5},{2,6},{3,7},{4,0},{5,1},{6,2},{7,3},{8,12},{9,13},{10,... | collective-permute-start | bytes 1572872 | tf_op jit(solution)/shard_map/ppermute | solution.py:181
  664.3 30.5 %collective-permute-start.95 = (bf16[256,1024]{0,1:T(8,128)(2,1)}, bf16[256,1024]{0,1:T(8,128)(2,1)}, u32[]{:S(2)}, u32[]{:S(2)}) collective-permute-start(bf16[256,1024]{0,1:T(8,128)(2,1)} %get-tuple-element.447), channel_id=1, source_target_pairs={{0,8},{1,9},{2,10},{3,11},{4,12},{5,13},{6,14},{7,15},{8,0},{9,1},... | collective-permute-start | bytes 1572872 | tf_op jit(solution)/shard_map/ppermute | solution.py:181
  665.9 31.6 %collective-permute-start.102 = (bf16[256,1024]{0,1:T(8,128)(2,1)}, bf16[256,1024]{0,1:T(8,128)(2,1)}, u32[]{:S(2)}, u32[]{:S(2)}) collective-permute-start(bf16[256,1024]{0,1:T(8,128)(2,1)} %get-tuple-element.441), channel_id=1, source_target_pairs={{0,8},{1,9},{2,10},{3,11},{4,12},{5,13},{6,14},{7,15},{8,0},{9,1},... | collective-permute-start | bytes 1572872 | tf_op jit(solution)/shard_map/ppermute | solution.py:181
  678.1 53.1 %collective-permute-start.69 = (bf16[256,2048]{1,0:T(8,128)(2,1)S(1)}, bf16[256,2048]{1,0:T(8,128)(2,1)S(1)}, u32[]{:S(2)}, u32[]{:S(2)}) collective-permute-start(bf16[256,2048]{1,0:T(8,128)(2,1)S(1)} %get-tuple-element.387), channel_id=1, source_target_pairs={{0,2},{1,3},{2,0},{3,1},{4,6},{5,7},{6,4},{7,5},{8,10},{9,11},{10,... | collective-permute-start | bytes 3145736 | tf_op jit(solution)/shard_map/ppermute | solution.py:181
  686.0 32.7 %collective-permute-start.109 = (bf16[256,1024]{0,1:T(8,128)(2,1)S(1)}, bf16[256,1024]{0,1:T(8,128)(2,1)S(1)}, u32[]{:S(2)}, u32[]{:S(2)}) collective-permute-start(bf16[256,1024]{0,1:T(8,128)(2,1)S(1)} %get-tuple-element.435), channel_id=1, source_target_pairs={{0,8},{1,9},{2,10},{3,11},{4,12},{5,13},{6,14},{7,15},{8,0},{9,1},... | collective-permute-start | bytes 1572872 | tf_op jit(solution)/shard_map/ppermute | solution.py:181
  686.0 37.4 %collective-permute-start.89 = (bf16[256,1024]{0,1:T(8,128)(2,1)}, bf16[256,1024]{0,1:T(8,128)(2,1)}, u32[]{:S(2)}, u32[]{:S(2)}) collective-permute-start(bf16[256,1024]{0,1:T(8,128)(2,1)} %get-tuple-element.452), channel_id=1, source_target_pairs={{0,4},{1,5},{2,6},{3,7},{4,0},{5,1},{6,2},{7,3},{8,12},{9,13},{10,... | collective-permute-start | bytes 1572872 | tf_op jit(solution)/shard_map/ppermute | solution.py:181
  694.8 30.4 %collective-permute-start.91 = (bf16[256,1024]{0,1:T(8,128)(2,1)}, bf16[256,1024]{0,1:T(8,128)(2,1)}, u32[]{:S(2)}, u32[]{:S(2)}) collective-permute-start(bf16[256,1024]{0,1:T(8,128)(2,1)} %get-tuple-element.448), channel_id=1, source_target_pairs={{0,16},{1,17},{2,18},{3,19},{4,20},{5,21},{6,22},{7,23},{8,24},{9,... | collective-permute-start | bytes 1572872 | tf_op jit(solution)/shard_map/ppermute | solution.py:181
  697.5 36.2 %collective-permute-start.96 = (bf16[256,1024]{0,1:T(8,128)(2,1)}, bf16[256,1024]{0,1:T(8,128)(2,1)}, u32[]{:S(2)}, u32[]{:S(2)}) collective-permute-start(bf16[256,1024]{0,1:T(8,128)(2,1)} %get-tuple-element.446), channel_id=1, source_target_pairs={{0,4},{1,5},{2,6},{3,7},{4,0},{5,1},{6,2},{7,3},{8,12},{9,13},{10,... | collective-permute-start | bytes 1572872 | tf_op jit(solution)/shard_map/ppermute | solution.py:181
  718.7 37.4 %collective-permute-start.98 = (bf16[256,1024]{0,1:T(8,128)(2,1)}, bf16[256,1024]{0,1:T(8,128)(2,1)}, u32[]{:S(2)}, u32[]{:S(2)}) collective-permute-start(bf16[256,1024]{0,1:T(8,128)(2,1)} %get-tuple-element.442), channel_id=1, source_target_pairs={{0,16},{1,17},{2,18},{3,19},{4,20},{5,21},{6,22},{7,23},{8,24},{9,... | collective-permute-start | bytes 1572872 | tf_op jit(solution)/shard_map/ppermute | solution.py:181
  723.4 155.3 %collective-permute-start.103 = (bf16[256,1024]{0,1:T(8,128)(2,1)}, bf16[256,1024]{0,1:T(8,128)(2,1)}, u32[]{:S(2)}, u32[]{:S(2)}) collective-permute-start(bf16[256,1024]{0,1:T(8,128)(2,1)} %get-tuple-element.440), channel_id=1, source_target_pairs={{0,4},{1,5},{2,6},{3,7},{4,0},{5,1},{6,2},{7,3},{8,12},{9,13},{10,... | collective-permute-start | bytes 1572872 | tf_op jit(solution)/shard_map/ppermute | solution.py:181
  725.2 34.9 %collective-permute-start.70 = (bf16[256,2048]{1,0:T(8,128)(2,1)S(1)}, bf16[256,2048]{1,0:T(8,128)(2,1)S(1)}, u32[]{:S(2)}, u32[]{:S(2)}) collective-permute-start(bf16[256,2048]{1,0:T(8,128)(2,1)S(1)} %get-tuple-element.387), channel_id=1, source_target_pairs={{0,1},{1,0},{2,3},{3,2},{4,5},{5,4},{6,7},{7,6},{8,9},{9,8},{10,11... | collective-permute-start | bytes 3145736 | tf_op jit(solution)/shard_map/ppermute | solution.py:181
  731.2 29.0 %collective-permute-start.71 = (bf16[256,2048]{1,0:T(8,128)(2,1)S(1)}, bf16[256,2048]{1,0:T(8,128)(2,1)S(1)}, u32[]{:S(2)}, u32[]{:S(2)}) collective-permute-start(bf16[256,2048]{1,0:T(8,128)(2,1)S(1)} %collective-permute-done.69), channel_id=1, source_target_pairs={{0,1},{1,0},{2,3},{3,2},{4,5},{5,4},{6,7},{7,6},{8,9},{9,8},{10,11... | collective-permute-start | bytes 3145736 | tf_op jit(solution)/shard_map/ppermute | solution.py:181
  733.7 147.0 %collective-permute-start.105 = (bf16[256,1024]{0,1:T(8,128)(2,1)}, bf16[256,1024]{0,1:T(8,128)(2,1)}, u32[]{:S(2)}, u32[]{:S(2)}) collective-permute-start(bf16[256,1024]{0,1:T(8,128)(2,1)} %get-tuple-element.436), channel_id=1, source_target_pairs={{0,16},{1,17},{2,18},{3,19},{4,20},{5,21},{6,22},{7,23},{8,24},{9,... | collective-permute-start | bytes 1572872 | tf_op jit(solution)/shard_map/ppermute | solution.py:181
  837.2 76.4 %collective-permute-start.73 = (bf16[256,2048]{1,0:T(8,128)(2,1)S(1)}, bf16[256,2048]{1,0:T(8,128)(2,1)S(1)}, u32[]{:S(2)}, u32[]{:S(2)}) collective-permute-start(bf16[256,2048]{1,0:T(8,128)(2,1)S(1)} %get-tuple-element.424), channel_id=1, source_target_pairs={{0,1},{1,0},{2,3},{3,2},{4,5},{5,4},{6,7},{7,6},{8,9},{9,8},{10,11... | collective-permute-start | bytes 3145736 | tf_op jit(solution)/shard_map/ppermute | solution.py:181
  894.7 48.4 %collective-permute-start.75 = (bf16[256,1024]{1,0:T(8,128)(2,1)S(1)}, bf16[256,1024]{1,0:T(8,128)(2,1)S(1)}, u32[]{:S(2)}, u32[]{:S(2)}) collective-permute-start(bf16[256,1024]{1,0:T(8,128)(2,1)S(1)} %get-tuple-element.417), channel_id=1, source_target_pairs={{0,4},{1,5},{2,6},{3,7},{4,0},{5,1},{6,2},{7,3},{8,12},{9,13},{10,... | collective-permute-start | bytes 1572872 | tf_op jit(solution)/shard_map/ppermute | solution.py:181
  898.6 44.4 %collective-permute-start.77 = (bf16[256,1024]{1,0:T(8,128)(2,1)S(1)}, bf16[256,1024]{1,0:T(8,128)(2,1)S(1)}, u32[]{:S(2)}, u32[]{:S(2)}) collective-permute-start(bf16[256,1024]{1,0:T(8,128)(2,1)S(1)} %get-tuple-element.421), channel_id=1, source_target_pairs={{0,8},{1,9},{2,10},{3,11},{4,12},{5,13},{6,14},{7,15},{8,0},{9,1},... | collective-permute-start | bytes 1572872 | tf_op jit(solution)/shard_map/ppermute | solution.py:181
  913.6 35.2 %collective-permute-start.81 = (bf16[256,1024]{1,0:T(8,128)(2,1)S(1)}, bf16[256,1024]{1,0:T(8,128)(2,1)S(1)}, u32[]{:S(2)}, u32[]{:S(2)}) collective-permute-start(bf16[256,1024]{1,0:T(8,128)(2,1)S(1)} %add_convert_fusion.11), channel_id=1, source_target_pairs={{0,16},{1,17},{2,18},{3,19},{4,20},{5,21},{6,22},{7,23},{8,24},{9,... | collective-permute-start | bytes 1572872 | tf_op jit(solution)/shard_map/ppermute | solution.py:181
  917.8 38.7 %collective-permute-start.72 = (bf16[256,2048]{1,0:T(8,128)(2,1)}, bf16[256,2048]{1,0:T(8,128)(2,1)}, u32[]{:S(2)}, u32[]{:S(2)}) collective-permute-start(bf16[256,2048]{1,0:T(8,128)(2,1)} %get-tuple-element.423), channel_id=1, source_target_pairs={{0,1},{1,0},{2,3},{3,2},{4,5},{5,4},{6,7},{7,6},{8,9},{9,8},{10,11... | collective-permute-start | bytes 3145736 | tf_op jit(solution)/shard_map/ppermute | solution.py:181
  972.4 30.1 %collective-permute-start.112 = (f32[4224]{0:T(1024)S(1)}, f32[4224]{0:T(1024)S(1)}, u32[]{:S(2)}, u32[]{:S(2)}) collective-permute-start(f32[4224]{0:T(1024)S(1)} %add.654), channel_id=1, source_target_pairs={{0,16},{1,17},{2,18},{3,19},{4,20},{5,21},{6,22},{7,23},{8,24},{9,... | collective-permute-start | bytes 50696 | tf_op jit(solution)/shard_map/ppermute | solution.py:181
  (162 other events, 3218.6 us)

commit v2 on v0

v2 whole, which is shorter than its diff:
```python
import functools

import jax
import jax.numpy as jnp
from jax import lax
from jax.experimental import pallas as pl
from jax.experimental.pallas import tpu as pltpu
from jax.sharding import PartitionSpec as P

HD = 256
STEP = 10


EPS_NORM = 1e-05
THETA = 1000042.0
LEARN_RATE = 0.02
BETA_ONE = 0.9
BETA_TWO = 0.95
ADAM_EPS = 1e-08
WEIGHT_DECAY = 0.1
MAX_NORM = 1.0
MASKED = -1000000000.0


def rotary_tables(count, head_dim):
    positions = jnp.arange(count).astype(jnp.float32)
    inverse = THETA ** (-2.0 * jnp.arange(head_dim // 2).astype(jnp.float32) / head_dim)
    angles = positions[:, None] * inverse[None, :]
    return (jnp.cos(angles), jnp.sin(angles))


def dot_rows(left, right):
    return lax.dot_general(
        left, right, (((0,), (0,)), ((), ())), preferred_element_type=jnp.float32
    )


def dot_last(left, right):
    return lax.dot_general(
        left, right, (((1,), (1,)), ((), ())), preferred_element_type=jnp.float32
    )


def adam_step(master, gradient, moment, square, factor):
    clipped = gradient * factor
    new_moment = BETA_ONE * moment + (1.0 - BETA_ONE) * clipped
    new_square = BETA_TWO * square + (1.0 - BETA_TWO) * clipped * clipped
    moment_hat = new_moment / (1.0 - BETA_ONE**STEP)
    square_hat = new_square / (1.0 - BETA_TWO**STEP)
    update = -LEARN_RATE * (moment_hat / (jnp.sqrt(square_hat) + ADAM_EPS) + WEIGHT_DECAY * master)
    return (new_moment, new_square, update)


F32, BF16 = jnp.float32, jnp.bfloat16
TILE = 256
VMEM_BYTES = 48 * 1024 * 1024
SMALL_COST = pl.CostEstimate(flops=1, bytes_accessed=1, transcendentals=0)


class Pinned:
    def __init__(self, value, before):
        self.value, self.before = value, before
        self.shape, self.dtype = value.shape, value.dtype


def pin(value, *before):
    if isinstance(value, Pinned):
        return Pinned(value.value, (*value.before, *before))
    return Pinned(value, before)


def unpin(operands):
    arrays, before = [], []
    for one in operands:
        if isinstance(one, Pinned):
            before += [other for other in one.before if all(other is not had for had in before)]
            one = one.value
        arrays.append(one)
    return arrays, before


def call_kernel(kernel, grid_spec, out_shape, operands, scalars=0, aliases=()):
    arrays, before = unpin(operands)
    count, spare = len(arrays), len(before)

    def body(*refs):
        kernel(*refs[:count], *refs[count + spare :])

    spec = pltpu.PrefetchScalarGridSpec(
        num_scalar_prefetch=scalars,
        grid=grid_spec["grid"],
        in_specs=list(grid_spec["in_specs"]) + [pl.BlockSpec(memory_space=pl.ANY)] * spare,
        out_specs=grid_spec["out_specs"],
        scratch_shapes=grid_spec.get("scratch", ()),
    )
    return pl.pallas_call(
        body,
        grid_spec=spec,
        out_shape=out_shape,
        input_output_aliases=dict(aliases),
        compiler_params=pltpu.CompilerParams(
            dimension_semantics=("arbitrary",) * len(grid_spec["grid"]),
            vmem_limit_bytes=VMEM_BYTES,
        ),
        cost_estimate=SMALL_COST,
    )(*arrays, *before)


def run_kernel(kernel, grid, in_specs, out_specs, out_shape, scratch=()):
    def call(*operands):
        spec = {"grid": grid, "in_specs": in_specs, "out_specs": out_specs, "scratch": scratch}
        return call_kernel(kernel, spec, out_shape, operands)

    return call


def hold_kernel(value_ref, out_ref):
    del value_ref, out_ref


def settle(value):
    if not isinstance(value, Pinned):
        return value
    anywhere = pl.BlockSpec(memory_space=pl.ANY)
    return call_kernel(
        hold_kernel,
        {"grid": (1,), "in_specs": [anywhere], "out_specs": anywhere},
        jax.ShapeDtypeStruct(value.shape, value.dtype),
        [value],
        aliases=((0, 0),),
    )


def weight_shape(weight):
    return (weight[0].shape[0] * 2, weight[0].shape[1])


def with_weights(weights, places, body, first_step, *refs):
    side_ref, refs = refs[0], list(refs[1:])
    scratch = refs[len(refs) - 2 * len(weights) :]
    refs = refs[: len(refs) - 2 * len(weights)]
    count = sum(len(weight) for weight in weights)
    held = refs[places : places + count]
    rest = refs[:places] + refs[places + count :]
    ways = lax.axis_size("fsdp")

    @pl.when(first_step())
    def _():
        copies = []
        for number, weight in enumerate(weights):
            rows = weight_shape(weight)[0] // ways
            block = 0
            for part in weight:
                ref = held.pop(0)
                for place in range(part.shape[0] // rows):
                    other, index = divmod(block, ways // 2)
                    row = pl.multiple_of((2 * index + (side_ref[0] ^ other)) * rows, rows)
                    copies.append(
                        pltpu.make_async_copy(
                            ref.at[pl.ds(place * rows, rows), :],
                            scratch[2 * number].at[pl.ds(row, rows), :],
                            scratch[2 * number + 1].at[block],
                        )
                    )
                    block += 1
        for copy in copies:
            copy.start()
        for copy in copies:
            copy.wait()

    body(*rest[:places], *scratch[0::2], *rest[places:])


def run_weights(body, grid, before, weights, after, out_specs, out_shape, scratch=()):
    side = my_bit("fsdp", 1).astype(jnp.int32).reshape((1,))
    spare = []
    for weight in weights:
        spare += [
            pltpu.VMEM(weight_shape(weight), BF16),
            pltpu.SemaphoreType.DMA((lax.axis_size("fsdp"),)),
        ]

    def first_step():
        first = pl.program_id(0) == 0
        for axis in range(1, len(grid)):
            first = first & (pl.program_id(axis) == 0)
        return first

    return run_kernel(
        functools.partial(with_weights, weights, len(before), body, first_step),
        grid,
        [pl.BlockSpec(memory_space=pltpu.SMEM)]
        + [spec for spec, _ in before]
        + [pl.BlockSpec(memory_space=pl.ANY)] * sum(len(weight) for weight in weights)
        + [spec for spec, _ in after],
        out_specs,
        out_shape,
        list(scratch) + spare,
    )(
        side,
        *[one for _, one in before],
        *[part for weight in weights for part in weight],
        *[one for _, one in after],
    )


def fixed(shape):
    return pl.BlockSpec(shape, lambda *_: (0,) * len(shape))


def by_rows(cols):
    return pl.BlockSpec((TILE, cols), lambda step: (step, 0))


def dot_plain(left, right):
    return jnp.dot(left, right, preferred_element_type=F32)


def qkv_kernel(rotated, x_ref, w_ref, cos_ref, sin_ref, out_ref):
    half = HD // 2
    cosine, sine = cos_ref[...], sin_ref[...]
    for head in range(w_ref.shape[1] // HD):
        here = slice(head * HD, (head + 1) * HD)
        lin = dot_plain(x_ref[...], w_ref[:, here])
        if head < rotated:
            first, second = lin[:, :half], lin[:, half:]
            out_ref[:, head * HD : head * HD + half] = (first * cosine - second * sine).astype(BF16)
            out_ref[:, head * HD + half : (head + 1) * HD] = (
                second * cosine + first * sine
            ).astype(BF16)
        else:
            out_ref[:, here] = lin.astype(BF16)


def project_qkv(attn_input, full_qkv, cosine_table, sine_table, rotated):
    rows, depth = attn_input.shape
    cols = weight_shape(full_qkv)[1]
    return run_weights(
        functools.partial(qkv_kernel, rotated),
        (rows // TILE,),
        [(by_rows(depth), attn_input)],
        [full_qkv],
        [(by_rows(HD // 2), cosine_table), (by_rows(HD // 2), sine_table)],
        by_rows(cols),
        jax.ShapeDtypeStruct((rows, cols), BF16),
    )


def soft_rows(query, keys, first_row, length):
    scores = dot_last(query, keys) * (HD**-0.5)
    rows = first_row + lax.broadcasted_iota(jnp.int32, scores.shape, 0)
    cols = lax.broadcasted_iota(jnp.int32, scores.shape, 1)
    scores = jnp.where((cols <= rows) & (cols < length), scores, MASKED)
    exponent = jnp.exp(scores - jnp.max(scores, axis=-1, keepdims=True))
    return exponent / jnp.sum(exponent, axis=-1, keepdims=True)


def attend_kernel(blocks, length_ref, q_ref, k_ref, v_ref, out_ref):
    for block in range(blocks):

        @pl.when(pl.program_id(1) == block)
        def _():
            width = (block + 1) * TILE
            probs = soft_rows(q_ref[...], k_ref[:width, :], block * TILE, length_ref[0])
            out_ref[...] = dot_plain(probs.astype(BF16), v_ref[:width, :]).astype(BF16)


def attend(qkv_rot, lengths, heads, heads_kv):
    rows = qkv_rot.shape[0]
    group = heads // heads_kv
    blocks = rows // TILE
    return run_kernel(
        functools.partial(attend_kernel, blocks),
        (heads, blocks),
        [
            pl.BlockSpec(memory_space=pltpu.SMEM),
            pl.BlockSpec((TILE, HD), lambda head, step: (step, head)),
            pl.BlockSpec((rows, HD), lambda head, step: (0, heads + head // group)),
            pl.BlockSpec((rows, HD), lambda head, step: (0, heads + heads_kv + head // group)),
        ],
        pl.BlockSpec((TILE, HD), lambda head, step: (step, head)),
        jax.ShapeDtypeStruct((rows, heads * HD), BF16),
    )(lengths, qkv_rot, qkv_rot, qkv_rot)


def attend_back_kernel(
    blocks, group, x_ref, w_ref, length_ref, q_ref, k_ref, v_ref, cos_ref, sin_ref,
    cos_all, sin_all, dq_ref, dk_ref, dv_ref, dk_sum, dv_sum,
):
    half = HD // 2
    step, member = pl.program_id(1), pl.program_id(2)

    @pl.when((step == 0) & (member == 0))
    def _():
        dk_sum[...] = jnp.zeros_like(dk_sum)
        dv_sum[...] = jnp.zeros_like(dv_sum)

    def unrotate(value, cosine, sine):
        first, second = value[:, :half], value[:, half:]
        return jnp.concatenate(
            [first * cosine + second * sine, second * cosine - first * sine], axis=1
        ).astype(BF16)

    for block in range(blocks):

        @pl.when(step == block)
        def _():
            width = (block + 1) * TILE
            query, keys, values = q_ref[...], k_ref[:width, :], v_ref[:width, :]
            here = pl.multiple_of((pl.program_id(0) * group + member) * HD, HD)
            grad = dot_plain(x_ref[...], w_ref[:, pl.ds(here, HD)]).astype(BF16)
            probs = soft_rows(query, keys, block * TILE, length_ref[0])
            prob_grad = dot_last(grad, values)
            delta = jnp.sum(probs * prob_grad, axis=-1, keepdims=True)
            score_grad = (probs * (prob_grad - delta) * (HD**-0.5)).astype(BF16)
            dq_ref[...] = unrotate(dot_plain(score_grad, keys), cos_ref[...], sin_ref[...])
            dk_sum[:width, :] += dot_rows(score_grad, query)
            dv_sum[:width, :] += dot_rows(probs.astype(BF16), grad)

    @pl.when((step == blocks - 1) & (member == group - 1))
    def _():
        dk_ref[...] = unrotate(dk_sum[...], cos_all[...], sin_all[...])
        dv_ref[...] = dv_sum[...].astype(BF16)


def attend_back(attn_grad_in, full_out, qkv_rot, lengths, cosine_table, sine_table, heads, heads_kv):
    rows, depth = attn_grad_in.shape
    group = heads // heads_kv
    blocks = rows // TILE
    half = HD // 2
    return run_weights(
        functools.partial(attend_back_kernel, blocks, group),
        (heads_kv, blocks, group),
        [(pl.BlockSpec((TILE, depth), lambda kv, step, one: (step, 0)), attn_grad_in)],
        [full_out],
        [
            (pl.BlockSpec(memory_space=pltpu.SMEM), lengths),
            (pl.BlockSpec((TILE, HD), lambda kv, step, one: (step, kv * group + one)), qkv_rot),
            (pl.BlockSpec((rows, HD), lambda kv, step, one: (0, heads + kv)), qkv_rot),
            (pl.BlockSpec((rows, HD), lambda kv, step, one: (0, heads + heads_kv + kv)), qkv_rot),
            (pl.BlockSpec((TILE, half), lambda kv, step, one: (step, 0)), cosine_table),
            (pl.BlockSpec((TILE, half), lambda kv, step, one: (step, 0)), sine_table),
            (fixed((rows, half)), cosine_table),
            (fixed((rows, half)), sine_table),
        ],
        [
            pl.BlockSpec((TILE, HD), lambda kv, step, one: (step, kv * group + one)),
            pl.BlockSpec((rows, HD), lambda kv, step, one: (0, kv)),
            pl.BlockSpec((rows, HD), lambda kv, step, one: (0, kv)),
        ],
        [
            jax.ShapeDtypeStruct((rows, heads * HD), BF16),
            jax.ShapeDtypeStruct((rows, heads_kv * HD), BF16),
            jax.ShapeDtypeStruct((rows, heads_kv * HD), BF16),
        ],
        [pltpu.VMEM((rows, HD), F32), pltpu.VMEM((rows, HD), F32)],
    )


def mlp_kernel(x_ref, gate_ref, up_ref, hidden_ref, up_part_ref, gate_part_ref):
    for start in range(0, gate_ref.shape[1], TILE):
        here = slice(start, start + TILE)
        gate = dot_plain(x_ref[...], gate_ref[:, here])
        up = dot_plain(x_ref[...], up_ref[:, here])
        sig = jax.nn.sigmoid(gate)
        act = gate * sig
        hidden_ref[:, here] = (act * up).astype(BF16)
        gate_part_ref[:, here] = (up * sig * (1.0 + gate * (1.0 - sig))).astype(BF16)
        up_part_ref[:, here] = act.astype(BF16)


def mlp_forward(block, full_gate, full_up):
    rows, depth = block.shape
    cols = weight_shape(full_gate)[1]
    return run_weights(
        mlp_kernel,
        (rows // TILE,),
        [(by_rows(depth), block)],
        [full_gate, full_up],
        [],
        [by_rows(cols)] * 3,
        [jax.ShapeDtypeStruct((rows, cols), BF16)] * 3,
    )


def mlp_grad_kernel(x_ref, down_ref, up_part_ref, gate_part_ref, gate_ref, up_ref):
    for start in range(0, down_ref.shape[1], TILE):
        here = slice(start, start + TILE)
        hidden_grad = dot_plain(x_ref[...], down_ref[:, here])
        gate_ref[:, here] = (hidden_grad * gate_part_ref[:, here].astype(F32)).astype(BF16)
        up_ref[:, here] = (hidden_grad * up_part_ref[:, here].astype(F32)).astype(BF16)


def mlp_backward(block, full_down, up_part, gate_part):
    rows, depth = block.shape
    cols = weight_shape(full_down)[1]
    return run_weights(
        mlp_grad_kernel,
        (rows // TILE,),
        [(by_rows(depth), block)],
        [full_down],
        [(by_rows(cols), up_part), (by_rows(cols), gate_part)],
        [by_rows(cols)] * 2,
        [jax.ShapeDtypeStruct((rows, cols), BF16)] * 2,
    )


def back_kernel(count, tiles, *refs):
    lefts, rights, outs = refs[:count], refs[count : 2 * count], refs[2 * count :]

    def write(out_ref):
        for start in range(0, out_ref.shape[1], TILE):
            here = slice(start, start + TILE)
            total = dot_last(lefts[0][...], rights[0][here, :])
            for number in range(1, count):
                total += dot_last(lefts[number][...], rights[number][here, :])
            out_ref[:, here] = total.astype(BF16)

    for number in range(len(outs)):
        first, last = number * tiles, (number + 1) * tiles

        @pl.when((pl.program_id(0) >= first) & (pl.program_id(0) < last))
        def _(number=number):
            write(outs[number])


def back_product(*operands, parts=1):
    count = len(operands) // 2
    lefts, rights = operands[:count], operands[count:]
    rows = lefts[0].shape[0]
    cols = weight_shape(rights[0])[0]
    tiles = rows // TILE // parts
    return run_weights(
        functools.partial(back_kernel, count, tiles),
        (rows // TILE,),
        [(by_rows(left.shape[1]), left) for left in lefts],
        list(rights),
        [],
        [
            pl.BlockSpec(
                (TILE, cols), lambda step, part=part: (jnp.clip(step - part * tiles, 0, tiles - 1), 0)
            )
            for part in range(parts)
        ],
        [jax.ShapeDtypeStruct((rows // parts, cols), BF16)] * parts,
    )


def arrange_kernel(parts, place_ref, *refs):
    for number in range(parts):

        @pl.when(pl.program_id(0) == number)
        def _():
            refs[parts][...] = refs[number][...]


def arrange(parts, places):
    rows, width = parts[0].shape
    count = len(parts)
    place = {
        "grid": (count,),
        "in_specs": [pl.BlockSpec((rows, width), lambda step, place: (0, 0))] * count,
        "out_specs": pl.BlockSpec((rows, width), lambda step, place: (place[step], 0)),
    }
    return call_kernel(
        functools.partial(arrange_kernel, count),
        place,
        jax.ShapeDtypeStruct((rows * count, width), parts[0].dtype),
        [jnp.stack([jnp.asarray(one, jnp.int32) for one in places]), *parts],
        scalars=1,
    )


def rowwise_kernel(fn, operands, outs, *refs):
    results = fn(*[ref[...] for ref in refs[:operands]])
    targets = refs[operands:]
    for number in range(outs):
        targets[number][...] = results[number].astype(targets[number].dtype)
    for number in range(outs, len(targets)):
        partial = jnp.broadcast_to(
            jnp.sum(results[number], axis=0, keepdims=True), targets[number].shape
        )

        @pl.when(pl.program_id(0) == 0)
        def _(number=number, partial=partial):
            targets[number][...] = partial

        @pl.when(pl.program_id(0) > 0)
        def _(number=number, partial=partial):
            targets[number][...] += partial


def rowwise(fn, rows, operands, outs, sums=0):
    tile = rows // 4
    specs = []
    for array, first in operands:
        cols = array.shape[1]
        if first is None:
            specs.append(fixed(array.shape))
        else:
            specs.append(pl.BlockSpec((tile, cols), lambda step, at=first // tile: (step + at, 0)))
    cols = operands[0][0].shape[1]
    return run_kernel(
        functools.partial(rowwise_kernel, fn, len(operands), len(outs)),
        (4,),
        specs,
        [pl.BlockSpec((tile, cols), lambda step: (step, 0))] * len(outs) + [fixed((8, cols))] * sums,
        [jax.ShapeDtypeStruct((rows, cols), one) for one in outs]
        + [jax.ShapeDtypeStruct((8, cols), F32)] * sums,
    )(*[array for array, _ in operands])


def sum_tiles(*tiles):
    total = tiles[0].astype(F32)
    for tile in tiles[1:]:
        total = total + tile.astype(F32)
    return total


def add_low(rows, *operands):
    return rowwise(lambda *tiles: (sum_tiles(*tiles),), rows, operands, [BF16])[0]


def row_scale_of(values):
    return lax.rsqrt(jnp.mean(values * values, axis=-1, keepdims=True) + EPS_NORM)


def enter_norm(tokens, gain):
    def body(values, gain):
        values = values.astype(F32)
        return (values * row_scale_of(values) * gain,)

    return rowwise(body, tokens.shape[0], [(tokens, 0), (gain, None)], [BF16])[0]


def middle_norm(rows, operands, gain):
    def body(*tiles):
        values = sum_tiles(*tiles[:-1])
        return values, values * row_scale_of(values) * tiles[-1]

    return rowwise(body, rows, [*operands, (gain, None)], [F32, BF16])


def leave_norm(rows, operands, values, passed, gain, outs):
    def body(*tiles):
        incoming = sum_tiles(*tiles[:-3])
        values, passed, gain = tiles[-3].astype(F32), tiles[-2].astype(F32), tiles[-1]
        scale = row_scale_of(values)
        weighted = incoming * gain
        mean = jnp.mean(weighted * values, axis=-1, keepdims=True)
        result = passed + scale * weighted - values * scale**3 * mean
        return *[result for _ in outs], incoming * values * scale

    return rowwise(body, rows, [*operands, (values, 0), (passed, 0), (gain, None)], outs, 1)


def spread_kernel(count, groups, *refs):
    weights, out_ref = refs[:count], refs[-1]
    if groups == 1:
        start = 0
        for weight in weights:
            width = weight.shape[1]
            out_ref[:, start : start + width] = weight[...].astype(BF16)
            start += width
    else:
        width = out_ref.shape[1]
        for group in range(groups):

            @pl.when(lax.rem(pl.program_id(0), groups) == group)
            def _():
                here = slice(group * width, (group + 1) * width)
                out_ref[...] = weights[0][:, here].astype(BF16)


def spread(weights, groups):
    ways = lax.axis_size("fsdp") // 2
    rows = weights[0].shape[0]
    width = sum(weight.shape[1] for weight in weights) // groups
    return run_kernel(
        functools.partial(spread_kernel, len(weights), groups),
        (ways,),
        [fixed(weight.shape) for weight in weights],
        by_rows(width) if rows == TILE else pl.BlockSpec((rows, width), lambda step: (step, 0)),
        jax.ShapeDtypeStruct((ways * rows, width), BF16),
    )(*weights)


def weight_kernel(count, half, order_ref, *refs):
    lefts, rights = refs[:count], refs[count : 2 * count]
    sent_ref, kept_ref = refs[2 * count :]

    def write(out_ref):
        for start in range(0, out_ref.shape[1], TILE):
            here = slice(start, start + TILE)
            total = dot_rows(lefts[0][...], rights[0][:, here])
            for number in range(1, count):
                total += dot_rows(lefts[number][...], rights[number][:, here])
            out_ref[:, here] = total.astype(BF16)

    @pl.when(pl.program_id(0) < half)
    def _():
        write(sent_ref)

    @pl.when(pl.program_id(0) >= half)
    def _():
        write(kept_ref)


def weight_grad(lefts, rights):
    count = len(lefts)
    rows, depth = lefts[0].shape
    cols = rights[0].shape[1]
    ways = lax.axis_size("fsdp")
    block, half = depth // ways, ways // 2
    side = my_bit("fsdp", 1).astype(jnp.int32)
    pairs = 2 * jnp.arange(half, dtype=jnp.int32)
    order = jnp.concatenate([pairs + 1 - side, pairs + side])
    if block % 128:
        lefts = [settle(left) for left in lefts]
        rights = [settle(right) for right in rights]
        total = sum(dot_rows(left, right) for left, right in zip(lefts, rights))
        blocks = total.astype(BF16).reshape(ways, block, cols)[order].reshape(-1, cols)
        return blocks[: block * half], blocks[block * half :]
    place = {
        "grid": (ways,),
        "in_specs": [pl.BlockSpec((rows, block), lambda step, order: (0, order[step]))] * count
        + [pl.BlockSpec((rows, cols), lambda step, order: (0, 0))] * count,
        "out_specs": [
            pl.BlockSpec((block, cols), lambda step, order: (jnp.minimum(step, half - 1), 0)),
            pl.BlockSpec((block, cols), lambda step, order: (jnp.maximum(step - half, 0), 0)),
        ],
    }
    return call_kernel(
        functools.partial(weight_kernel, count, half),
        place,
        [jax.ShapeDtypeStruct((half * block, cols), BF16)] * 2,
        [order, *lefts, *rights],
        scalars=1,
    )


def finish_kernel(rows, groups, in_ref, out_ref, square_ref):
    width = in_ref.shape[1]
    total_square = jnp.zeros((1, 1), F32)
    for group in range(groups):
        total = jnp.zeros((rows, width), F32)
        for block in range(group, in_ref.shape[0] // rows, groups):
            total += in_ref[block * rows : (block + 1) * rows, :].astype(F32)
        out_ref[:, group * width : (group + 1) * width] = total
        total_square += jnp.sum(total * total)
    square_ref[...] = jnp.broadcast_to(total_square, square_ref.shape)


def finish_shard(arrived, rows, groups):
    width = arrived.shape[1]
    shard, square = run_kernel(
        functools.partial(finish_kernel, rows, groups),
        (1,),
        [fixed(arrived.shape)],
        [fixed((rows, width * groups)), fixed((8, 128))],
        [
            jax.ShapeDtypeStruct((rows, width * groups), F32),
            jax.ShapeDtypeStruct((8, 128), F32),
        ],
    )(arrived)
    return shard, square


AXES = ("fsdp", "tp")
PAIR = 2


def swap(value, fsdp_mask, tp_mask, odd_masks=None):
    fsdp_ways, tp_ways = lax.axis_size("fsdp"), lax.axis_size("tp")
    pairs = []
    for row in range(fsdp_ways):
        for col in range(tp_ways):
            masks = (fsdp_mask, tp_mask)
            if odd_masks is not None and col & 1:
                masks = odd_masks
            pairs.append((row * tp_ways + col, (row ^ masks[0]) * tp_ways + (col ^ masks[1])))
    return lax.ppermute(settle(value), AXES, pairs)


def swap_bit(value, axis, bit):
    return swap(value, bit, 0) if axis == "fsdp" else swap(value, 0, bit)


def my_bit(axis, bit):
    return (lax.axis_index(axis) // bit) % 2


def bits_of(ways):
    return [1 << power for power in reversed(range(ways.bit_length() - 1))]


def trade_far(blocks):
    ways = lax.axis_size("fsdp")
    groups = [list(range(side, ways, 2)) for side in range(2)]
    return lax.all_to_all(settle(blocks), "fsdp", 0, 0, axis_index_groups=groups, tiled=True)


def cross(value):
    return swap(value, 1, 0)


def swap_one(value):
    return swap(value, 0, 2, (PAIR, 0))


def swap_two(value):
    return swap(value, PAIR, 0, (0, 2))


def gather_slot(block, other):
    other = settle(other)
    me = lax.axis_index("tp")
    near, far = swap(block, 0, 1), swap(other, 0, 1)
    return arrange([block, other, near, far], [me, me ^ 2, me ^ 1, me ^ 3])


def slot_kernel(x_ref, w_ref, order_ref, *outs):
    rows = outs[0].shape[0]
    place = order_ref[pl.program_id(0)]
    left = x_ref[pl.ds(pl.multiple_of(place * rows, rows), rows), :]
    for number, out_ref in enumerate(outs):

        @pl.when(pl.program_id(0) == number)
        def _(out_ref=out_ref):
            for start in range(0, out_ref.shape[1], TILE):
                here = slice(start, start + TILE)
                out_ref[:, here] = dot_last(left, w_ref[here, :]).astype(BF16)


def slot_product(left, weight):
    me = lax.axis_index("tp")
    rows = left.shape[0] // 4
    cols = weight_shape(weight)[0]
    order = jnp.stack([me ^ 3, me ^ 1, me ^ 2, me]).astype(jnp.int32)
    return run_weights(
        slot_kernel,
        (4,),
        [(fixed(left.shape), left)],
        [weight],
        [(pl.BlockSpec(memory_space=pltpu.SMEM), order)],
        [fixed((rows, cols))] * 4,
        [jax.ShapeDtypeStruct((rows, cols), BF16)] * 4,
    )


def sum_everywhere(value):
    for bit in bits_of(lax.axis_size("tp"))[::-1]:
        value = value + swap(value, 0, bit)
    for bit in bits_of(lax.axis_size("fsdp")):
        value = value + swap(value, bit, 0)
    return value


def on_device(
    tokens,
    out_grad,
    lengths,
    w_query,
    w_key,
    w_value,
    w_out,
    w_gate,
    w_up,
    w_down,
    norm_attn,
    norm_mlp,
    moment_query,
    moment_key,
    moment_value,
    moment_out,
    moment_gate,
    moment_up,
    moment_down,
    moment_norm_attn,
    moment_norm_mlp,
    square_query,
    square_key,
    square_value,
    square_out,
    square_gate,
    square_up,
    square_down,
    square_norm_attn,
    square_norm_mlp,
):
    rows_dev = tokens.shape[0]
    tp_ways = lax.axis_size("tp")
    slot_rows = rows_dev * tp_ways
    heads, heads_kv = w_query.shape[1] // HD, w_key.shape[1] // HD
    shard_rows = w_query.shape[0]
    length = lengths[0]
    row_pos = lax.axis_index("tp") * rows_dev + jnp.arange(rows_dev)
    gain_attn, gain_mlp = norm_attn[None], norm_mlp[None]
    far_rows = shard_rows * (lax.axis_size("fsdp") // 2)

    normed_attn = enter_norm(tokens, gain_attn)
    slot_other = swap(normed_attn, 0, 2)
    qkv_blocks = spread([pin(w_query, normed_attn), w_key, w_value], 1)
    qkv_rows = trade_far(qkv_blocks)
    out_blocks = spread([pin(w_out, qkv_blocks)], 1)
    gate_blocks = spread([pin(w_gate, out_blocks)], 2)
    cosine_table, sine_table = rotary_tables(slot_rows, HD)
    full_qkv = (qkv_rows, cross(qkv_rows))
    cotangent = jnp.where(row_pos[:, None] < length, out_grad, jnp.zeros_like(out_grad))
    grad_pair = swap(cotangent, PAIR, 0)
    attn_input = gather_slot(normed_attn, pin(slot_other, grad_pair))
    out_rows = trade_far(pin(out_blocks, qkv_rows, attn_input))
    full_out = (out_rows, cross(out_rows))
    grad_other, grad_both = swap(cotangent, 0, 2), swap(grad_pair, 0, 2)
    gate_rows = trade_far(pin(gate_blocks, out_rows))

    qkv_rot = project_qkv(pin(attn_input, out_rows), full_qkv, cosine_table, sine_table, heads + heads_kv)
    odd = my_bit("tp", 1)
    grad_mine = arrange(
        [pin(cotangent, qkv_rot), grad_other, grad_pair, grad_both], [0, 1 + odd, 2 - odd, 3]
    )
    grad_near = swap(grad_mine, 0, 1)
    up_blocks = spread([pin(w_up, qkv_rot)], 2)
    attn_bf = attend(pin(qkv_rot, up_blocks), lengths, heads, heads_kv)
    attn_parts = slot_product(pin(attn_bf, grad_mine), full_out)
    attn_got = [swap(part, 0, 1) for part in attn_parts[:2]]
    attn_sent = add_low(rows_dev, (attn_parts[2], 0), (attn_got[0], 0))
    attn_last = swap(attn_sent, 0, 2)
    gate_rows = settle(pin(gate_rows, attn_sent))
    gate_crossed = cross(gate_rows)
    full_gate = (gate_rows, gate_crossed)
    up_rows = trade_far(pin(up_blocks, gate_rows))
    down_blocks = spread([pin(w_down, attn_sent)], 2)
    middle, normed_mlp = middle_norm(
        rows_dev,
        [
            (tokens, 0),
            (attn_parts[3], 0),
            (attn_got[1], 0),
            (pin(attn_last, down_blocks, grad_near), 0),
        ],
        gain_mlp,
    )
    first = swap_one(normed_mlp)
    second = swap_two(normed_mlp)
    up_rows = settle(pin(up_rows, first, gate_crossed))
    up_crossed = cross(up_rows)
    full_up = (up_rows, up_crossed)
    both = swap_two(first)
    mlp_mine = arrange([normed_mlp, first, second, pin(both, up_crossed)], range(4))
    mlp_near = arrange([swap(one, 0, 1) for one in (normed_mlp, first, second, both)], range(4))
    down_rows = trade_far(pin(down_blocks, up_rows, first))
    hid_mine, upp_mine, gatep_mine = mlp_forward(mlp_mine, full_gate, full_up)
    down_rows = settle(pin(down_rows, hid_mine))
    full_down = (down_rows, cross(down_rows))
    hid_near, upp_near, gatep_near = mlp_forward(pin(mlp_near, down_rows), full_gate, full_up)

    down_sent, down_own = weight_grad([grad_mine, grad_near], [hid_mine, hid_near])
    down_got = cross(down_sent)
    dgate_near, dup_near = mlp_backward(pin(grad_near, down_own), full_down, upp_near, gatep_near)
    dgate_mine, dup_mine = mlp_backward(
        pin(grad_mine, dgate_near), full_down, upp_mine, gatep_mine
    )
    gate_sent, gate_own = weight_grad([mlp_mine, mlp_near], [dgate_mine, dgate_near])
    gate_got = cross(gate_sent)
    up_sent, up_own = weight_grad([pin(mlp_mine, gate_own), mlp_near], [dup_mine, dup_near])
    up_got = cross(up_sent)
    down_far = trade_far(add_low(far_rows, (pin(down_got, gate_own), 0), (down_own, 0)))
    back_near = back_product(pin(dgate_near, up_own), dup_near, full_gate, full_up, parts=4)
    back_got = [swap(part, 0, 1) for part in back_near]
    back_mine = back_product(pin(dgate_mine, back_near[0], gate_got), dup_mine, full_gate, full_up, parts=4)
    sent = [add_low(rows_dev, (back_mine[one], 0), (back_got[one], 0)) for one in (2, 3)]
    back_two = [swap_two(one) for one in sent]
    (out_near,) = back_product(pin(hid_near, *sent), full_down)
    (out_mine,) = back_product(pin(hid_mine, out_near), full_down)
    sent = add_low(
        rows_dev, (back_mine[1], 0), (back_got[1], 0), (pin(back_two[1], out_mine, down_far), 0)
    )
    back_one = swap_one(sent)
    out_got = swap(pin(out_near, sent), 0, 1)
    gate_far = trade_far(add_low(far_rows, (pin(gate_got, sent), 0), (gate_own, 0)))
    middle_grad, low_grad, gain_mlp_part = leave_norm(
        rows_dev,
        [(back_mine[0], 0), (back_got[0], 0), (back_two[0], 0), (pin(back_one, up_got), 0)],
        middle,
        cotangent,
        gain_mlp,
        [F32, BF16],
    )
    slot_other = swap(low_grad, 0, 2)
    attn_grad_in = gather_slot(low_grad, slot_other)
    proj_sent, proj_own = weight_grad([attn_grad_in], [attn_bf])
    proj_got = cross(proj_sent)
    query_grad, key_grad, value_grad = attend_back(
        pin(attn_grad_in, proj_own, gate_far),
        full_out, qkv_rot, lengths, cosine_table, sine_table, heads, heads_kv,
    )
    up_far = trade_far(add_low(far_rows, (pin(up_got, attn_grad_in, gate_far), 0), (up_own, 0)))
    shard_down, square_down_part = finish_shard(pin(down_far, query_grad), shard_rows, 2)
    sent = add_low(
        2 * rows_dev, (out_mine, 2 * rows_dev), (pin(out_got, query_grad), 2 * rows_dev)
    )
    out_two = swap_two(sent)
    qkv_grad = jnp.concatenate([query_grad, key_grad, value_grad], axis=1)
    qkv_sent, qkv_own = weight_grad([attn_input], [qkv_grad])
    qkv_got = cross(qkv_sent)
    input_parts = slot_product(pin(qkv_grad, qkv_own, proj_got), full_qkv)
    input_got = [swap(part, 0, 1) for part in input_parts[:2]]
    proj_low = add_low(far_rows, (pin(proj_got, up_far, input_parts[3]), 0), (proj_own, 0))
    proj_far = trade_far(proj_low)
    sent = add_low(
        rows_dev, (out_mine, rows_dev), (out_got, rows_dev), (pin(out_two, proj_low), rows_dev)
    )
    out_one = swap_one(sent)
    input_sent = add_low(
        rows_dev, (input_parts[2], 0), (pin(input_got[0], sent, qkv_got), 0)
    )
    input_last = swap(input_sent, 0, 2)
    shard_gate, square_gate_part = finish_shard(pin(gate_far, input_sent), shard_rows, 2)
    shard_up, square_up_part = finish_shard(pin(up_far, input_sent), shard_rows, 2)
    qkv_far = trade_far(add_low(far_rows, (pin(qkv_got, proj_far), 0), (qkv_own, 0)))
    input_grad, gain_attn_part = leave_norm(
        rows_dev,
        [(input_parts[3], 0), (input_got[1], 0), (pin(input_last, shard_gate, shard_up), 0)],
        tokens,
        middle_grad,
        gain_attn,
        [F32],
    )
    block_out = add_low(
        rows_dev,
        (middle, 0),
        (out_mine, 0),
        (out_got, 0),
        (out_two, 0),
        (pin(out_one, input_grad), 0),
    )
    gains = jnp.concatenate([gain_attn_part[0], gain_mlp_part[0]]).reshape(-1, 128)
    gains = sum_everywhere(gains).reshape(-1)
    shard_out, square_out_part = finish_shard(proj_far, shard_rows, 1)
    shard_qkv, square_qkv_part = finish_shard(qkv_far, shard_rows, 1)
    width_query, width_key = w_query.shape[1], w_key.shape[1]
    shard_grads = (
        shard_qkv[:, :width_query],
        shard_qkv[:, width_query : width_query + width_key],
        shard_qkv[:, width_query + width_key :],
        shard_out,
        shard_gate,
        shard_up,
        shard_down,
    )
    square_part = (
        square_down_part + square_gate_part + square_up_part + square_qkv_part + square_out_part
    )
    square_total = sum_everywhere(square_part)[0, 0]
    gain_attn_grad = gains[: norm_attn.shape[0]]
    gain_mlp_grad = gains[norm_attn.shape[0] :]
    clip_norm = jnp.sqrt(
        square_total
        + jnp.sum(gain_attn_grad * gain_attn_grad)
        + jnp.sum(gain_mlp_grad * gain_mlp_grad)
    )
    factor = jnp.minimum(1.0, MAX_NORM / (clip_norm + 1e-06))
    every_grad = tuple(shard_grads) + (gain_attn_grad, gain_mlp_grad)
    params = (w_query, w_key, w_value, w_out, w_gate, w_up, w_down, norm_attn, norm_mlp)
    moments = (
        moment_query,
        moment_key,
        moment_value,
        moment_out,
        moment_gate,
        moment_up,
        moment_down,
        moment_norm_attn,
        moment_norm_mlp,
    )
    squares = (
        square_query,
        square_key,
        square_value,
        square_out,
        square_gate,
        square_up,
        square_down,
        square_norm_attn,
        square_norm_mlp,
    )
    results = [
        adam_step(params[number], every_grad[number], moments[number], squares[number], factor)
        for number in range(9)
    ]
    return (
        block_out,
        input_grad,
        every_grad[0],
        every_grad[1],
        every_grad[2],
        every_grad[3],
        every_grad[4],
        every_grad[5],
        every_grad[6],
        every_grad[7],
        every_grad[8],
        results[0][0],
        results[1][0],
        results[2][0],
        results[3][0],
        results[4][0],
        results[5][0],
        results[6][0],
        results[7][0],
        results[8][0],
        results[0][1],
        results[1][1],
        results[2][1],
        results[3][1],
        results[4][1],
        results[5][1],
        results[6][1],
        results[7][1],
        results[8][1],
        results[0][2],
        results[1][2],
        results[2][2],
        results[3][2],
        results[4][2],
        results[5][2],
        results[6][2],
        results[7][2],
        results[8][2],
        clip_norm,
    )


def solution(mesh):
    return jax.shard_map(
        on_device,
        mesh=mesh,
        in_specs=(
            P(("fsdp", "tp"), None),
            P(("fsdp", "tp"), None),
            P("fsdp"),
            P("fsdp", "tp"),
            P("fsdp", "tp"),
            P("fsdp", "tp"),
            P("fsdp", "tp"),
            P("fsdp", "tp"),
            P("fsdp", "tp"),
            P("fsdp", "tp"),
            P(),
            P(),
            P("fsdp", "tp"),
            P("fsdp", "tp"),
            P("fsdp", "tp"),
            P("fsdp", "tp"),
            P("fsdp", "tp"),
            P("fsdp", "tp"),
            P("fsdp", "tp"),
            P(),
            P(),
            P("fsdp", "tp"),
            P("fsdp", "tp"),
            P("fsdp", "tp"),
            P("fsdp", "tp"),
            P("fsdp", "tp"),
            P("fsdp", "tp"),
            P("fsdp", "tp"),
            P(),
            P(),
        ),
        out_specs=(
            P(("fsdp", "tp"), None),
            P(("fsdp", "tp"), None),
            P("fsdp", "tp"),
            P("fsdp", "tp"),
            P("fsdp", "tp"),
            P("fsdp", "tp"),
            P("fsdp", "tp"),
            P("fsdp", "tp"),
            P("fsdp", "tp"),
            P(),
            P(),
            P("fsdp", "tp"),
            P("fsdp", "tp"),
            P("fsdp", "tp"),
            P("fsdp", "tp"),
            P("fsdp", "tp"),
            P("fsdp", "tp"),
            P("fsdp", "tp"),
            P(),
            P(),
            P("fsdp", "tp"),
            P("fsdp", "tp"),
            P("fsdp", "tp"),
            P("fsdp", "tp"),
            P("fsdp", "tp"),
            P("fsdp", "tp"),
            P("fsdp", "tp"),
            P(),
            P(),
            P("fsdp", "tp"),
            P("fsdp", "tp"),
            P("fsdp", "tp"),
            P("fsdp", "tp"),
            P("fsdp", "tp"),
            P("fsdp", "tp"),
            P("fsdp", "tp"),
            P(),
            P(),
            P(),
        ),
        check_vma=False,
    )
```

time: 2380 us -> 792 us (0.33)
  waiting for transfers between devices: 1940 us -> 305 us
  Pallas kernels: 0 us -> 279 us
  matrix products: 240 us -> 0 us
  starting transfers between devices: 1.88 us -> 86.7 us
  other arithmetic: 86.4 us -> 22.9 us
  local copies, waits for them, and re-layouts: 24.1 us -> 80.4 us
  blocking collectives: 40 us -> 0 us
    reduce_scatter x11 -> x0, waiting for transfers between devices: 1320 us -> none  [the longest x1 285 us: on_device(): lax.psum_scatter(grad_gate, 'fsdp', scatter_dimension=0, tiled=True)]
    all_gather x11 -> x0, waiting for transfers between devices: 620 us -> none  [the longest x1 128 us: on_device(): lax.all_gather(low_down, 'fsdp', axis=0, tiled=True)]
    pallas_call x0 -> x59, Pallas kernels: none -> 279 us  [call_kernel(): pl.pallas_call(body, grid_spec=spec, out_shape=out_shape, input_output_al...]
    ppermute x0 -> x53, waiting for transfers between devices: none -> 278 us  [swap(): return lax.ppermute(settle(value), AXES, pairs)]
    dot_general x35 -> x0, matrix products: 240 us -> none  [the longest x7 68.9 us: dot_rows(): lax.dot_general(left, right, (((0,), (0,)), ((), ())), preferred_element_...]
    unnamed x138 -> x241, local copies, waits for them, and re-layouts: 14.9 us -> 79.8 us
    all_to_all x0 -> x10, starting transfers between devices: none -> 45.8 us  [trade_far(): lax.all_to_all(settle(blocks), 'fsdp', 0, 0, axis_index_groups=groups, ti...]
    ppermute x0 -> x53, starting transfers between devices: none -> 40.8 us  [swap(): return lax.ppermute(settle(value), AXES, pairs)]
  transfers between devices with their start and end apart: 22 -> 63, of which waited for: 21 -> 29; matrix products, arithmetic and copies ran while one was open for 8% -> 1% of each run, Pallas kernels for 0% -> 35%
where the time goes in v2:
time: 792 us; the launch traced here: 780 us
  waiting for transfers between devices  305 us (39%)
  Pallas kernels  279 us (35%)
  starting transfers between devices  86.7 us (11%)
  local copies, waits for them, and re-layouts  80.4 us (10%)
  other arithmetic  22.9 us (3%)
    pallas_call x59, Pallas kernels, call_kernel(): pl.pallas_call(body, grid_spec=spec, out_shape=out_shape, input_output_al...  279 us
    ppermute x53, waiting for transfers between devices, swap(): return lax.ppermute(settle(value), AXES, pairs)  278 us
    unnamed x241, local copies, waits for them, and re-layouts  79.8 us
    all_to_all x10, starting transfers between devices, trade_far(): lax.all_to_all(settle(blocks), 'fsdp', 0, 0, axis_index_groups=groups, ti...  45.8 us
    ppermute x53, starting transfers between devices, swap(): return lax.ppermute(settle(value), AXES, pairs)  40.8 us
    all_to_all x10, waiting for transfers between devices, trade_far(): lax.all_to_all(settle(blocks), 'fsdp', 0, 0, axis_index_groups=groups, ti...  26.4 us
    mul x7, other arithmetic, adam_step(): -LEARN_RATE  19.9 us
  transfers between devices with their start and end apart: 63, of which 29 were waited for; matrix products, arithmetic and copies ran while one was open for 1% of the time, Pallas kernels for 35%

profile of v2, /device:TPU:0, one launch (start us, length us, event | category | flops | bytes accessed | tf_op | source)
XLA Modules:
  0.0 780.3 jit_solution(16560276818558078704)
XLA Ops:
  6.1 6.4 all-to-all-start
  17.9 19.6 %collective-permute-done.refs_0_ = bf16[256,2048]{1,0:T(8,128)(2,1)} collective-permute-done((bf16[256,2048]{1,0:T(8,128)(2,1)}, bf16[256,2048]{1,0:T(8,128)(2,1)}, u32[]{:S(2)}, u32[]{:S(2)}) %collective-permute-start) | collective-permute-done | bytes 1048608 | tf_op jit(solution)/shard_map/ppermute | solution.py:682
  37.5 33.7 %collective-permute-done.1.refs_1_.refs_3_ = bf16[256,2048]{1,0:T(8,128)(2,1)} collective-permute-done((bf16[256,2048]{1,0:T(8,128)(2,1)S(1)}, bf16[256,2048]{1,0:T(8,128)(2,1)}, u32[]{:S(2)}, u32[]{:S(2)}) %collective-permute-start.1) | collective-permute-done | bytes 1048608 | tf_op jit(solution)/shard_map/ppermute | solution.py:682
  74.2 5.2 shard_map.591.refs_2_.refs_1_
  82.4 3.7 all-to-all-start.1
  94.1 18.1 %all-to-all-done.1 = bf16[4,256,512]{2,1,0:T(8,128)(2,1)S(1)} async-done(((bf16[4,256,512]{2,1,0:T(8,128)(2,1)}), bf16[4,256,512]{2,1,0:T(8,128)(2,1)S(1)}, u32[]{:S(2)}, u32[]{:S(2)}) %all-to-all-start.1) | async-done | bytes 1048608 | tf_op jit(solution)/shard_map/all_to_all | solution.py:700
  115.5 4.5 all-to-all-start.2
  123.6 11.1 %collective-permute-done.4.refs_3_ = bf16[1024,1024]{1,0:T(8,128)(2,1)} collective-permute-done((bf16[1024,1024]{1,0:T(8,128)(2,1)S(1)}, bf16[1024,1024]{1,0:T(8,128)(2,1)}, u32[]{:S(2)}, u32[]{:S(2)}) %collective-permute-start.4) | collective-permute-done | bytes 2097184 | tf_op jit(solution)/shard_map/ppermute | solution.py:682
  134.7 8.8 %shard_map.595.refs_1_.refs_2_.refs_3_.refs_5_.refs_6_.refs_7_ = bf16[1024,1024]{1,0:T(8,128)(2,1)S(1)} custom-call(s32[1]{0:T(128)} %bitcast.refs_0_, bf16[1024,2048]{1,0:T(8,128)(2,1)} %shard_map.591.refs_2_.refs_1_, bf16[1024,1024]{1,0:T(8,128)(2,1)} %bitcast.44, bf16[1024,1024]{1,0:T(8,128)(2,1)} %collective-permute-done.4.refs_3_, ...), custom_call_target="tpu_custom_call" | custom-call | flops 1 | bytes 1 | tf_op jit(solution)/shard_map/pallas_call | solution.py:96
  144.9 5.0 shard_map.598.refs_5_.refs_1_
  151.5 7.2 shard_map.597.refs_1_.refs_2_
  159.8 5.4 shard_map.599
  171.4 5.3 all-to-all-start.3
  183.0 19.2 %collective-permute-done.10.refs_3_ = bf16[256,2048]{1,0:T(8,128)(2,1)S(1)} collective-permute-done((bf16[256,2048]{1,0:T(8,128)(2,1)S(1)}, bf16[256,2048]{1,0:T(8,128)(2,1)S(1)}, u32[]{:S(2)}, u32[]{:S(2)}) %collective-permute-start.10) | collective-permute-done | bytes 1048608 | tf_op jit(solution)/shard_map/ppermute | solution.py:682
  206.0 20.2 %collective-permute-done.15.refs_2_.refs_3_.refs_4_ = bf16[1024,1024]{1,0:T(8,128)(2,1)S(1)} collective-permute-done((bf16[1024,1024]{1,0:T(8,128)(2,1)}, bf16[1024,1024]{1,0:T(8,128)(2,1)S(1)}, u32[]{:S(2)}, u32[]{:S(2)}) %collective-permute-start.15) | collective-permute-done | bytes 2097184 | tf_op jit(solution)/shard_map/ppermute | solution.py:682
  232.0 5.3 all-to-all-start.4
  241.5 42.2 %collective-permute-done.13.refs_3_ = bf16[256,2048]{1,0:T(8,128)(2,1)S(1)} collective-permute-done((bf16[256,2048]{1,0:T(8,128)(2,1)}, bf16[256,2048]{1,0:T(8,128)(2,1)S(1)}, u32[]{:S(2)}, u32[]{:S(2)}) %collective-permute-start.13) | collective-permute-done | bytes 1048608 | tf_op jit(solution)/shard_map/ppermute | solution.py:682
  283.7 13.4 %collective-permute-done.14.refs_4_ = bf16[256,2048]{1,0:T(8,128)(2,1)S(1)} collective-permute-done((bf16[256,2048]{1,0:T(8,128)(2,1)S(1)}, bf16[256,2048]{1,0:T(8,128)(2,1)S(1)}, u32[]{:S(2)}, u32[]{:S(2)}) %collective-permute-start.14) | collective-permute-done | bytes 1048608 | tf_op jit(solution)/shard_map/ppermute | solution.py:682
  299.7 3.2 shard_map.608.refs_1_
  302.9 3.1 shard_map.612.refs_1_.refs_2_
  305.9 15.5 %shard_map.609 = (bf16[1024,1024]{1,0:T(8,128)(2,1)S(1)}, bf16[1024,1024]{1,0:T(8,128)(2,1)S(1)}, bf16[1024,1024]{1,0:T(8,128)(2,1)}) custom-call(s32[1]{0:T(128)} %bitcast.refs_0_, bf16[1024,2048]{1,0:T(8,128)(2,1)} %shard_map.608.refs_1_, bf16[1024,1024]{1,0:T(8,128)(2,1)} %shard_map.605.refs_1_.refs_2_.refs_3_, bf16[1024,1024]{1,0:T(8,128)(2,1)} %copy-done.3, ...), custom_call_target="tpu_custom_call" | custom-call | flops 1 | bytes 1 | tf_op jit(solution)/shard_map/pallas_call | solution.py:96
  325.7 15.5 %shard_map.613 = (bf16[1024,1024]{1,0:T(8,128)(2,1)S(1)}, bf16[1024,1024]{1,0:T(8,128)(2,1)S(1)}, bf16[1024,1024]{1,0:T(8,128)(2,1)}) custom-call(s32[1]{0:T(128)} %bitcast.refs_0_, bf16[1024,2048]{1,0:T(8,128)(2,1)} %shard_map.612.refs_1_.refs_2_, bf16[1024,1024]{1,0:T(8,128)(2,1)} %shard_map.605.refs_1_.refs_2_.refs_3_, bf16[1024,1024]{1,0:T(8,128)(2,1)} %copy-done.3, ...), custom_call_target="tpu_custom_call" | custom-call | flops 1 | bytes 1 | tf_op jit(solution)/shard_map/pallas_call | solution.py:96
  343.9 13.9 %shard_map.614 = (bf16[1024,1024]{1,0:T(8,128)(2,1)S(1)}, bf16[1024,1024]{1,0:T(8,128)(2,1)S(1)}) custom-call(s32[8]{0:T(128)S(1)} %pad_add_fusion.3.refs_0_, bf16[1024,2048]{1,0:T(8,128)(2,1)} %shard_map.598.refs_5_.refs_1_, bf16[1024,2048]{1,0:T(8,128)(2,1)} %collective-permute-done.11.refs_6_.refs_2_.refs_1_, bf16[1024,1024]{1,0:T(8,128)(2,1)} %copy-done.16, ...), custom_call_target="tpu_custom_call" | custom-call | flops 1 | bytes 1 | tf_op jit(solution)/shard_map/pallas_call | solution.py:96
  359.6 13.2 %collective-permute-done.17.refs_3_ = bf16[1024,1024]{1,0:T(8,128)(2,1)S(1)} collective-permute-done((bf16[1024,1024]{1,0:T(8,128)(2,1)}, bf16[1024,1024]{1,0:T(8,128)(2,1)S(1)}, u32[]{:S(2)}, u32[]{:S(2)}) %collective-permute-start.17) | collective-permute-done | bytes 2097184 | tf_op jit(solution)/shard_map/ppermute | solution.py:682
  374.0 9.5 %shard_map.615 = (bf16[1024,1024]{1,0:T(8,128)(2,1)S(1)}, bf16[1024,1024]{1,0:T(8,128)(2,1)S(1)}) custom-call(s32[1]{0:T(128)} %bitcast.refs_0_, bf16[1024,2048]{1,0:T(8,128)(2,1)} %collective-permute-done.11.refs_6_.refs_2_.refs_1_, bf16[1024,1024]{1,0:T(8,128)(2,1)} %shard_map.611.refs_6_.refs_2_, bf16[1024,1024]{1,0:T(8,128)(2,1)} %copy-done.97, ...), custom_call_target="tpu_custom_call" | custom-call | flops 1 | bytes 1 | tf_op jit(solution)/shard_map/pallas_call | solution.py:96
  386.2 9.5 %shard_map.616 = (bf16[1024,1024]{1,0:T(8,128)(2,1)S(1)}, bf16[1024,1024]{1,0:T(8,128)(2,1)S(1)}) custom-call(s32[1]{0:T(128)} %bitcast.refs_0_, bf16[1024,2048]{1,0:T(8,128)(2,1)} %shard_map.598.refs_5_.refs_1_, bf16[1024,1024]{1,0:T(8,128)(2,1)} %shard_map.611.refs_6_.refs_2_, bf16[1024,1024]{1,0:T(8,128)(2,1)} %copy-done.97, ...), custom_call_target="tpu_custom_call" | custom-call | flops 1 | bytes 1 | tf_op jit(solution)/shard_map/pallas_call | solution.py:96
  398.3 15.0 %shard_map.617 = (bf16[1024,1024]{1,0:T(8,128)(2,1)}, bf16[1024,1024]{1,0:T(8,128)(2,1)S(1)}) custom-call(s32[8]{0:T(128)S(1)} %pad_add_fusion.3.refs_0_, bf16[1024,2048]{1,0:T(8,128)(2,1)} %shard_map.608.refs_1_, bf16[1024,2048]{1,0:T(8,128)(2,1)} %shard_map.612.refs_1_.refs_2_, bf16[1024,1024]{1,0:T(8,128)(2,1)} %copy-done.40, bf16[1024,1024]{1,0:T(8,128)(2,1)} %copy-done.26), custom_call_target="tpu_custom_call" | custom-call | flops 1 | bytes 1 | tf_op jit(solution)/shard_map/pallas_call | solution.py:96
  421.6 3.7 all-to-all-start.5
  425.4 14.8 %shard_map.618 = (bf16[1024,1024]{1,0:T(8,128)(2,1)}, bf16[1024,1024]{1,0:T(8,128)(2,1)S(1)}) custom-call(s32[8]{0:T(128)S(1)} %pad_add_fusion.3.refs_0_, bf16[1024,2048]{1,0:T(8,128)(2,1)} %shard_map.608.refs_1_, bf16[1024,2048]{1,0:T(8,128)(2,1)} %shard_map.612.refs_1_.refs_2_, bf16[1024,1024]{1,0:T(8,128)(2,1)} %copy-done.50, ...), custom_call_target="tpu_custom_call" | custom-call | flops 1 | bytes 1 | tf_op jit(solution)/shard_map/pallas_call | solution.py:96
  441.5 15.5 %shard_map.619 = (bf16[256,2048]{1,0:T(8,128)(2,1)}, bf16[256,2048]{1,0:T(8,128)(2,1)S(1)}, bf16[256,2048]{1,0:T(8,128)(2,1)S(1)}, bf16[256,2048]{1,0:T(8,128)(2,1)S(1)}) custom-call(s32[1]{0:T(128)} %bitcast.refs_0_, bf16[1024,1024]{1,0:T(8,128)(2,1)} %copy-done.26, bf16[1024,1024]{1,0:T(8,128)(2,1)} %copy-done.58, ...), custom_call_target="tpu_custom_call" | custom-call | flops 1 | bytes 1 | tf_op jit(solution)/shard_map/pallas_call | solution.py:96
  457.7 4.7 collective-permute-done.22.refs_8_.refs_0_
  462.3 14.9 %shard_map.620 = (bf16[256,2048]{1,0:T(8,128)(2,1)S(1)}, bf16[256,2048]{1,0:T(8,128)(2,1)S(1)}, bf16[256,2048]{1,0:T(8,128)(2,1)S(1)}, bf16[256,2048]{1,0:T(8,128)(2,1)S(1)}) custom-call(s32[1]{0:T(128)} %bitcast.refs_0_, bf16[1024,1024]{1,0:T(8,128)(2,1)} %copy-done.40, bf16[1024,1024]{1,0:T(8,128)(2,1)} %copy-done.50, ...), custom_call_target="tpu_custom_call" | custom-call | flops 1 | bytes 1 | tf_op jit(solution)/shard_map/pallas_call | solution.py:96
  481.9 8.8 %shard_map.623.refs_4_.refs_0_ = bf16[1024,2048]{1,0:T(8,128)(2,1)} custom-call(s32[1]{0:T(128)} %bitcast.refs_0_, bf16[1024,1024]{1,0:T(8,128)(2,1)S(1)} %copy-done.39, bf16[1024,1024]{1,0:T(8,128)(2,1)} %shard_map.611.refs_6_.refs_2_, bf16[1024,1024]{1,0:T(8,128)(2,1)} %copy-done.97, bf16[256,2048]{1,0:T(8,128)(2,1)} %shard_map.621.refs_4_, ...), custom_call_target="tpu_custom_call" | custom-call | flops 1 | bytes 1 | tf_op jit(solution)/shard_map/pallas_call | solution.py:96
  492.6 8.5 %shard_map.624.refs_3_.refs_0_.refs_1_ = bf16[1024,2048]{1,0:T(8,128)(2,1)} custom-call(s32[1]{0:T(128)} %bitcast.refs_0_, bf16[1024,1024]{1,0:T(8,128)(2,1)S(1)} %copy-done.17, bf16[1024,1024]{1,0:T(8,128)(2,1)} %shard_map.611.refs_6_.refs_2_, bf16[1024,1024]{1,0:T(8,128)(2,1)} %copy-done.97, bf16[1024,2048]{1,0:T(8,128)(2,1)} %shard_map.623.refs_4_.refs_0_), custom_call_target="tpu_custom_call" | custom-call | flops 1 | bytes 1 | tf_op jit(solution)/shard_map/pallas_call | solution.py:96
  508.8 3.0 shard_map.631
  513.2 3.9 all-to-all-start.6
  517.1 8.6 %collective-permute-done.32.refs_7_.refs_0_ = bf16[1024,1024]{1,0:T(8,128)(2,1)} collective-permute-done((bf16[1024,1024]{1,0:T(8,128)(2,1)}, bf16[1024,1024]{1,0:T(8,128)(2,1)}, u32[]{:S(2)}, u32[]{:S(2)}) %collective-permute-start.32) | collective-permute-done | bytes 2097184 | tf_op jit(solution)/shard_map/ppermute | solution.py:682
  526.9 5.6 shard_map.628
  533.9 22.4 %collective-permute-done.33.refs_2_ = bf16[256,2048]{1,0:T(8,128)(2,1)S(1)} collective-permute-done((bf16[256,2048]{1,0:T(8,128)(2,1)S(1)}, bf16[256,2048]{1,0:T(8,128)(2,1)S(1)}, u32[]{:S(2)}, u32[]{:S(2)}) %collective-permute-start.33) | collective-permute-done | bytes 1048608 | tf_op jit(solution)/shard_map/ppermute | solution.py:682
  558.9 3.0 shard_map.629.refs_1_.refs_2_
  561.9 3.4 all-to-all-done.6
  566.7 3.0 shard_map.634
  571.1 3.6 all-to-all-start.7
  575.9 7.4 shard_map.630
  584.8 14.4 %shard_map.632 = (bf16[1024,512]{1,0:T(8,128)(2,1)S(1)}, bf16[1024,256]{1,0:T(8,128)(2,1)S(1)}, bf16[1024,256]{1,0:T(8,128)(2,1)S(1)}) custom-call(s32[1]{0:T(128)} %bitcast.refs_0_, bf16[1024,2048]{1,0:T(8,128)(2,1)} %shard_map.629.refs_1_.refs_2_, bf16[1024,512]{1,0:T(8,128)(2,1)S(1)} %bitcast.54, bf16[1024,512]{1,0:T(8,128)(2,1)S(1)} %copy-done.62, ...), custom_call_target="tpu_custom_call" | custom-call | flops 1 | bytes 1 | tf_op jit(solution)/shard_map/pallas_call | solution.py:96
  600.8 10.6 %shard_map.635 = (bf16[1024,1024]{1,0:T(8,128)(2,1)}, bf16[1024,1024]{1,0:T(8,128)(2,1)S(1)}) custom-call(s32[8]{0:T(128)S(1)} %pad_add_fusion.3.refs_0_, bf16[1024,2048]{1,0:T(8,128)(2,1)} %shard_map.591.refs_2_.refs_1_, bf16[1024,1024]{1,0:T(8,128)(2,1)} %copy-done.98), custom_call_target="tpu_custom_call" | custom-call | flops 1 | bytes 1 | tf_op jit(solution)/shard_map/pallas_call | solution.py:96
  614.2 10.9 %shard_map.636 = (bf16[256,2048]{1,0:T(8,128)(2,1)}, bf16[256,2048]{1,0:T(8,128)(2,1)}, bf16[256,2048]{1,0:T(8,128)(2,1)S(1)}, bf16[256,2048]{1,0:T(8,128)(2,1)S(1)}) custom-call(s32[1]{0:T(128)} %bitcast.refs_0_, bf16[1024,1024]{1,0:T(8,128)(2,1)} %copy-done.98, bf16[1024,1024]{1,0:T(8,128)(2,1)} %bitcast.45, ...), custom_call_target="tpu_custom_call" | custom-call | flops 1 | bytes 1 | tf_op jit(solution)/shard_map/pallas_call | solution.py:96
  634.7 5.1 all-to-all-start.8
  639.7 4.3 shard_map.633
  646.0 13.7 %collective-permute-done.41.refs_3_.refs_0_ = bf16[1024,1024]{1,0:T(8,128)(2,1)} collective-permute-done((bf16[1024,1024]{1,0:T(8,128)(2,1)}, bf16[1024,1024]{1,0:T(8,128)(2,1)}, u32[]{:S(2)}, u32[]{:S(2)}) %collective-permute-start.41) | collective-permute-done | bytes 2097184 | tf_op jit(solution)/shard_map/ppermute | solution.py:682
  659.7 4.8 all-to-all-done.8
  664.5 3.0 shard_map.644
  668.9 4.4 all-to-all-start.9
  673.9 21.0 %collective-permute-done.36.refs_2_.refs_3_ = bf16[512,2048]{1,0:T(8,128)(2,1)} collective-permute-done((bf16[512,2048]{1,0:T(8,128)(2,1)}, bf16[512,2048]{1,0:T(8,128)(2,1)}, u32[]{:S(2)}, u32[]{:S(2)}) %collective-permute-start.36) | collective-permute-done | bytes 2097184 | tf_op jit(solution)/shard_map/ppermute | solution.py:682
  695.0 2.7 shard_map.638.refs_2_
  703.6 9.3 %collective-permute-done.42.refs_2_ = bf16[256,2048]{1,0:T(8,128)(2,1)S(1)} collective-permute-done((bf16[256,2048]{1,0:T(8,128)(2,1)S(1)}, bf16[256,2048]{1,0:T(8,128)(2,1)S(1)}, u32[]{:S(2)}, u32[]{:S(2)}) %collective-permute-start.42) | collective-permute-done | bytes 1048608 | tf_op jit(solution)/shard_map/ppermute | solution.py:682
  712.9 4.9 shard_map.642
  720.5 4.0 collective-permute-done.44
  726.2 2.9 collective-permute-done.45
  737.5 4.4 collective-permute-done.50
  745.6 4.5 shard_map.643
  756.5 7.0 add_multiply_fusion.1
  763.5 4.0 add_multiply_fusion.2
  772.6 4.0 add_multiply_fusion
  (398 shorter events, 166.8 us)
Async XLA Ops:
  6.1 73.3 %all-to-all-start = ((bf16[4,256,1024]{2,1,0:T(8,128)(2,1)}), bf16[4,256,1024]{2,1,0:T(8,128)(2,1)S(1)}, u32[]{:S(2)}, u32[]{:S(2)}) async-start(bf16[4,256,1024]{2,1,0:T(8,128)(2,1)} %bitcast.59), calls=%async_computation | async-start | bytes 4194304 | tf_op jit(solution)/shard_map/all_to_all | solution.py:700
  12.6 24.9 %collective-permute-start = (bf16[256,2048]{1,0:T(8,128)(2,1)}, bf16[256,2048]{1,0:T(8,128)(2,1)}, u32[]{:S(2)}, u32[]{:S(2)}) collective-permute-start(bf16[256,2048]{1,0:T(8,128)(2,1)} %shard_map.589.refs_1_.refs_3_), channel_id=1, source_target_pairs={{0,2},{1,3},{2,0},{3,1},{4,6},{5,7},{6,4},{7,5},{8,10},{9,11},{10,... | collective-permute-start | bytes 3145736 | tf_op jit(solution)/shard_map/ppermute | solution.py:682
  15.9 55.4 %copy-start.70 = (f32[256,512]{1,0:T(8,128)S(1)}, f32[256,512]{1,0:T(8,128)}, u32[]{:S(2)}) copy-start(f32[256,512]{1,0:T(8,128)} %refs_0_.10) | copy-start | bytes 1572868
  15.9 55.3 %collective-permute-start.1 = (bf16[256,2048]{1,0:T(8,128)(2,1)S(1)}, bf16[256,2048]{1,0:T(8,128)(2,1)}, u32[]{:S(2)}, u32[]{:S(2)}) collective-permute-start(bf16[256,2048]{1,0:T(8,128)(2,1)S(1)} %broadcast_select_fusion.refs_1_.refs_5_), channel_id=1, source_target_pairs={{0,8},{1,9},{2,10},{3,11},{4,12},{5,13},{6,14},{7,15},{8,0},{9,1},... | collective-permute-start | bytes 3145736 | tf_op jit(solution)/shard_map/ppermute | solution.py:682
  17.9 54.6 %collective-permute-start.2 = (bf16[256,2048]{1,0:T(8,128)(2,1)}, bf16[256,2048]{1,0:T(8,128)(2,1)}, u32[]{:S(2)}, u32[]{:S(2)}) collective-permute-start(bf16[256,2048]{1,0:T(8,128)(2,1)} %shard_map.589.refs_1_.refs_3_), channel_id=1, source_target_pairs={{0,1},{1,0},{2,3},{3,2},{4,5},{5,4},{6,7},{7,6},{8,9},{9,8},{10,11... | collective-permute-start | bytes 3145736 | tf_op jit(solution)/shard_map/ppermute | solution.py:682
  71.2 3.0 collective-permute-start.3
  82.4 29.8 %all-to-all-start.1 = ((bf16[4,256,512]{2,1,0:T(8,128)(2,1)}), bf16[4,256,512]{2,1,0:T(8,128)(2,1)S(1)}, u32[]{:S(2)}, u32[]{:S(2)}) async-start(bf16[4,256,512]{2,1,0:T(8,128)(2,1)} %bitcast.63), calls=%async_computation.1 | async-start | bytes 2097152 | tf_op jit(solution)/shard_map/all_to_all | solution.py:700
  86.1 48.6 %collective-permute-start.4 = (bf16[1024,1024]{1,0:T(8,128)(2,1)S(1)}, bf16[1024,1024]{1,0:T(8,128)(2,1)}, u32[]{:S(2)}, u32[]{:S(2)}) collective-permute-start(bf16[1024,1024]{1,0:T(8,128)(2,1)S(1)} %bitcast.43), channel_id=1, source_target_pairs={{0,4},{1,5},{2,6},{3,7},{4,0},{5,1},{6,2},{7,3},{8,12},{9,13},{10,... | collective-permute-start | bytes 6291464 | tf_op jit(solution)/shard_map/ppermute | solution.py:682
  87.6 57.2 %collective-permute-start.6 = (bf16[256,2048]{1,0:T(8,128)(2,1)}, bf16[256,2048]{1,0:T(8,128)(2,1)}, u32[]{:S(2)}, u32[]{:S(2)}) collective-permute-start(bf16[256,2048]{1,0:T(8,128)(2,1)} %copy-done.36), channel_id=1, source_target_pairs={{0,2},{1,3},{2,0},{3,1},{4,6},{5,7},{6,4},{7,5},{8,10},{9,11},{10,... | collective-permute-start | bytes 3145736 | tf_op jit(solution)/shard_map/ppermute | solution.py:682
  93.6 51.3 %collective-permute-start.7 = (bf16[256,2048]{1,0:T(8,128)(2,1)}, bf16[256,2048]{1,0:T(8,128)(2,1)}, u32[]{:S(2)}, u32[]{:S(2)}) collective-permute-start(bf16[256,2048]{1,0:T(8,128)(2,1)} %collective-permute-done.1.refs_1_.refs_3_), channel_id=1, source_target_pairs={{0,2},{1,3},{2,0},{3,1},{4,6},{5,7},{6,4},{7,5},{8,10},{9,11},{10,... | collective-permute-start | bytes 3145736 | tf_op jit(solution)/shard_map/ppermute | solution.py:682
  115.5 54.5 %all-to-all-start.2 = ((bf16[4,256,1024]{2,1,0:T(8,128)(2,1)}), bf16[4,256,1024]{2,1,0:T(8,128)(2,1)}, u32[]{:S(2)}, u32[]{:S(2)}) async-start(bf16[4,256,1024]{2,1,0:T(8,128)(2,1)} %bitcast.60), calls=%async_computation.2 | async-start | bytes 4194304 | tf_op jit(solution)/shard_map/all_to_all | solution.py:700
  122.0 36.7 %collective-permute-start.5 = (bf16[1024,512]{1,0:T(8,128)(2,1)S(1)}, bf16[1024,512]{1,0:T(8,128)(2,1)S(1)}, u32[]{:S(2)}, u32[]{:S(2)}) collective-permute-start(bf16[1024,512]{1,0:T(8,128)(2,1)S(1)} %bitcast.51), channel_id=1, source_target_pairs={{0,4},{1,5},{2,6},{3,7},{4,0},{5,1},{6,2},{7,3},{8,12},{9,13},{10,... | collective-permute-start | bytes 3145736 | tf_op jit(solution)/shard_map/ppermute | solution.py:682
  149.9 52.4 %collective-permute-start.11 = (bf16[1024,2048]{1,0:T(8,128)(2,1)}, bf16[1024,2048]{1,0:T(8,128)(2,1)}, u32[]{:S(2)}, u32[]{:S(2)}) collective-permute-start(bf16[1024,2048]{1,0:T(8,128)(2,1)} %shard_map.598.refs_5_.refs_1_), channel_id=1, source_target_pairs={{0,1},{1,0},{2,3},{3,2},{4,5},{5,4},{6,7},{7,6},{8,9},{9,8},{10,11... | collective-permute-start | bytes 12582920 | tf_op jit(solution)/shard_map/ppermute | solution.py:682
  167.1 2.7 collective-permute-start.9
  171.4 56.1 %all-to-all-start.3 = ((bf16[4,256,1024]{2,1,0:T(8,128)(2,1)}), bf16[4,256,1024]{2,1,0:T(8,128)(2,1)S(1)}, u32[]{:S(2)}, u32[]{:S(2)}) async-start(bf16[4,256,1024]{2,1,0:T(8,128)(2,1)} %bitcast.41), calls=%async_computation.3 | async-start | bytes 4194304 | tf_op jit(solution)/shard_map/all_to_all | solution.py:700
  176.7 6.3 collective-permute-start.8
  176.7 25.6 %collective-permute-start.10 = (bf16[256,2048]{1,0:T(8,128)(2,1)S(1)}, bf16[256,2048]{1,0:T(8,128)(2,1)S(1)}, u32[]{:S(2)}, u32[]{:S(2)}) collective-permute-start(bf16[256,2048]{1,0:T(8,128)(2,1)S(1)} %shard_map.600.refs_1_), channel_id=1, source_target_pairs={{0,2},{1,3},{2,0},{3,1},{4,6},{5,7},{6,4},{7,5},{8,10},{9,11},{10,... | collective-permute-start | bytes 3145736 | tf_op jit(solution)/shard_map/ppermute | solution.py:682
  178.3 47.9 %collective-permute-start.15 = (bf16[1024,1024]{1,0:T(8,128)(2,1)}, bf16[1024,1024]{1,0:T(8,128)(2,1)S(1)}, u32[]{:S(2)}, u32[]{:S(2)}) collective-permute-start(bf16[1024,1024]{1,0:T(8,128)(2,1)} %shard_map.605.refs_1_.refs_2_.refs_3_), channel_id=1, source_target_pairs={{0,4},{1,5},{2,6},{3,7},{4,0},{5,1},{6,2},{7,3},{8,12},{9,13},{10,... | collective-permute-start | bytes 6291464 | tf_op jit(solution)/shard_map/ppermute | solution.py:682
  204.5 23.0 %collective-permute-start.12 = (bf16[256,2048]{1,0:T(8,128)(2,1)S(1)}, bf16[256,2048]{1,0:T(8,128)(2,1)S(1)}, u32[]{:S(2)}, u32[]{:S(2)}) collective-permute-start(bf16[256,2048]{1,0:T(8,128)(2,1)S(1)} %get-tuple-element.100.refs_1_), channel_id=1, source_target_pairs={{0,2},{1,9},{2,0},{3,11},{4,6},{5,13},{6,4},{7,15},{8,10},{9,1},{1... | collective-permute-start | bytes 3145736 | tf_op jit(solution)/shard_map/ppermute | solution.py:682
  232.0 90.7 %all-to-all-start.4 = ((bf16[4,256,1024]{2,1,0:T(8,128)(2,1)}), bf16[4,256,1024]{2,1,0:T(8,128)(2,1)}, u32[]{:S(2)}, u32[]{:S(2)}) async-start(bf16[4,256,1024]{2,1,0:T(8,128)(2,1)} %bitcast.49), calls=%async_computation.4 | async-start | bytes 4194304 | tf_op jit(solution)/shard_map/all_to_all | solution.py:700
  237.3 59.8 %collective-permute-start.16 = (bf16[1024,1024]{1,0:T(8,128)(2,1)S(1)}, bf16[1024,1024]{1,0:T(8,128)(2,1)S(1)}, u32[]{:S(2)}, u32[]{:S(2)}) collective-permute-start(bf16[1024,1024]{1,0:T(8,128)(2,1)S(1)} %shard_map.607.refs_4_.refs_1_.refs_5_), channel_id=1, source_target_pairs={{0,4},{1,5},{2,6},{3,7},{4,0},{5,1},{6,2},{7,3},{8,12},{9,13},{10,... | collective-permute-start | bytes 6291464 | tf_op jit(solution)/shard_map/ppermute | solution.py:682
  238.9 44.8 %collective-permute-start.13 = (bf16[256,2048]{1,0:T(8,128)(2,1)}, bf16[256,2048]{1,0:T(8,128)(2,1)S(1)}, u32[]{:S(2)}, u32[]{:S(2)}) collective-permute-start(bf16[256,2048]{1,0:T(8,128)(2,1)} %copy-done.90), channel_id=1, source_target_pairs={{0,8},{1,3},{2,10},{3,1},{4,12},{5,7},{6,14},{7,5},{8,0},{9,11},{1... | collective-permute-start | bytes 3145736 | tf_op jit(solution)/shard_map/ppermute | solution.py:682
  240.9 56.2 %collective-permute-start.14 = (bf16[256,2048]{1,0:T(8,128)(2,1)S(1)}, bf16[256,2048]{1,0:T(8,128)(2,1)S(1)}, u32[]{:S(2)}, u32[]{:S(2)}) collective-permute-start(bf16[256,2048]{1,0:T(8,128)(2,1)S(1)} %collective-permute-done.12.refs_1_.refs_2_), channel_id=1, source_target_pairs={{0,8},{1,3},{2,10},{3,1},{4,12},{5,7},{6,14},{7,5},{8,0},{9,11},{1... | collective-permute-start | bytes 3145736 | tf_op jit(solution)/shard_map/ppermute | solution.py:682
  241.0 61.9 %collective-permute-start.18 = (bf16[256,2048]{1,0:T(8,128)(2,1)}, bf16[256,2048]{1,0:T(8,128)(2,1)S(1)}, u32[]{:S(2)}, u32[]{:S(2)}) collective-permute-start(bf16[256,2048]{1,0:T(8,128)(2,1)} %copy-done.90), channel_id=1, source_target_pairs={{0,1},{1,0},{2,3},{3,2},{4,5},{5,4},{6,7},{7,6},{8,9},{9,8},{10,11... | collective-permute-start | bytes 3145736 | tf_op jit(solution)/shard_map/ppermute | solution.py:682
  241.0 61.9 %collective-permute-start.19 = (bf16[256,2048]{1,0:T(8,128)(2,1)S(1)}, bf16[256,2048]{1,0:T(8,128)(2,1)S(1)}, u32[]{:S(2)}, u32[]{:S(2)}) collective-permute-start(bf16[256,2048]{1,0:T(8,128)(2,1)S(1)} %collective-permute-done.12.refs_1_.refs_2_), channel_id=1, source_target_pairs={{0,1},{1,0},{2,3},{3,2},{4,5},{5,4},{6,7},{7,6},{8,9},{9,8},{10,11... | collective-permute-start | bytes 3145736 | tf_op jit(solution)/shard_map/ppermute | solution.py:682
  283.7 19.2 %collective-permute-start.20 = (bf16[256,2048]{1,0:T(8,128)(2,1)S(1)}, bf16[256,2048]{1,0:T(8,128)(2,1)S(1)}, u32[]{:S(2)}, u32[]{:S(2)}) collective-permute-start(bf16[256,2048]{1,0:T(8,128)(2,1)S(1)} %collective-permute-done.13.refs_3_), channel_id=1, source_target_pairs={{0,1},{1,0},{2,3},{3,2},{4,5},{5,4},{6,7},{7,6},{8,9},{9,8},{10,11... | collective-permute-start | bytes 3145736 | tf_op jit(solution)/shard_map/ppermute | solution.py:682
  297.1 5.7 collective-permute-start.21
  324.1 48.6 %collective-permute-start.17 = (bf16[1024,1024]{1,0:T(8,128)(2,1)}, bf16[1024,1024]{1,0:T(8,128)(2,1)S(1)}, u32[]{:S(2)}, u32[]{:S(2)}) collective-permute-start(bf16[1024,1024]{1,0:T(8,128)(2,1)} %shard_map.611.refs_6_.refs_2_), channel_id=1, source_target_pairs={{0,4},{1,5},{2,6},{3,7},{4,0},{5,1},{6,2},{7,3},{8,12},{9,13},{10,... | collective-permute-start | bytes 6291464 | tf_op jit(solution)/shard_map/ppermute | solution.py:682
  359.1 58.6 %collective-permute-start.27 = (bf16[1024,1024]{1,0:T(8,128)(2,1)S(1)}, bf16[1024,1024]{1,0:T(8,128)(2,1)S(1)}, u32[]{:S(2)}, u32[]{:S(2)}) collective-permute-start(bf16[1024,1024]{1,0:T(8,128)(2,1)S(1)} %get-tuple-element.122), channel_id=1, source_target_pairs={{0,4},{1,5},{2,6},{3,7},{4,0},{5,1},{6,2},{7,3},{8,12},{9,13},{10,... | collective-permute-start | bytes 6291464 | tf_op jit(solution)/shard_map/ppermute | solution.py:682
  414.7 47.6 %collective-permute-start.22 = (bf16[1024,1024]{1,0:T(8,128)(2,1)}, bf16[1024,1024]{1,0:T(8,128)(2,1)}, u32[]{:S(2)}, u32[]{:S(2)}) collective-permute-start(bf16[1024,1024]{1,0:T(8,128)(2,1)} %get-tuple-element.115), channel_id=1, source_target_pairs={{0,4},{1,5},{2,6},{3,7},{4,0},{5,1},{6,2},{7,3},{8,12},{9,13},{10,... | collective-permute-start | bytes 6291464 | tf_op jit(solution)/shard_map/ppermute | solution.py:682
  421.6 80.4 %all-to-all-start.5 = ((bf16[4,256,1024]{2,1,0:T(8,128)(2,1)}), bf16[4,256,1024]{2,1,0:T(8,128)(2,1)S(1)}, u32[]{:S(2)}, u32[]{:S(2)}) async-start(bf16[4,256,1024]{2,1,0:T(8,128)(2,1)} %bitcast.66), calls=%async_computation.5 | async-start | bytes 4194304 | tf_op jit(solution)/shard_map/all_to_all | solution.py:700
  457.0 21.2 %collective-permute-start.24 = (bf16[256,2048]{1,0:T(8,128)(2,1)S(1)}, bf16[256,2048]{1,0:T(8,128)(2,1)S(1)}, u32[]{:S(2)}, u32[]{:S(2)}) collective-permute-start(bf16[256,2048]{1,0:T(8,128)(2,1)S(1)} %get-tuple-element.119), channel_id=1, source_target_pairs={{0,1},{1,0},{2,3},{3,2},{4,5},{5,4},{6,7},{7,6},{8,9},{9,8},{10,11... | collective-permute-start | bytes 3145736 | tf_op jit(solution)/shard_map/ppermute | solution.py:682
  457.1 23.2 %collective-permute-start.23 = (bf16[256,2048]{1,0:T(8,128)(2,1)S(1)}, bf16[256,2048]{1,0:T(8,128)(2,1)S(1)}, u32[]{:S(2)}, u32[]{:S(2)}) collective-permute-start(bf16[256,2048]{1,0:T(8,128)(2,1)S(1)} %get-tuple-element.117), channel_id=1, source_target_pairs={{0,1},{1,0},{2,3},{3,2},{4,5},{5,4},{6,7},{7,6},{8,9},{9,8},{10,11... | collective-permute-start | bytes 3145736 | tf_op jit(solution)/shard_map/ppermute | solution.py:682
  457.6 43.5 %collective-permute-start.25 = (bf16[256,2048]{1,0:T(8,128)(2,1)S(1)}, bf16[256,2048]{1,0:T(8,128)(2,1)S(1)}, u32[]{:S(2)}, u32[]{:S(2)}) collective-permute-start(bf16[256,2048]{1,0:T(8,128)(2,1)S(1)} %get-tuple-element.121), channel_id=1, source_target_pairs={{0,1},{1,0},{2,3},{3,2},{4,5},{5,4},{6,7},{7,6},{8,9},{9,8},{10,11... | collective-permute-start | bytes 3145736 | tf_op jit(solution)/shard_map/ppermute | solution.py:682
  478.5 23.6 %collective-permute-start.26 = (bf16[256,2048]{1,0:T(8,128)(2,1)S(1)}, bf16[256,2048]{1,0:T(8,128)(2,1)}, u32[]{:S(2)}, u32[]{:S(2)}) collective-permute-start(bf16[256,2048]{1,0:T(8,128)(2,1)S(1)} %shard_map.622.refs_5_), channel_id=1, source_target_pairs={{0,8},{1,3},{2,10},{3,1},{4,12},{5,7},{6,14},{7,5},{8,0},{9,11},{1... | collective-permute-start | bytes 3145736 | tf_op jit(solution)/shard_map/ppermute | solution.py:682
  478.8 46.9 %collective-permute-start.32 = (bf16[1024,1024]{1,0:T(8,128)(2,1)}, bf16[1024,1024]{1,0:T(8,128)(2,1)}, u32[]{:S(2)}, u32[]{:S(2)}) collective-permute-start(bf16[1024,1024]{1,0:T(8,128)(2,1)} %get-tuple-element.124), channel_id=1, source_target_pairs={{0,4},{1,5},{2,6},{3,7},{4,0},{5,1},{6,2},{7,3},{8,12},{9,13},{10,... | collective-permute-start | bytes 6291464 | tf_op jit(solution)/shard_map/ppermute | solution.py:682
  481.9 35.1 %collective-permute-start.29 = (bf16[256,2048]{1,0:T(8,128)(2,1)}, bf16[256,2048]{1,0:T(8,128)(2,1)}, u32[]{:S(2)}, u32[]{:S(2)}) collective-permute-start(bf16[256,2048]{1,0:T(8,128)(2,1)} %get-tuple-element.114.refs_7_), channel_id=1, source_target_pairs={{0,1},{1,0},{2,3},{3,2},{4,5},{5,4},{6,7},{7,6},{8,9},{9,8},{10,11... | collective-permute-start | bytes 3145736 | tf_op jit(solution)/shard_map/ppermute | solution.py:682
  490.7 35.0 %collective-permute-start.30 = (bf16[256,2048]{1,0:T(8,128)(2,1)}, bf16[256,2048]{1,0:T(8,128)(2,1)}, u32[]{:S(2)}, u32[]{:S(2)}) collective-permute-start(bf16[256,2048]{1,0:T(8,128)(2,1)} %shard_map.621.refs_4_), channel_id=1, source_target_pairs={{0,8},{1,3},{2,10},{3,1},{4,12},{5,7},{6,14},{7,5},{8,0},{9,11},{1... | collective-permute-start | bytes 3145736 | tf_op jit(solution)/shard_map/ppermute | solution.py:682
  508.1 17.6 %collective-permute-start.31 = (bf16[256,2048]{1,0:T(8,128)(2,1)S(1)}, bf16[256,2048]{1,0:T(8,128)(2,1)}, u32[]{:S(2)}, u32[]{:S(2)}) collective-permute-start(bf16[256,2048]{1,0:T(8,128)(2,1)S(1)} %shard_map.626.refs_1_.refs_2_), channel_id=1, source_target_pairs={{0,2},{1,9},{2,0},{3,11},{4,6},{5,13},{6,4},{7,15},{8,10},{9,1},{1... | collective-permute-start | bytes 3145736 | tf_op jit(solution)/shard_map/ppermute | solution.py:682
  513.2 52.2 %all-to-all-start.6 = ((bf16[4,256,1024]{2,1,0:T(8,128)(2,1)}), bf16[4,256,1024]{2,1,0:T(8,128)(2,1)S(1)}, u32[]{:S(2)}, u32[]{:S(2)}) async-start(bf16[4,256,1024]{2,1,0:T(8,128)(2,1)} %bitcast.65), calls=%async_computation.6 | async-start | bytes 4194304 | tf_op jit(solution)/shard_map/all_to_all | solution.py:700
  532.5 23.8 %collective-permute-start.33 = (bf16[256,2048]{1,0:T(8,128)(2,1)S(1)}, bf16[256,2048]{1,0:T(8,128)(2,1)S(1)}, u32[]{:S(2)}, u32[]{:S(2)}) collective-permute-start(bf16[256,2048]{1,0:T(8,128)(2,1)S(1)} %get-tuple-element.125.refs_1_), channel_id=1, source_target_pairs={{0,2},{1,3},{2,0},{3,1},{4,6},{5,7},{6,4},{7,5},{8,10},{9,11},{10,... | collective-permute-start | bytes 3145736 | tf_op jit(solution)/shard_map/ppermute | solution.py:682
  533.9 22.4 %collective-permute-start.34 = (bf16[256,2048]{1,0:T(8,128)(2,1)S(1)}, bf16[256,2048]{1,0:T(8,128)(2,1)S(1)}, u32[]{:S(2)}, u32[]{:S(2)}) collective-permute-start(bf16[256,2048]{1,0:T(8,128)(2,1)S(1)} %get-tuple-element.125.refs_1_), channel_id=1, source_target_pairs={{0,1},{1,0},{2,3},{3,2},{4,5},{5,4},{6,7},{7,6},{8,9},{9,8},{10,11... | collective-permute-start | bytes 3145736 | tf_op jit(solution)/shard_map/ppermute | solution.py:682
  556.3 2.7 collective-permute-start.35
  571.1 57.0 %all-to-all-start.7 = ((bf16[4,256,1024]{2,1,0:T(8,128)(2,1)}), bf16[4,256,1024]{2,1,0:T(8,128)(2,1)S(1)}, u32[]{:S(2)}, u32[]{:S(2)}) async-start(bf16[4,256,1024]{2,1,0:T(8,128)(2,1)} %bitcast.67), calls=%async_computation.7 | async-start | bytes 4194304 | tf_op jit(solution)/shard_map/all_to_all | solution.py:700
  574.7 65.0 %collective-permute-start.28 = (bf16[1024,2048]{1,0:T(8,128)(2,1)}, bf16[1024,2048]{1,0:T(8,128)(2,1)}, u32[]{:S(2)}, u32[]{:S(2)}) collective-permute-start(bf16[1024,2048]{1,0:T(8,128)(2,1)} %shard_map.627), channel_id=1, source_target_pairs={{0,1},{1,0},{2,3},{3,2},{4,5},{5,4},{6,7},{7,6},{8,9},{9,8},{10,11... | collective-permute-start | bytes 12582920 | tf_op jit(solution)/shard_map/ppermute | solution.py:682
  584.2 30.0 %collective-permute-start.37 = (bf16[1024,512]{1,0:T(8,128)(2,1)S(1)}, bf16[1024,512]{1,0:T(8,128)(2,1)S(1)}, u32[]{:S(2)}, u32[]{:S(2)}) collective-permute-start(bf16[1024,512]{1,0:T(8,128)(2,1)S(1)} %get-tuple-element.128), channel_id=1, source_target_pairs={{0,4},{1,5},{2,6},{3,7},{4,0},{5,1},{6,2},{7,3},{8,12},{9,13},{10,... | collective-permute-start | bytes 3145736 | tf_op jit(solution)/shard_map/ppermute | solution.py:682
  612.7 47.0 %collective-permute-start.41 = (bf16[1024,1024]{1,0:T(8,128)(2,1)}, bf16[1024,1024]{1,0:T(8,128)(2,1)}, u32[]{:S(2)}, u32[]{:S(2)}) collective-permute-start(bf16[1024,1024]{1,0:T(8,128)(2,1)} %get-tuple-element.136), channel_id=1, source_target_pairs={{0,4},{1,5},{2,6},{3,7},{4,0},{5,1},{6,2},{7,3},{8,12},{9,13},{10,... | collective-permute-start | bytes 6291464 | tf_op jit(solution)/shard_map/ppermute | solution.py:682
  634.7 29.9 %all-to-all-start.8 = ((bf16[4,256,512]{2,1,0:T(8,128)(2,1)}), bf16[4,256,512]{2,1,0:T(8,128)(2,1)S(1)}, u32[]{:S(2)}, u32[]{:S(2)}) async-start(bf16[4,256,512]{2,1,0:T(8,128)(2,1)} %bitcast.26), calls=%async_computation.8 | async-start | bytes 2097152 | tf_op jit(solution)/shard_map/all_to_all | solution.py:700
  644.0 50.9 %collective-permute-start.36 = (bf16[512,2048]{1,0:T(8,128)(2,1)}, bf16[512,2048]{1,0:T(8,128)(2,1)}, u32[]{:S(2)}, u32[]{:S(2)}) collective-permute-start(bf16[512,2048]{1,0:T(8,128)(2,1)} %shard_map.633), channel_id=1, source_target_pairs={{0,8},{1,3},{2,10},{3,1},{4,12},{5,7},{6,14},{7,5},{8,0},{9,11},{1... | collective-permute-start | bytes 6291464 | tf_op jit(solution)/shard_map/ppermute | solution.py:682
  668.9 61.3 %all-to-all-start.9 = ((bf16[4,256,1024]{2,1,0:T(8,128)(2,1)}), bf16[4,256,1024]{2,1,0:T(8,128)(2,1)}, u32[]{:S(2)}, u32[]{:S(2)}) async-start(bf16[4,256,1024]{2,1,0:T(8,128)(2,1)} %bitcast.64), calls=%async_computation.9 | async-start | bytes 4194304 | tf_op jit(solution)/shard_map/all_to_all | solution.py:700
  673.3 24.3 %collective-permute-start.40 = (bf16[256,2048]{1,0:T(8,128)(2,1)}, bf16[256,2048]{1,0:T(8,128)(2,1)S(1)}, u32[]{:S(2)}, u32[]{:S(2)}) collective-permute-start(bf16[256,2048]{1,0:T(8,128)(2,1)} %get-tuple-element.135), channel_id=1, source_target_pairs={{0,1},{1,0},{2,3},{3,2},{4,5},{5,4},{6,7},{7,6},{8,9},{9,8},{10,11... | collective-permute-start | bytes 3145736 | tf_op jit(solution)/shard_map/ppermute | solution.py:682
  673.4 30.2 %collective-permute-start.39 = (bf16[256,2048]{1,0:T(8,128)(2,1)}, bf16[256,2048]{1,0:T(8,128)(2,1)S(1)}, u32[]{:S(2)}, u32[]{:S(2)}) collective-permute-start(bf16[256,2048]{1,0:T(8,128)(2,1)} %get-tuple-element.133), channel_id=1, source_target_pairs={{0,1},{1,0},{2,3},{3,2},{4,5},{5,4},{6,7},{7,6},{8,9},{9,8},{10,11... | collective-permute-start | bytes 3145736 | tf_op jit(solution)/shard_map/ppermute | solution.py:682
  698.1 14.9 %collective-permute-start.42 = (bf16[256,2048]{1,0:T(8,128)(2,1)S(1)}, bf16[256,2048]{1,0:T(8,128)(2,1)S(1)}, u32[]{:S(2)}, u32[]{:S(2)}) collective-permute-start(bf16[256,2048]{1,0:T(8,128)(2,1)S(1)} %shard_map.639.refs_1_), channel_id=1, source_target_pairs={{0,2},{1,3},{2,0},{3,1},{4,6},{5,7},{6,4},{7,5},{8,10},{9,11},{10,... | collective-permute-start | bytes 3145736 | tf_op jit(solution)/shard_map/ppermute | solution.py:682
  699.5 44.5 %collective-permute-start.38 = (bf16[256,2048]{1,0:T(8,128)(2,1)S(1)}, bf16[256,2048]{1,0:T(8,128)(2,1)}, u32[]{:S(2)}, u32[]{:S(2)}) collective-permute-start(bf16[256,2048]{1,0:T(8,128)(2,1)S(1)} %shard_map.638.refs_2_), channel_id=1, source_target_pairs={{0,2},{1,9},{2,0},{3,11},{4,6},{5,13},{6,4},{7,15},{8,10},{9,1},{1... | collective-permute-start | bytes 3145736 | tf_op jit(solution)/shard_map/ppermute | solution.py:682
  717.8 1.2 collective-permute-start.43
  719.1 5.4 collective-permute-start.44
  724.5 4.6 collective-permute-start.45
  729.2 3.7 collective-permute-start.46
  732.6 1.2 collective-permute-start.48
  732.9 17.2 %collective-permute-start.47 = (f32[32,128]{1,0:T(8,128)S(1)}, f32[32,128]{1,0:T(8,128)S(1)}, u32[]{:S(2)}, u32[]{:S(2)}) collective-permute-start(f32[32,128]{1,0:T(8,128)S(1)} %add.226), channel_id=1, source_target_pairs={{0,4},{1,5},{2,6},{3,7},{4,0},{5,1},{6,2},{7,3},{8,12},{9,13},{10,... | collective-permute-start | bytes 49160 | tf_op jit(solution)/shard_map/ppermute | solution.py:682
  733.9 3.6 collective-permute-start.49
  737.5 4.5 collective-permute-start.50
  742.0 8.2 %collective-permute-start.51 = (f32[8,128]{1,0:T(8,128)S(1)}, f32[8,128]{1,0:T(8,128)S(1)}, u32[]{:S(2)}, u32[]{:S(2)}) collective-permute-start(f32[8,128]{1,0:T(8,128)S(1)} %add.234), channel_id=1, source_target_pairs={{0,8},{1,9},{2,10},{3,11},{4,12},{5,13},{6,14},{7,15},{8,0},{9,1},... | collective-permute-start | bytes 12296 | tf_op jit(solution)/shard_map/ppermute | solution.py:682
  750.2 3.7 collective-permute-start.52
  (118 other events, 606.2 us)

commit v3 on v2

--- a/solution.py
+++ b/solution.py
@@ -809,7 +809,7 @@
     cotangent = jnp.where(row_pos[:, None] < length, out_grad, jnp.zeros_like(out_grad))
     grad_pair = swap(cotangent, PAIR, 0)
     attn_input = gather_slot(normed_attn, pin(slot_other, grad_pair))
-    out_rows = trade_far(pin(out_blocks, qkv_rows, attn_input))
+    out_rows = trade_far(pin(out_blocks, qkv_rows, slot_other))
     full_out = (out_rows, cross(out_rows))
     grad_other, grad_both = swap(cotangent, 0, 2), swap(grad_pair, 0, 2)
     gate_rows = trade_far(pin(gate_blocks, out_rows))
@@ -848,8 +848,10 @@
     full_up = (up_rows, up_crossed)
     both = swap_two(first)
     mlp_mine = arrange([normed_mlp, first, second, pin(both, up_crossed)], range(4))
-    mlp_near = arrange([swap(one, 0, 1) for one in (normed_mlp, first, second, both)], range(4))
-    down_rows = trade_far(pin(down_blocks, up_rows, first))
+    near_blocks = [swap(one, 0, 1) for one in (normed_mlp, first, second)]
+    near_blocks.append(swap(pin(both, up_crossed), 0, 1))
+    mlp_near = arrange(near_blocks, range(4))
+    down_rows = trade_far(pin(down_blocks, up_rows, both, second))
     hid_mine, upp_mine, gatep_mine = mlp_forward(mlp_mine, full_gate, full_up)
     down_rows = settle(pin(down_rows, hid_mine))
     full_down = (down_rows, cross(down_rows))

time: 792 us -> 765 us (0.966)
  waiting for transfers between devices: 305 us -> 273 us
  local copies, waits for them, and re-layouts: 80.4 us -> 70.5 us
    ppermute x53, waiting for transfers between devices: 278 us -> 209 us  [swap(): return lax.ppermute(settle(value), AXES, pairs)]
    all_to_all x10, waiting for transfers between devices: 26.4 us -> 63.7 us  [trade_far(): lax.all_to_all(settle(blocks), 'fsdp', 0, 0, axis_index_groups=groups, ti...]
    unnamed x241 -> x225, local copies, waits for them, and re-layouts: 79.8 us -> 69.9 us
    ppermute x53, starting transfers between devices: 40.8 us -> 48.9 us  [swap(): return lax.ppermute(settle(value), AXES, pairs)]
    pallas_call x59 -> x60, Pallas kernels: 279 us -> 284 us  [call_kernel(): pl.pallas_call(body, grid_spec=spec, out_shape=out_shape, input_output_al...]
  transfers between devices with their start and end apart: 63 -> 63, of which waited for: 29 -> 31; matrix products, arithmetic and copies ran while one was open for 1% -> 1% of each run, Pallas kernels for 35% -> 37%
where the time goes in v3:
time: 765 us; the launch traced here: 754 us
  Pallas kernels  284 us (37%)
  waiting for transfers between devices  273 us (36%)
  starting transfers between devices  94.5 us (12%)
  local copies, waits for them, and re-layouts  70.5 us (9%)
  other arithmetic  26.2 us (3%)
    pallas_call x60, Pallas kernels, call_kernel(): pl.pallas_call(body, grid_spec=spec, out_shape=out_shape, input_output_al...  284 us
    ppermute x53, waiting for transfers between devices, swap(): return lax.ppermute(settle(value), AXES, pairs)  209 us
    unnamed x225, local copies, waits for them, and re-layouts  69.9 us
    all_to_all x10, waiting for transfers between devices, trade_far(): lax.all_to_all(settle(blocks), 'fsdp', 0, 0, axis_index_groups=groups, ti...  63.7 us
    ppermute x53, starting transfers between devices, swap(): return lax.ppermute(settle(value), AXES, pairs)  48.9 us
    all_to_all x10, starting transfers between devices, trade_far(): lax.all_to_all(settle(blocks), 'fsdp', 0, 0, axis_index_groups=groups, ti...  45.6 us
    mul x7, other arithmetic, adam_step(): -LEARN_RATE  19.9 us
  transfers between devices with their start and end apart: 63, of which 31 were waited for; matrix products, arithmetic and copies ran while one was open for 1% of the time, Pallas kernels for 37%

profile of v3, /device:TPU:0, one launch (start us, length us, event | category | flops | bytes accessed | tf_op | source)
XLA Modules:
  0.0 754.3 jit_solution(3691716663840130575)
XLA Ops:
  6.1 6.3 all-to-all-start
  19.0 41.8 %all-to-all-done = bf16[4,256,1024]{2,1,0:T(8,128)(2,1)S(1)} async-done(((bf16[4,256,1024]{2,1,0:T(8,128)(2,1)}), bf16[4,256,1024]{2,1,0:T(8,128)(2,1)S(1)}, u32[]{:S(2)}, u32[]{:S(2)}) %all-to-all-start) | async-done | bytes 2097184 | tf_op jit(solution)/shard_map/all_to_all | solution.py:700
  66.0 3.5 all-to-all-start.1
  78.0 5.2 shard_map.591.refs_1_
  83.2 11.2 %all-to-all-done.1 = bf16[4,256,512]{2,1,0:T(8,128)(2,1)S(1)} async-done(((bf16[4,256,512]{2,1,0:T(8,128)(2,1)}), bf16[4,256,512]{2,1,0:T(8,128)(2,1)S(1)}, u32[]{:S(2)}, u32[]{:S(2)}) %all-to-all-start.1) | async-done | bytes 1048608 | tf_op jit(solution)/shard_map/all_to_all | solution.py:700
  97.7 4.5 all-to-all-start.2
  102.1 5.3 collective-permute-done.4.refs_3_
  109.5 8.7 %shard_map.595.refs_1_.refs_2_.refs_3_.refs_5_.refs_6_.refs_7_ = bf16[1024,1024]{1,0:T(8,128)(2,1)S(1)} custom-call(s32[1]{0:T(128)} %bitcast.refs_0_, bf16[1024,2048]{1,0:T(8,128)(2,1)} %shard_map.591.refs_1_, bf16[1024,1024]{1,0:T(8,128)(2,1)} %bitcast.44, bf16[1024,1024]{1,0:T(8,128)(2,1)} %collective-permute-done.4.refs_3_, f32[1024,128]{1,0:T(8,128)S(1)} %copy-done.43, ...), custom_call_target="tpu_custom_call" | custom-call | flops 1 | bytes 1 | tf_op jit(solution)/shard_map/pallas_call | solution.py:96
  119.5 5.3 shard_map.598.refs_5_.refs_1_
  127.1 7.3 shard_map.597.refs_1_.refs_2_
  134.4 16.1 %collective-permute-done.5.refs_3_ = bf16[1024,512]{1,0:T(8,128)(2,1)S(1)} collective-permute-done((bf16[1024,512]{1,0:T(8,128)(2,1)S(1)}, bf16[1024,512]{1,0:T(8,128)(2,1)S(1)}, u32[]{:S(2)}, u32[]{:S(2)}) %collective-permute-start.5) | collective-permute-done | bytes 1048608 | tf_op jit(solution)/shard_map/ppermute | solution.py:682
  151.5 6.3 shard_map.599
  159.3 3.6 collective-permute-done.9.refs_1_
  166.1 3.8 all-to-all-start.3
  174.9 13.8 %collective-permute-done.10.refs_3_ = bf16[256,2048]{1,0:T(8,128)(2,1)} collective-permute-done((bf16[256,2048]{1,0:T(8,128)(2,1)S(1)}, bf16[256,2048]{1,0:T(8,128)(2,1)}, u32[]{:S(2)}, u32[]{:S(2)}) %collective-permute-start.10) | collective-permute-done | bytes 1048608 | tf_op jit(solution)/shard_map/ppermute | solution.py:682
  188.6 4.2 shard_map.602
  194.7 22.9 %collective-permute-done.12.refs_1_.refs_2_ = bf16[256,2048]{1,0:T(8,128)(2,1)} collective-permute-done((bf16[256,2048]{1,0:T(8,128)(2,1)}, bf16[256,2048]{1,0:T(8,128)(2,1)}, u32[]{:S(2)}, u32[]{:S(2)}) %collective-permute-start.12) | collective-permute-done | bytes 1048608 | tf_op jit(solution)/shard_map/ppermute | solution.py:682
  225.2 3.4 collective-permute-done.13.refs_3_
  228.6 11.1 %collective-permute-done.14.refs_4_.refs_2_.refs_0_ = bf16[256,2048]{1,0:T(8,128)(2,1)S(1)} collective-permute-done((bf16[256,2048]{1,0:T(8,128)(2,1)}, bf16[256,2048]{1,0:T(8,128)(2,1)S(1)}, u32[]{:S(2)}, u32[]{:S(2)}) %collective-permute-start.14) | collective-permute-done | bytes 1048608 | tf_op jit(solution)/shard_map/ppermute | solution.py:682
  241.1 4.7 all-to-all-start.4
  246.9 18.7 %collective-permute-done.16.refs_5_.refs_1_.refs_6_ = bf16[1024,1024]{1,0:T(8,128)(2,1)} collective-permute-done((bf16[1024,1024]{1,0:T(8,128)(2,1)S(1)}, bf16[1024,1024]{1,0:T(8,128)(2,1)}, u32[]{:S(2)}, u32[]{:S(2)}) %collective-permute-start.16) | collective-permute-done | bytes 2097184 | tf_op jit(solution)/shard_map/ppermute | solution.py:682
  265.6 4.9 shard_map.608.refs_1_
  270.5 6.6 collective-permute-start.19
  277.0 15.5 %shard_map.609 = (bf16[1024,1024]{1,0:T(8,128)(2,1)S(1)}, bf16[1024,1024]{1,0:T(8,128)(2,1)S(1)}, bf16[1024,1024]{1,0:T(8,128)(2,1)}) custom-call(s32[1]{0:T(128)} %bitcast.refs_0_, bf16[1024,2048]{1,0:T(8,128)(2,1)} %shard_map.608.refs_1_, bf16[1024,1024]{1,0:T(8,128)(2,1)} %shard_map.605.refs_1_.refs_2_.refs_3_, bf16[1024,1024]{1,0:T(8,128)(2,1)} %copy-done.3, ...), custom_call_target="tpu_custom_call" | custom-call | flops 1 | bytes 1 | tf_op jit(solution)/shard_map/pallas_call | solution.py:96
  293.9 3.1 shard_map.613.refs_1_.refs_2_
  298.9 15.5 %shard_map.614 = (bf16[1024,1024]{1,0:T(8,128)(2,1)S(1)}, bf16[1024,1024]{1,0:T(8,128)(2,1)S(1)}, bf16[1024,1024]{1,0:T(8,128)(2,1)}) custom-call(s32[1]{0:T(128)} %bitcast.refs_0_, bf16[1024,2048]{1,0:T(8,128)(2,1)} %shard_map.613.refs_1_.refs_2_, bf16[1024,1024]{1,0:T(8,128)(2,1)} %shard_map.605.refs_1_.refs_2_.refs_3_, bf16[1024,1024]{1,0:T(8,128)(2,1)} %copy-done.3, ...), custom_call_target="tpu_custom_call" | custom-call | flops 1 | bytes 1 | tf_op jit(solution)/shard_map/pallas_call | solution.py:96
  317.0 13.9 %shard_map.615 = (bf16[1024,1024]{1,0:T(8,128)(2,1)S(1)}, bf16[1024,1024]{1,0:T(8,128)(2,1)S(1)}) custom-call(s32[8]{0:T(128)S(1)} %pad_add_fusion.3.refs_0_, bf16[1024,2048]{1,0:T(8,128)(2,1)} %shard_map.598.refs_5_.refs_1_, bf16[1024,2048]{1,0:T(8,128)(2,1)} %collective-permute-done.11.refs_6_.refs_2_.refs_1_, bf16[1024,1024]{1,0:T(8,128)(2,1)} %copy-done.16, ...), custom_call_target="tpu_custom_call" | custom-call | flops 1 | bytes 1 | tf_op jit(solution)/shard_map/pallas_call | solution.py:96
  332.5 13.1 %collective-permute-done.17.refs_3_ = bf16[1024,1024]{1,0:T(8,128)(2,1)S(1)} collective-permute-done((bf16[1024,1024]{1,0:T(8,128)(2,1)}, bf16[1024,1024]{1,0:T(8,128)(2,1)S(1)}, u32[]{:S(2)}, u32[]{:S(2)}) %collective-permute-start.17) | collective-permute-done | bytes 2097184 | tf_op jit(solution)/shard_map/ppermute | solution.py:682
  347.0 9.5 %shard_map.616 = (bf16[1024,1024]{1,0:T(8,128)(2,1)S(1)}, bf16[1024,1024]{1,0:T(8,128)(2,1)S(1)}) custom-call(s32[1]{0:T(128)} %bitcast.refs_0_, bf16[1024,2048]{1,0:T(8,128)(2,1)} %collective-permute-done.11.refs_6_.refs_2_.refs_1_, bf16[1024,1024]{1,0:T(8,128)(2,1)} %shard_map.611.refs_6_.refs_2_, bf16[1024,1024]{1,0:T(8,128)(2,1)} %copy-done.90, ...), custom_call_target="tpu_custom_call" | custom-call | flops 1 | bytes 1 | tf_op jit(solution)/shard_map/pallas_call | solution.py:96
  359.1 9.5 %shard_map.617 = (bf16[1024,1024]{1,0:T(8,128)(2,1)S(1)}, bf16[1024,1024]{1,0:T(8,128)(2,1)S(1)}) custom-call(s32[1]{0:T(128)} %bitcast.refs_0_, bf16[1024,2048]{1,0:T(8,128)(2,1)} %shard_map.598.refs_5_.refs_1_, bf16[1024,1024]{1,0:T(8,128)(2,1)} %shard_map.611.refs_6_.refs_2_, bf16[1024,1024]{1,0:T(8,128)(2,1)} %copy-done.90, ...), custom_call_target="tpu_custom_call" | custom-call | flops 1 | bytes 1 | tf_op jit(solution)/shard_map/pallas_call | solution.py:96
  371.2 14.8 %shard_map.618 = (bf16[1024,1024]{1,0:T(8,128)(2,1)}, bf16[1024,1024]{1,0:T(8,128)(2,1)S(1)}) custom-call(s32[8]{0:T(128)S(1)} %pad_add_fusion.3.refs_0_, bf16[1024,2048]{1,0:T(8,128)(2,1)} %shard_map.608.refs_1_, bf16[1024,2048]{1,0:T(8,128)(2,1)} %shard_map.613.refs_1_.refs_2_, bf16[1024,1024]{1,0:T(8,128)(2,1)} %copy-done.37, bf16[1024,1024]{1,0:T(8,128)(2,1)} %copy-done.26), custom_call_target="tpu_custom_call" | custom-call | flops 1 | bytes 1 | tf_op jit(solution)/shard_map/pallas_call | solution.py:96
  394.5 4.7 all-to-all-start.5
  399.2 14.8 %shard_map.619 = (bf16[1024,1024]{1,0:T(8,128)(2,1)}, bf16[1024,1024]{1,0:T(8,128)(2,1)S(1)}) custom-call(s32[8]{0:T(128)S(1)} %pad_add_fusion.3.refs_0_, bf16[1024,2048]{1,0:T(8,128)(2,1)} %shard_map.608.refs_1_, bf16[1024,2048]{1,0:T(8,128)(2,1)} %shard_map.613.refs_1_.refs_2_, bf16[1024,1024]{1,0:T(8,128)(2,1)} %copy-done.47, ...), custom_call_target="tpu_custom_call" | custom-call | flops 1 | bytes 1 | tf_op jit(solution)/shard_map/pallas_call | solution.py:96
  415.3 15.5 %shard_map.620 = (bf16[256,2048]{1,0:T(8,128)(2,1)}, bf16[256,2048]{1,0:T(8,128)(2,1)S(1)}, bf16[256,2048]{1,0:T(8,128)(2,1)S(1)}, bf16[256,2048]{1,0:T(8,128)(2,1)S(1)}) custom-call(s32[1]{0:T(128)} %bitcast.refs_0_, bf16[1024,1024]{1,0:T(8,128)(2,1)} %copy-done.26, bf16[1024,1024]{1,0:T(8,128)(2,1)} %copy-done.55, ...), custom_call_target="tpu_custom_call" | custom-call | flops 1 | bytes 1 | tf_op jit(solution)/shard_map/pallas_call | solution.py:96
  431.5 3.8 collective-permute-done.22.refs_8_.refs_0_
  435.3 14.9 %shard_map.621 = (bf16[256,2048]{1,0:T(8,128)(2,1)S(1)}, bf16[256,2048]{1,0:T(8,128)(2,1)S(1)}, bf16[256,2048]{1,0:T(8,128)(2,1)S(1)}, bf16[256,2048]{1,0:T(8,128)(2,1)S(1)}) custom-call(s32[1]{0:T(128)} %bitcast.refs_0_, bf16[1024,1024]{1,0:T(8,128)(2,1)} %copy-done.37, bf16[1024,1024]{1,0:T(8,128)(2,1)} %copy-done.47, ...), custom_call_target="tpu_custom_call" | custom-call | flops 1 | bytes 1 | tf_op jit(solution)/shard_map/pallas_call | solution.py:96
  456.4 8.7 %shard_map.624.refs_4_.refs_0_ = bf16[1024,2048]{1,0:T(8,128)(2,1)} custom-call(s32[1]{0:T(128)} %bitcast.refs_0_, bf16[1024,1024]{1,0:T(8,128)(2,1)S(1)} %copy-done.36, bf16[1024,1024]{1,0:T(8,128)(2,1)} %shard_map.611.refs_6_.refs_2_, bf16[1024,1024]{1,0:T(8,128)(2,1)} %copy-done.90, bf16[256,2048]{1,0:T(8,128)(2,1)} %shard_map.622.refs_4_, ...), custom_call_target="tpu_custom_call" | custom-call | flops 1 | bytes 1 | tf_op jit(solution)/shard_map/pallas_call | solution.py:96
  465.8 8.5 %shard_map.625.refs_3_.refs_0_.refs_1_ = bf16[1024,2048]{1,0:T(8,128)(2,1)} custom-call(s32[1]{0:T(128)} %bitcast.refs_0_, bf16[1024,1024]{1,0:T(8,128)(2,1)S(1)} %copy-done.17, bf16[1024,1024]{1,0:T(8,128)(2,1)} %shard_map.611.refs_6_.refs_2_, bf16[1024,1024]{1,0:T(8,128)(2,1)} %copy-done.90, bf16[1024,2048]{1,0:T(8,128)(2,1)} %shard_map.624.refs_4_.refs_0_), custom_call_target="tpu_custom_call" | custom-call | flops 1 | bytes 1 | tf_op jit(solution)/shard_map/pallas_call | solution.py:96
  486.3 5.0 all-to-all-start.6
  491.2 7.4 collective-permute-done.32.refs_7_.refs_0_
  499.9 5.6 shard_map.629
  507.0 21.0 %collective-permute-done.33.refs_2_ = bf16[256,2048]{1,0:T(8,128)(2,1)S(1)} collective-permute-done((bf16[256,2048]{1,0:T(8,128)(2,1)S(1)}, bf16[256,2048]{1,0:T(8,128)(2,1)S(1)}, u32[]{:S(2)}, u32[]{:S(2)}) %collective-permute-start.33) | collective-permute-done | bytes 1048608 | tf_op jit(solution)/shard_map/ppermute | solution.py:682
  530.7 3.1 shard_map.630.refs_1_.refs_2_
  533.7 5.6 all-to-all-done.6
  545.0 3.6 all-to-all-start.7
  549.9 7.4 shard_map.631
  558.5 14.4 %shard_map.633 = (bf16[1024,512]{1,0:T(8,128)(2,1)S(1)}, bf16[1024,256]{1,0:T(8,128)(2,1)S(1)}, bf16[1024,256]{1,0:T(8,128)(2,1)S(1)}) custom-call(s32[1]{0:T(128)} %bitcast.refs_0_, bf16[1024,2048]{1,0:T(8,128)(2,1)} %shard_map.630.refs_1_.refs_2_, bf16[1024,512]{1,0:T(8,128)(2,1)S(1)} %bitcast.54, bf16[1024,512]{1,0:T(8,128)(2,1)S(1)} %copy-done.59, ...), custom_call_target="tpu_custom_call" | custom-call | flops 1 | bytes 1 | tf_op jit(solution)/shard_map/pallas_call | solution.py:96
  574.5 10.6 %shard_map.636 = (bf16[1024,1024]{1,0:T(8,128)(2,1)}, bf16[1024,1024]{1,0:T(8,128)(2,1)S(1)}) custom-call(s32[8]{0:T(128)S(1)} %pad_add_fusion.3.refs_0_, bf16[1024,2048]{1,0:T(8,128)(2,1)} %shard_map.591.refs_1_, bf16[1024,1024]{1,0:T(8,128)(2,1)} %copy-done.91), custom_call_target="tpu_custom_call" | custom-call | flops 1 | bytes 1 | tf_op jit(solution)/shard_map/pallas_call | solution.py:96
  588.2 10.9 %shard_map.637 = (bf16[256,2048]{1,0:T(8,128)(2,1)}, bf16[256,2048]{1,0:T(8,128)(2,1)}, bf16[256,2048]{1,0:T(8,128)(2,1)S(1)}, bf16[256,2048]{1,0:T(8,128)(2,1)S(1)}) custom-call(s32[1]{0:T(128)} %bitcast.refs_0_, bf16[1024,1024]{1,0:T(8,128)(2,1)} %copy-done.91, bf16[1024,1024]{1,0:T(8,128)(2,1)} %bitcast.45, ...), custom_call_target="tpu_custom_call" | custom-call | flops 1 | bytes 1 | tf_op jit(solution)/shard_map/pallas_call | solution.py:96
  608.6 5.1 all-to-all-start.8
  613.7 4.3 shard_map.634
  620.0 13.4 %collective-permute-done.41.refs_3_.refs_0_ = bf16[1024,1024]{1,0:T(8,128)(2,1)} collective-permute-done((bf16[1024,1024]{1,0:T(8,128)(2,1)}, bf16[1024,1024]{1,0:T(8,128)(2,1)}, u32[]{:S(2)}, u32[]{:S(2)}) %collective-permute-start.41) | collective-permute-done | bytes 2097184 | tf_op jit(solution)/shard_map/ppermute | solution.py:682
  633.5 5.1 all-to-all-done.8
  638.5 3.0 shard_map.645
  642.9 4.5 all-to-all-start.9
  647.9 21.0 %collective-permute-done.36.refs_2_.refs_3_ = bf16[512,2048]{1,0:T(8,128)(2,1)} collective-permute-done((bf16[512,2048]{1,0:T(8,128)(2,1)}, bf16[512,2048]{1,0:T(8,128)(2,1)}, u32[]{:S(2)}, u32[]{:S(2)}) %collective-permute-start.36) | collective-permute-done | bytes 2097184 | tf_op jit(solution)/shard_map/ppermute | solution.py:682
  677.6 9.3 %collective-permute-done.42.refs_2_ = bf16[256,2048]{1,0:T(8,128)(2,1)S(1)} collective-permute-done((bf16[256,2048]{1,0:T(8,128)(2,1)S(1)}, bf16[256,2048]{1,0:T(8,128)(2,1)S(1)}, u32[]{:S(2)}, u32[]{:S(2)}) %collective-permute-start.42) | collective-permute-done | bytes 1048608 | tf_op jit(solution)/shard_map/ppermute | solution.py:682
  686.9 4.9 shard_map.643
  694.2 4.2 collective-permute-done.44
  711.5 4.4 collective-permute-done.50
  719.6 4.5 shard_map.644
  730.4 7.0 add_multiply_fusion.1
  737.5 4.0 add_multiply_fusion.2
  746.6 4.0 add_multiply_fusion
  (383 shorter events, 169.9 us)
Async XLA Ops:
  6.1 54.6 %all-to-all-start = ((bf16[4,256,1024]{2,1,0:T(8,128)(2,1)}), bf16[4,256,1024]{2,1,0:T(8,128)(2,1)S(1)}, u32[]{:S(2)}, u32[]{:S(2)}) async-start(bf16[4,256,1024]{2,1,0:T(8,128)(2,1)} %bitcast.59), calls=%async_computation | async-start | bytes 4194304 | tf_op jit(solution)/shard_map/all_to_all | solution.py:700
  12.5 49.8 %copy-start.67 = (f32[256,512]{1,0:T(8,128)S(1)}, f32[256,512]{1,0:T(8,128)}, u32[]{:S(2)}) copy-start(f32[256,512]{1,0:T(8,128)} %refs_0_.10) | copy-start | bytes 1572868
  12.5 51.7 %collective-permute-start = (bf16[256,2048]{1,0:T(8,128)(2,1)}, bf16[256,2048]{1,0:T(8,128)(2,1)}, u32[]{:S(2)}, u32[]{:S(2)}) collective-permute-start(bf16[256,2048]{1,0:T(8,128)(2,1)} %shard_map.589.refs_1_.refs_3_), channel_id=1, source_target_pairs={{0,2},{1,3},{2,0},{3,1},{4,6},{5,7},{6,4},{7,5},{8,10},{9,11},{10,... | collective-permute-start | bytes 3145736 | tf_op jit(solution)/shard_map/ppermute | solution.py:682
  16.9 54.2 %collective-permute-start.1 = (bf16[256,2048]{1,0:T(8,128)(2,1)}, bf16[256,2048]{1,0:T(8,128)(2,1)}, u32[]{:S(2)}, u32[]{:S(2)}) collective-permute-start(bf16[256,2048]{1,0:T(8,128)(2,1)} %broadcast_select_fusion.refs_1_.refs_5_), channel_id=1, source_target_pairs={{0,8},{1,9},{2,10},{3,11},{4,12},{5,13},{6,14},{7,15},{8,0},{9,1},... | collective-permute-start | bytes 3145736 | tf_op jit(solution)/shard_map/ppermute | solution.py:682
  60.8 46.6 %collective-permute-start.4 = (bf16[1024,1024]{1,0:T(8,128)(2,1)S(1)}, bf16[1024,1024]{1,0:T(8,128)(2,1)}, u32[]{:S(2)}, u32[]{:S(2)}) collective-permute-start(bf16[1024,1024]{1,0:T(8,128)(2,1)S(1)} %bitcast.42), channel_id=1, source_target_pairs={{0,4},{1,5},{2,6},{3,7},{4,0},{5,1},{6,2},{7,3},{8,12},{9,13},{10,... | collective-permute-start | bytes 6291464 | tf_op jit(solution)/shard_map/ppermute | solution.py:682
  66.0 28.4 %all-to-all-start.1 = ((bf16[4,256,512]{2,1,0:T(8,128)(2,1)}), bf16[4,256,512]{2,1,0:T(8,128)(2,1)S(1)}, u32[]{:S(2)}, u32[]{:S(2)}) async-start(bf16[4,256,512]{2,1,0:T(8,128)(2,1)} %bitcast.63), calls=%async_computation.1 | async-start | bytes 2097152 | tf_op jit(solution)/shard_map/all_to_all | solution.py:700
  69.5 8.4 %collective-permute-start.2 = (bf16[256,2048]{1,0:T(8,128)(2,1)}, bf16[256,2048]{1,0:T(8,128)(2,1)}, u32[]{:S(2)}, u32[]{:S(2)}) collective-permute-start(bf16[256,2048]{1,0:T(8,128)(2,1)} %shard_map.589.refs_1_.refs_3_), channel_id=1, source_target_pairs={{0,1},{1,0},{2,3},{3,2},{4,5},{5,4},{6,7},{7,6},{8,9},{9,8},{10,11... | collective-permute-start | bytes 3145736 | tf_op jit(solution)/shard_map/ppermute | solution.py:682
  71.1 6.8 collective-permute-start.3
  71.1 48.4 %collective-permute-start.6 = (bf16[256,2048]{1,0:T(8,128)(2,1)}, bf16[256,2048]{1,0:T(8,128)(2,1)}, u32[]{:S(2)}, u32[]{:S(2)}) collective-permute-start(bf16[256,2048]{1,0:T(8,128)(2,1)} %broadcast_select_fusion.refs_1_.refs_5_), channel_id=1, source_target_pairs={{0,2},{1,3},{2,0},{3,1},{4,6},{5,7},{6,4},{7,5},{8,10},{9,11},{10,... | collective-permute-start | bytes 3145736 | tf_op jit(solution)/shard_map/ppermute | solution.py:682
  72.6 46.9 %collective-permute-start.7 = (bf16[256,2048]{1,0:T(8,128)(2,1)}, bf16[256,2048]{1,0:T(8,128)(2,1)}, u32[]{:S(2)}, u32[]{:S(2)}) collective-permute-start(bf16[256,2048]{1,0:T(8,128)(2,1)} %collective-permute-done.1.refs_1_.refs_3_), channel_id=1, source_target_pairs={{0,2},{1,3},{2,0},{3,1},{4,6},{5,7},{6,4},{7,5},{8,10},{9,11},{10,... | collective-permute-start | bytes 3145736 | tf_op jit(solution)/shard_map/ppermute | solution.py:682
  97.7 65.6 %all-to-all-start.2 = ((bf16[4,256,1024]{2,1,0:T(8,128)(2,1)}), bf16[4,256,1024]{2,1,0:T(8,128)(2,1)}, u32[]{:S(2)}, u32[]{:S(2)}) async-start(bf16[4,256,1024]{2,1,0:T(8,128)(2,1)} %bitcast.60), calls=%async_computation.2 | async-start | bytes 4194304 | tf_op jit(solution)/shard_map/all_to_all | solution.py:700
  124.8 63.8 %collective-permute-start.11 = (bf16[1024,2048]{1,0:T(8,128)(2,1)}, bf16[1024,2048]{1,0:T(8,128)(2,1)}, u32[]{:S(2)}, u32[]{:S(2)}) collective-permute-start(bf16[1024,2048]{1,0:T(8,128)(2,1)} %shard_map.598.refs_5_.refs_1_), channel_id=1, source_target_pairs={{0,1},{1,0},{2,3},{3,2},{4,5},{5,4},{6,7},{7,6},{8,9},{9,8},{10,11... | collective-permute-start | bytes 12582920 | tf_op jit(solution)/shard_map/ppermute | solution.py:682
  124.8 25.7 %collective-permute-start.5 = (bf16[1024,512]{1,0:T(8,128)(2,1)S(1)}, bf16[1024,512]{1,0:T(8,128)(2,1)S(1)}, u32[]{:S(2)}, u32[]{:S(2)}) collective-permute-start(bf16[1024,512]{1,0:T(8,128)(2,1)S(1)} %bitcast.52), channel_id=1, source_target_pairs={{0,4},{1,5},{2,6},{3,7},{4,0},{5,1},{6,2},{7,3},{8,12},{9,13},{10,... | collective-permute-start | bytes 3145736 | tf_op jit(solution)/shard_map/ppermute | solution.py:682
  158.8 4.1 collective-permute-start.9
  158.8 16.1 %collective-permute-start.8 = (bf16[256,2048]{1,0:T(8,128)(2,1)}, bf16[256,2048]{1,0:T(8,128)(2,1)}, u32[]{:S(2)}, u32[]{:S(2)}) collective-permute-start(bf16[256,2048]{1,0:T(8,128)(2,1)} %get-tuple-element.96), channel_id=1, source_target_pairs={{0,1},{1,0},{2,3},{3,2},{4,5},{5,4},{6,7},{7,6},{8,9},{9,8},{10,11... | collective-permute-start | bytes 3145736 | tf_op jit(solution)/shard_map/ppermute | solution.py:682
  163.3 25.4 %collective-permute-start.10 = (bf16[256,2048]{1,0:T(8,128)(2,1)S(1)}, bf16[256,2048]{1,0:T(8,128)(2,1)}, u32[]{:S(2)}, u32[]{:S(2)}) collective-permute-start(bf16[256,2048]{1,0:T(8,128)(2,1)S(1)} %shard_map.600.refs_1_), channel_id=1, source_target_pairs={{0,2},{1,3},{2,0},{3,1},{4,6},{5,7},{6,4},{7,5},{8,10},{9,11},{10,... | collective-permute-start | bytes 3145736 | tf_op jit(solution)/shard_map/ppermute | solution.py:682
  166.1 55.7 %all-to-all-start.3 = ((bf16[4,256,1024]{2,1,0:T(8,128)(2,1)}), bf16[4,256,1024]{2,1,0:T(8,128)(2,1)S(1)}, u32[]{:S(2)}, u32[]{:S(2)}) async-start(bf16[4,256,1024]{2,1,0:T(8,128)(2,1)} %bitcast.41), calls=%async_computation.3 | async-start | bytes 4194304 | tf_op jit(solution)/shard_map/all_to_all | solution.py:700
  173.1 47.4 %collective-permute-start.15 = (bf16[1024,1024]{1,0:T(8,128)(2,1)}, bf16[1024,1024]{1,0:T(8,128)(2,1)S(1)}, u32[]{:S(2)}, u32[]{:S(2)}) collective-permute-start(bf16[1024,1024]{1,0:T(8,128)(2,1)} %shard_map.605.refs_1_.refs_2_.refs_3_), channel_id=1, source_target_pairs={{0,4},{1,5},{2,6},{3,7},{4,0},{5,1},{6,2},{7,3},{8,12},{9,13},{10,... | collective-permute-start | bytes 6291464 | tf_op jit(solution)/shard_map/ppermute | solution.py:682
  192.9 24.8 %collective-permute-start.12 = (bf16[256,2048]{1,0:T(8,128)(2,1)}, bf16[256,2048]{1,0:T(8,128)(2,1)}, u32[]{:S(2)}, u32[]{:S(2)}) collective-permute-start(bf16[256,2048]{1,0:T(8,128)(2,1)} %get-tuple-element.100.refs_1_), channel_id=1, source_target_pairs={{0,2},{1,9},{2,0},{3,11},{4,6},{5,13},{6,4},{7,15},{8,10},{9,1},{1... | collective-permute-start | bytes 3145736 | tf_op jit(solution)/shard_map/ppermute | solution.py:682
  194.3 34.3 %collective-permute-start.13 = (bf16[256,2048]{1,0:T(8,128)(2,1)}, bf16[256,2048]{1,0:T(8,128)(2,1)}, u32[]{:S(2)}, u32[]{:S(2)}) collective-permute-start(bf16[256,2048]{1,0:T(8,128)(2,1)} %get-tuple-element.100.refs_1_), channel_id=1, source_target_pairs={{0,8},{1,3},{2,10},{3,1},{4,12},{5,7},{6,14},{7,5},{8,0},{9,11},{1... | collective-permute-start | bytes 3145736 | tf_op jit(solution)/shard_map/ppermute | solution.py:682
  217.6 22.2 %collective-permute-start.14 = (bf16[256,2048]{1,0:T(8,128)(2,1)}, bf16[256,2048]{1,0:T(8,128)(2,1)S(1)}, u32[]{:S(2)}, u32[]{:S(2)}) collective-permute-start(bf16[256,2048]{1,0:T(8,128)(2,1)} %collective-permute-done.12.refs_1_.refs_2_), channel_id=1, source_target_pairs={{0,8},{1,3},{2,10},{3,1},{4,12},{5,7},{6,14},{7,5},{8,0},{9,11},{1... | collective-permute-start | bytes 3145736 | tf_op jit(solution)/shard_map/ppermute | solution.py:682
  223.5 42.1 %collective-permute-start.16 = (bf16[1024,1024]{1,0:T(8,128)(2,1)S(1)}, bf16[1024,1024]{1,0:T(8,128)(2,1)}, u32[]{:S(2)}, u32[]{:S(2)}) collective-permute-start(bf16[1024,1024]{1,0:T(8,128)(2,1)S(1)} %shard_map.607.refs_4_.refs_1_.refs_5_), channel_id=1, source_target_pairs={{0,4},{1,5},{2,6},{3,7},{4,0},{5,1},{6,2},{7,3},{8,12},{9,13},{10,... | collective-permute-start | bytes 6291464 | tf_op jit(solution)/shard_map/ppermute | solution.py:682
  241.1 55.9 %all-to-all-start.4 = ((bf16[4,256,1024]{2,1,0:T(8,128)(2,1)}), bf16[4,256,1024]{2,1,0:T(8,128)(2,1)}, u32[]{:S(2)}, u32[]{:S(2)}) async-start(bf16[4,256,1024]{2,1,0:T(8,128)(2,1)} %bitcast.49), calls=%async_computation.4 | async-start | bytes 4194304 | tf_op jit(solution)/shard_map/all_to_all | solution.py:700
  245.8 48.1 %collective-permute-start.18 = (bf16[256,2048]{1,0:T(8,128)(2,1)}, bf16[256,2048]{1,0:T(8,128)(2,1)S(1)}, u32[]{:S(2)}, u32[]{:S(2)}) collective-permute-start(bf16[256,2048]{1,0:T(8,128)(2,1)} %get-tuple-element.100.refs_1_), channel_id=1, source_target_pairs={{0,1},{1,0},{2,3},{3,2},{4,5},{5,4},{6,7},{7,6},{8,9},{9,8},{10,11... | collective-permute-start | bytes 3145736 | tf_op jit(solution)/shard_map/ppermute | solution.py:682
  246.8 47.1 %collective-permute-start.20 = (bf16[256,2048]{1,0:T(8,128)(2,1)}, bf16[256,2048]{1,0:T(8,128)(2,1)S(1)}, u32[]{:S(2)}, u32[]{:S(2)}) collective-permute-start(bf16[256,2048]{1,0:T(8,128)(2,1)} %collective-permute-done.13.refs_3_), channel_id=1, source_target_pairs={{0,1},{1,0},{2,3},{3,2},{4,5},{5,4},{6,7},{7,6},{8,9},{9,8},{10,11... | collective-permute-start | bytes 3145736 | tf_op jit(solution)/shard_map/ppermute | solution.py:682
  270.5 23.4 %collective-permute-start.19 = (bf16[256,2048]{1,0:T(8,128)(2,1)}, bf16[256,2048]{1,0:T(8,128)(2,1)S(1)}, u32[]{:S(2)}, u32[]{:S(2)}) collective-permute-start(bf16[256,2048]{1,0:T(8,128)(2,1)} %collective-permute-done.12.refs_1_.refs_2_), channel_id=1, source_target_pairs={{0,1},{1,0},{2,3},{3,2},{4,5},{5,4},{6,7},{7,6},{8,9},{9,8},{10,11... | collective-permute-start | bytes 3145736 | tf_op jit(solution)/shard_map/ppermute | solution.py:682
  277.0 16.9 %collective-permute-start.21 = (bf16[256,2048]{1,0:T(8,128)(2,1)S(1)}, bf16[256,2048]{1,0:T(8,128)(2,1)S(1)}, u32[]{:S(2)}, u32[]{:S(2)}) collective-permute-start(bf16[256,2048]{1,0:T(8,128)(2,1)S(1)} %shard_map.612), channel_id=1, source_target_pairs={{0,1},{1,0},{2,3},{3,2},{4,5},{5,4},{6,7},{7,6},{8,9},{9,8},{10,11... | collective-permute-start | bytes 3145736 | tf_op jit(solution)/shard_map/ppermute | solution.py:682
  297.0 48.6 %collective-permute-start.17 = (bf16[1024,1024]{1,0:T(8,128)(2,1)}, bf16[1024,1024]{1,0:T(8,128)(2,1)S(1)}, u32[]{:S(2)}, u32[]{:S(2)}) collective-permute-start(bf16[1024,1024]{1,0:T(8,128)(2,1)} %shard_map.611.refs_6_.refs_2_), channel_id=1, source_target_pairs={{0,4},{1,5},{2,6},{3,7},{4,0},{5,1},{6,2},{7,3},{8,12},{9,13},{10,... | collective-permute-start | bytes 6291464 | tf_op jit(solution)/shard_map/ppermute | solution.py:682
  332.3 58.4 %collective-permute-start.27 = (bf16[1024,1024]{1,0:T(8,128)(2,1)S(1)}, bf16[1024,1024]{1,0:T(8,128)(2,1)S(1)}, u32[]{:S(2)}, u32[]{:S(2)}) collective-permute-start(bf16[1024,1024]{1,0:T(8,128)(2,1)S(1)} %get-tuple-element.122), channel_id=1, source_target_pairs={{0,4},{1,5},{2,6},{3,7},{4,0},{5,1},{6,2},{7,3},{8,12},{9,13},{10,... | collective-permute-start | bytes 6291464 | tf_op jit(solution)/shard_map/ppermute | solution.py:682
  387.5 47.8 %collective-permute-start.22 = (bf16[1024,1024]{1,0:T(8,128)(2,1)}, bf16[1024,1024]{1,0:T(8,128)(2,1)}, u32[]{:S(2)}, u32[]{:S(2)}) collective-permute-start(bf16[1024,1024]{1,0:T(8,128)(2,1)} %get-tuple-element.115), channel_id=1, source_target_pairs={{0,4},{1,5},{2,6},{3,7},{4,0},{5,1},{6,2},{7,3},{8,12},{9,13},{10,... | collective-permute-start | bytes 6291464 | tf_op jit(solution)/shard_map/ppermute | solution.py:682
  394.5 80.8 %all-to-all-start.5 = ((bf16[4,256,1024]{2,1,0:T(8,128)(2,1)}), bf16[4,256,1024]{2,1,0:T(8,128)(2,1)S(1)}, u32[]{:S(2)}, u32[]{:S(2)}) async-start(bf16[4,256,1024]{2,1,0:T(8,128)(2,1)} %bitcast.66), calls=%async_computation.5 | async-start | bytes 4194304 | tf_op jit(solution)/shard_map/all_to_all | solution.py:700
  430.8 20.3 %collective-permute-start.24 = (bf16[256,2048]{1,0:T(8,128)(2,1)S(1)}, bf16[256,2048]{1,0:T(8,128)(2,1)S(1)}, u32[]{:S(2)}, u32[]{:S(2)}) collective-permute-start(bf16[256,2048]{1,0:T(8,128)(2,1)S(1)} %get-tuple-element.119), channel_id=1, source_target_pairs={{0,1},{1,0},{2,3},{3,2},{4,5},{5,4},{6,7},{7,6},{8,9},{9,8},{10,11... | collective-permute-start | bytes 3145736 | tf_op jit(solution)/shard_map/ppermute | solution.py:682
  430.9 23.8 %collective-permute-start.23 = (bf16[256,2048]{1,0:T(8,128)(2,1)S(1)}, bf16[256,2048]{1,0:T(8,128)(2,1)S(1)}, u32[]{:S(2)}, u32[]{:S(2)}) collective-permute-start(bf16[256,2048]{1,0:T(8,128)(2,1)S(1)} %get-tuple-element.117), channel_id=1, source_target_pairs={{0,1},{1,0},{2,3},{3,2},{4,5},{5,4},{6,7},{7,6},{8,9},{9,8},{10,11... | collective-permute-start | bytes 3145736 | tf_op jit(solution)/shard_map/ppermute | solution.py:682
  431.4 42.8 %collective-permute-start.25 = (bf16[256,2048]{1,0:T(8,128)(2,1)S(1)}, bf16[256,2048]{1,0:T(8,128)(2,1)S(1)}, u32[]{:S(2)}, u32[]{:S(2)}) collective-permute-start(bf16[256,2048]{1,0:T(8,128)(2,1)S(1)} %get-tuple-element.121), channel_id=1, source_target_pairs={{0,1},{1,0},{2,3},{3,2},{4,5},{5,4},{6,7},{7,6},{8,9},{9,8},{10,11... | collective-permute-start | bytes 3145736 | tf_op jit(solution)/shard_map/ppermute | solution.py:682
  451.5 23.8 %collective-permute-start.26 = (bf16[256,2048]{1,0:T(8,128)(2,1)S(1)}, bf16[256,2048]{1,0:T(8,128)(2,1)}, u32[]{:S(2)}, u32[]{:S(2)}) collective-permute-start(bf16[256,2048]{1,0:T(8,128)(2,1)S(1)} %shard_map.623.refs_5_), channel_id=1, source_target_pairs={{0,8},{1,3},{2,10},{3,1},{4,12},{5,7},{6,14},{7,5},{8,0},{9,11},{1... | collective-permute-start | bytes 3145736 | tf_op jit(solution)/shard_map/ppermute | solution.py:682
  453.0 45.7 %collective-permute-start.32 = (bf16[1024,1024]{1,0:T(8,128)(2,1)}, bf16[1024,1024]{1,0:T(8,128)(2,1)}, u32[]{:S(2)}, u32[]{:S(2)}) collective-permute-start(bf16[1024,1024]{1,0:T(8,128)(2,1)} %get-tuple-element.124), channel_id=1, source_target_pairs={{0,4},{1,5},{2,6},{3,7},{4,0},{5,1},{6,2},{7,3},{8,12},{9,13},{10,... | collective-permute-start | bytes 6291464 | tf_op jit(solution)/shard_map/ppermute | solution.py:682
  456.4 34.9 %collective-permute-start.29 = (bf16[256,2048]{1,0:T(8,128)(2,1)}, bf16[256,2048]{1,0:T(8,128)(2,1)}, u32[]{:S(2)}, u32[]{:S(2)}) collective-permute-start(bf16[256,2048]{1,0:T(8,128)(2,1)} %get-tuple-element.114.refs_7_), channel_id=1, source_target_pairs={{0,1},{1,0},{2,3},{3,2},{4,5},{5,4},{6,7},{7,6},{8,9},{9,8},{10,11... | collective-permute-start | bytes 3145736 | tf_op jit(solution)/shard_map/ppermute | solution.py:682
  465.1 33.5 %collective-permute-start.30 = (bf16[256,2048]{1,0:T(8,128)(2,1)}, bf16[256,2048]{1,0:T(8,128)(2,1)}, u32[]{:S(2)}, u32[]{:S(2)}) collective-permute-start(bf16[256,2048]{1,0:T(8,128)(2,1)} %shard_map.622.refs_4_), channel_id=1, source_target_pairs={{0,8},{1,3},{2,10},{3,1},{4,12},{5,7},{6,14},{7,5},{8,0},{9,11},{1... | collective-permute-start | bytes 3145736 | tf_op jit(solution)/shard_map/ppermute | solution.py:682
  481.3 17.4 %collective-permute-start.31 = (bf16[256,2048]{1,0:T(8,128)(2,1)S(1)}, bf16[256,2048]{1,0:T(8,128)(2,1)}, u32[]{:S(2)}, u32[]{:S(2)}) collective-permute-start(bf16[256,2048]{1,0:T(8,128)(2,1)S(1)} %shard_map.627.refs_1_.refs_2_), channel_id=1, source_target_pairs={{0,2},{1,9},{2,0},{3,11},{4,6},{5,13},{6,4},{7,15},{8,10},{9,1},{1... | collective-permute-start | bytes 3145736 | tf_op jit(solution)/shard_map/ppermute | solution.py:682
  486.3 53.1 %all-to-all-start.6 = ((bf16[4,256,1024]{2,1,0:T(8,128)(2,1)}), bf16[4,256,1024]{2,1,0:T(8,128)(2,1)S(1)}, u32[]{:S(2)}, u32[]{:S(2)}) async-start(bf16[4,256,1024]{2,1,0:T(8,128)(2,1)} %bitcast.65), calls=%async_computation.6 | async-start | bytes 4194304 | tf_op jit(solution)/shard_map/all_to_all | solution.py:700
  505.5 22.5 %collective-permute-start.33 = (bf16[256,2048]{1,0:T(8,128)(2,1)S(1)}, bf16[256,2048]{1,0:T(8,128)(2,1)S(1)}, u32[]{:S(2)}, u32[]{:S(2)}) collective-permute-start(bf16[256,2048]{1,0:T(8,128)(2,1)S(1)} %get-tuple-element.125.refs_1_), channel_id=1, source_target_pairs={{0,2},{1,3},{2,0},{3,1},{4,6},{5,7},{6,4},{7,5},{8,10},{9,11},{10,... | collective-permute-start | bytes 3145736 | tf_op jit(solution)/shard_map/ppermute | solution.py:682
  507.0 21.0 %collective-permute-start.34 = (bf16[256,2048]{1,0:T(8,128)(2,1)S(1)}, bf16[256,2048]{1,0:T(8,128)(2,1)S(1)}, u32[]{:S(2)}, u32[]{:S(2)}) collective-permute-start(bf16[256,2048]{1,0:T(8,128)(2,1)S(1)} %get-tuple-element.125.refs_1_), channel_id=1, source_target_pairs={{0,1},{1,0},{2,3},{3,2},{4,5},{5,4},{6,7},{7,6},{8,9},{9,8},{10,11... | collective-permute-start | bytes 3145736 | tf_op jit(solution)/shard_map/ppermute | solution.py:682
  528.0 2.7 collective-permute-start.35
  545.0 57.0 %all-to-all-start.7 = ((bf16[4,256,1024]{2,1,0:T(8,128)(2,1)}), bf16[4,256,1024]{2,1,0:T(8,128)(2,1)S(1)}, u32[]{:S(2)}, u32[]{:S(2)}) async-start(bf16[4,256,1024]{2,1,0:T(8,128)(2,1)} %bitcast.67), calls=%async_computation.7 | async-start | bytes 4194304 | tf_op jit(solution)/shard_map/all_to_all | solution.py:700
  548.7 65.0 %collective-permute-start.28 = (bf16[1024,2048]{1,0:T(8,128)(2,1)}, bf16[1024,2048]{1,0:T(8,128)(2,1)}, u32[]{:S(2)}, u32[]{:S(2)}) collective-permute-start(bf16[1024,2048]{1,0:T(8,128)(2,1)} %shard_map.628), channel_id=1, source_target_pairs={{0,1},{1,0},{2,3},{3,2},{4,5},{5,4},{6,7},{7,6},{8,9},{9,8},{10,11... | collective-permute-start | bytes 12582920 | tf_op jit(solution)/shard_map/ppermute | solution.py:682
  558.2 30.0 %collective-permute-start.37 = (bf16[1024,512]{1,0:T(8,128)(2,1)S(1)}, bf16[1024,512]{1,0:T(8,128)(2,1)S(1)}, u32[]{:S(2)}, u32[]{:S(2)}) collective-permute-start(bf16[1024,512]{1,0:T(8,128)(2,1)S(1)} %get-tuple-element.128), channel_id=1, source_target_pairs={{0,4},{1,5},{2,6},{3,7},{4,0},{5,1},{6,2},{7,3},{8,12},{9,13},{10,... | collective-permute-start | bytes 3145736 | tf_op jit(solution)/shard_map/ppermute | solution.py:682
  586.5 47.0 %collective-permute-start.41 = (bf16[1024,1024]{1,0:T(8,128)(2,1)}, bf16[1024,1024]{1,0:T(8,128)(2,1)}, u32[]{:S(2)}, u32[]{:S(2)}) collective-permute-start(bf16[1024,1024]{1,0:T(8,128)(2,1)} %get-tuple-element.136), channel_id=1, source_target_pairs={{0,4},{1,5},{2,6},{3,7},{4,0},{5,1},{6,2},{7,3},{8,12},{9,13},{10,... | collective-permute-start | bytes 6291464 | tf_op jit(solution)/shard_map/ppermute | solution.py:682
  608.6 29.9 %all-to-all-start.8 = ((bf16[4,256,512]{2,1,0:T(8,128)(2,1)}), bf16[4,256,512]{2,1,0:T(8,128)(2,1)S(1)}, u32[]{:S(2)}, u32[]{:S(2)}) async-start(bf16[4,256,512]{2,1,0:T(8,128)(2,1)} %bitcast.26), calls=%async_computation.8 | async-start | bytes 2097152 | tf_op jit(solution)/shard_map/all_to_all | solution.py:700
  618.0 50.9 %collective-permute-start.36 = (bf16[512,2048]{1,0:T(8,128)(2,1)}, bf16[512,2048]{1,0:T(8,128)(2,1)}, u32[]{:S(2)}, u32[]{:S(2)}) collective-permute-start(bf16[512,2048]{1,0:T(8,128)(2,1)} %shard_map.634), channel_id=1, source_target_pairs={{0,8},{1,3},{2,10},{3,1},{4,12},{5,7},{6,14},{7,5},{8,0},{9,11},{1... | collective-permute-start | bytes 6291464 | tf_op jit(solution)/shard_map/ppermute | solution.py:682
  642.9 61.2 %all-to-all-start.9 = ((bf16[4,256,1024]{2,1,0:T(8,128)(2,1)}), bf16[4,256,1024]{2,1,0:T(8,128)(2,1)}, u32[]{:S(2)}, u32[]{:S(2)}) async-start(bf16[4,256,1024]{2,1,0:T(8,128)(2,1)} %bitcast.64), calls=%async_computation.9 | async-start | bytes 4194304 | tf_op jit(solution)/shard_map/all_to_all | solution.py:700
  647.4 24.3 %collective-permute-start.40 = (bf16[256,2048]{1,0:T(8,128)(2,1)}, bf16[256,2048]{1,0:T(8,128)(2,1)S(1)}, u32[]{:S(2)}, u32[]{:S(2)}) collective-permute-start(bf16[256,2048]{1,0:T(8,128)(2,1)} %get-tuple-element.135), channel_id=1, source_target_pairs={{0,1},{1,0},{2,3},{3,2},{4,5},{5,4},{6,7},{7,6},{8,9},{9,8},{10,11... | collective-permute-start | bytes 3145736 | tf_op jit(solution)/shard_map/ppermute | solution.py:682
  647.4 30.1 %collective-permute-start.39 = (bf16[256,2048]{1,0:T(8,128)(2,1)}, bf16[256,2048]{1,0:T(8,128)(2,1)S(1)}, u32[]{:S(2)}, u32[]{:S(2)}) collective-permute-start(bf16[256,2048]{1,0:T(8,128)(2,1)} %get-tuple-element.133), channel_id=1, source_target_pairs={{0,1},{1,0},{2,3},{3,2},{4,5},{5,4},{6,7},{7,6},{8,9},{9,8},{10,11... | collective-permute-start | bytes 3145736 | tf_op jit(solution)/shard_map/ppermute | solution.py:682
  672.0 14.9 %collective-permute-start.42 = (bf16[256,2048]{1,0:T(8,128)(2,1)S(1)}, bf16[256,2048]{1,0:T(8,128)(2,1)S(1)}, u32[]{:S(2)}, u32[]{:S(2)}) collective-permute-start(bf16[256,2048]{1,0:T(8,128)(2,1)S(1)} %shard_map.640.refs_1_), channel_id=1, source_target_pairs={{0,2},{1,3},{2,0},{3,1},{4,6},{5,7},{6,4},{7,5},{8,10},{9,11},{10,... | collective-permute-start | bytes 3145736 | tf_op jit(solution)/shard_map/ppermute | solution.py:682
  673.3 44.7 %collective-permute-start.38 = (bf16[256,2048]{1,0:T(8,128)(2,1)S(1)}, bf16[256,2048]{1,0:T(8,128)(2,1)}, u32[]{:S(2)}, u32[]{:S(2)}) collective-permute-start(bf16[256,2048]{1,0:T(8,128)(2,1)S(1)} %shard_map.639.refs_2_), channel_id=1, source_target_pairs={{0,2},{1,9},{2,0},{3,11},{4,6},{5,13},{6,4},{7,15},{8,10},{9,1},{1... | collective-permute-start | bytes 3145736 | tf_op jit(solution)/shard_map/ppermute | solution.py:682
  691.8 1.2 collective-permute-start.43
  693.0 5.4 collective-permute-start.44
  698.5 4.6 collective-permute-start.45
  703.1 3.7 collective-permute-start.46
  706.6 1.2 collective-permute-start.48
  706.9 17.2 %collective-permute-start.47 = (f32[32,128]{1,0:T(8,128)S(1)}, f32[32,128]{1,0:T(8,128)S(1)}, u32[]{:S(2)}, u32[]{:S(2)}) collective-permute-start(f32[32,128]{1,0:T(8,128)S(1)} %add.226), channel_id=1, source_target_pairs={{0,4},{1,5},{2,6},{3,7},{4,0},{5,1},{6,2},{7,3},{8,12},{9,13},{10,... | collective-permute-start | bytes 49160 | tf_op jit(solution)/shard_map/ppermute | solution.py:682
  707.8 3.6 collective-permute-start.49
  711.4 4.5 collective-permute-start.50
  716.0 8.2 %collective-permute-start.51 = (f32[8,128]{1,0:T(8,128)S(1)}, f32[8,128]{1,0:T(8,128)S(1)}, u32[]{:S(2)}, u32[]{:S(2)}) collective-permute-start(f32[8,128]{1,0:T(8,128)S(1)} %add.234), channel_id=1, source_target_pairs={{0,8},{1,9},{2,10},{3,11},{4,12},{5,13},{6,14},{7,15},{8,0},{9,1},... | collective-permute-start | bytes 12296 | tf_op jit(solution)/shard_map/ppermute | solution.py:682
  724.2 3.7 collective-permute-start.52
  (110 other events, 487.4 us)

commit v4 on v3

--- a/solution.py
+++ b/solution.py
@@ -880,7 +880,7 @@
     )
     back_one = swap_one(sent)
     out_got = swap(pin(out_near, sent), 0, 1)
-    gate_far = trade_far(add_low(far_rows, (pin(gate_got, sent), 0), (gate_own, 0)))
+    gate_far = trade_far(add_low(far_rows, (pin(gate_got, out_near, down_far), 0), (gate_own, 0)))
     middle_grad, low_grad, gain_mlp_part = leave_norm(
         rows_dev,
         [(back_mine[0], 0), (back_got[0], 0), (back_two[0], 0), (pin(back_one, up_got), 0)],
@@ -938,9 +938,8 @@
         (pin(out_one, input_grad), 0),
     )
     gains = jnp.concatenate([gain_attn_part[0], gain_mlp_part[0]]).reshape(-1, 128)
-    gains = sum_everywhere(gains).reshape(-1)
     shard_out, square_out_part = finish_shard(proj_far, shard_rows, 1)
-    shard_qkv, square_qkv_part = finish_shard(qkv_far, shard_rows, 1)
+    shard_qkv, square_qkv_part = finish_shard(pin(qkv_far, block_out), shard_rows, 1)
     width_query, width_key = w_query.shape[1], w_key.shape[1]
     shard_grads = (
         shard_qkv[:, :width_query],
@@ -954,7 +953,9 @@
     square_part = (
         square_down_part + square_gate_part + square_up_part + square_qkv_part + square_out_part
     )
-    square_total = sum_everywhere(square_part)[0, 0]
+    summed = sum_everywhere(jnp.concatenate([gains, square_part]))
+    square_total = summed[-1, 0]
+    gains = summed[: gains.shape[0]].reshape(-1)
     gain_attn_grad = gains[: norm_attn.shape[0]]
     gain_mlp_grad = gains[norm_attn.shape[0] :]
     clip_norm = jnp.sqrt(

time: 765 us -> 762 us (level)
    ppermute x53 -> x48, waiting for transfers between devices: 209 us -> 207 us  [swap(): return lax.ppermute(settle(value), AXES, pairs)]
    ppermute x53 -> x48, starting transfers between devices: 48.9 us -> 48.6 us  [swap(): return lax.ppermute(settle(value), AXES, pairs)]
    unnamed x225 -> x227, local copies, waits for them, and re-layouts: 69.9 us -> 70.1 us
  transfers between devices with their start and end apart: 63 -> 58, of which waited for: 31 -> 29; matrix products, arithmetic and copies ran while one was open for 1% -> 1% of each run, Pallas kernels for 37% -> 37%
where the time goes in v4:
time: 762 us; the launch traced here: 751 us
  Pallas kernels  283 us (37%)
  waiting for transfers between devices  271 us (36%)
  starting transfers between devices  94.8 us (12%)
  local copies, waits for them, and re-layouts  70.7 us (9%)
  other arithmetic  26 us (3%)
    pallas_call x60, Pallas kernels, call_kernel(): pl.pallas_call(body, grid_spec=spec, out_shape=out_shape, input_output_al...  283 us
    ppermute x48, waiting for transfers between devices, swap(): return lax.ppermute(settle(value), AXES, pairs)  207 us
    unnamed x227, local copies, waits for them, and re-layouts  70.1 us
    all_to_all x10, waiting for transfers between devices, trade_far(): lax.all_to_all(settle(blocks), 'fsdp', 0, 0, axis_index_groups=groups, ti...  63.8 us
    ppermute x48, starting transfers between devices, swap(): return lax.ppermute(settle(value), AXES, pairs)  48.6 us
    all_to_all x10, starting transfers between devices, trade_far(): lax.all_to_all(settle(blocks), 'fsdp', 0, 0, axis_index_groups=groups, ti...  46.2 us
    mul x7, other arithmetic, adam_step(): -LEARN_RATE  19.7 us
  transfers between devices with their start and end apart: 58, of which 29 were waited for; matrix products, arithmetic and copies ran while one was open for 1% of the time, Pallas kernels for 37%

profile of v4, /device:TPU:0, one launch (start us, length us, event | category | flops | bytes accessed | tf_op | source)
XLA Modules:
  0.0 751.3 jit_solution(7946433010454137710)
XLA Ops:
  6.1 6.3 all-to-all-start
  19.0 41.8 %all-to-all-done = bf16[4,256,1024]{2,1,0:T(8,128)(2,1)S(1)} async-done(((bf16[4,256,1024]{2,1,0:T(8,128)(2,1)}), bf16[4,256,1024]{2,1,0:T(8,128)(2,1)S(1)}, u32[]{:S(2)}, u32[]{:S(2)}) %all-to-all-start) | async-done | bytes 2097184 | tf_op jit(solution)/shard_map/all_to_all | solution.py:700
  66.0 3.5 all-to-all-start.1
  78.0 5.2 shard_map.591.refs_1_
  83.2 11.2 %all-to-all-done.1 = bf16[4,256,512]{2,1,0:T(8,128)(2,1)S(1)} async-done(((bf16[4,256,512]{2,1,0:T(8,128)(2,1)}), bf16[4,256,512]{2,1,0:T(8,128)(2,1)S(1)}, u32[]{:S(2)}, u32[]{:S(2)}) %all-to-all-start.1) | async-done | bytes 1048608 | tf_op jit(solution)/shard_map/all_to_all | solution.py:700
  97.7 4.5 all-to-all-start.2
  102.1 5.3 collective-permute-done.4.refs_3_
  109.5 8.7 %shard_map.595.refs_1_.refs_2_.refs_3_.refs_5_.refs_6_.refs_7_ = bf16[1024,1024]{1,0:T(8,128)(2,1)S(1)} custom-call(s32[1]{0:T(128)} %bitcast.refs_0_, bf16[1024,2048]{1,0:T(8,128)(2,1)} %shard_map.591.refs_1_, bf16[1024,1024]{1,0:T(8,128)(2,1)} %bitcast.44, bf16[1024,1024]{1,0:T(8,128)(2,1)} %collective-permute-done.4.refs_3_, f32[1024,128]{1,0:T(8,128)S(1)} %copy-done.42, ...), custom_call_target="tpu_custom_call" | custom-call | flops 1 | bytes 1 | tf_op jit(solution)/shard_map/pallas_call | solution.py:96
  119.5 5.3 shard_map.598.refs_5_.refs_1_
  127.1 7.3 shard_map.597.refs_1_.refs_2_
  134.4 16.1 %collective-permute-done.5.refs_3_ = bf16[1024,512]{1,0:T(8,128)(2,1)S(1)} collective-permute-done((bf16[1024,512]{1,0:T(8,128)(2,1)S(1)}, bf16[1024,512]{1,0:T(8,128)(2,1)S(1)}, u32[]{:S(2)}, u32[]{:S(2)}) %collective-permute-start.5) | collective-permute-done | bytes 1048608 | tf_op jit(solution)/shard_map/ppermute | solution.py:682
  151.5 6.3 shard_map.599
  159.4 3.6 collective-permute-done.9.refs_1_
  166.2 3.8 all-to-all-start.3
  174.9 13.7 %collective-permute-done.10.refs_3_ = bf16[256,2048]{1,0:T(8,128)(2,1)} collective-permute-done((bf16[256,2048]{1,0:T(8,128)(2,1)S(1)}, bf16[256,2048]{1,0:T(8,128)(2,1)}, u32[]{:S(2)}, u32[]{:S(2)}) %collective-permute-start.10) | collective-permute-done | bytes 1048608 | tf_op jit(solution)/shard_map/ppermute | solution.py:682
  188.7 4.2 shard_map.602
  194.7 22.9 %collective-permute-done.12.refs_1_.refs_2_ = bf16[256,2048]{1,0:T(8,128)(2,1)} collective-permute-done((bf16[256,2048]{1,0:T(8,128)(2,1)}, bf16[256,2048]{1,0:T(8,128)(2,1)}, u32[]{:S(2)}, u32[]{:S(2)}) %collective-permute-start.12) | collective-permute-done | bytes 1048608 | tf_op jit(solution)/shard_map/ppermute | solution.py:682
  225.3 3.4 collective-permute-done.13.refs_3_
  228.7 11.1 %collective-permute-done.14.refs_4_.refs_2_.refs_0_ = bf16[256,2048]{1,0:T(8,128)(2,1)S(1)} collective-permute-done((bf16[256,2048]{1,0:T(8,128)(2,1)}, bf16[256,2048]{1,0:T(8,128)(2,1)S(1)}, u32[]{:S(2)}, u32[]{:S(2)}) %collective-permute-start.14) | collective-permute-done | bytes 1048608 | tf_op jit(solution)/shard_map/ppermute | solution.py:682
  241.1 4.7 all-to-all-start.4
  246.9 18.7 %collective-permute-done.16.refs_5_.refs_1_.refs_6_ = bf16[1024,1024]{1,0:T(8,128)(2,1)} collective-permute-done((bf16[1024,1024]{1,0:T(8,128)(2,1)S(1)}, bf16[1024,1024]{1,0:T(8,128)(2,1)}, u32[]{:S(2)}, u32[]{:S(2)}) %collective-permute-start.16) | collective-permute-done | bytes 2097184 | tf_op jit(solution)/shard_map/ppermute | solution.py:682
  265.6 4.9 shard_map.608.refs_1_
  270.5 6.6 collective-permute-start.19
  277.1 15.5 %shard_map.609 = (bf16[1024,1024]{1,0:T(8,128)(2,1)S(1)}, bf16[1024,1024]{1,0:T(8,128)(2,1)S(1)}, bf16[1024,1024]{1,0:T(8,128)(2,1)}) custom-call(s32[1]{0:T(128)} %bitcast.refs_0_, bf16[1024,2048]{1,0:T(8,128)(2,1)} %shard_map.608.refs_1_, bf16[1024,1024]{1,0:T(8,128)(2,1)} %shard_map.605.refs_1_.refs_2_.refs_3_, bf16[1024,1024]{1,0:T(8,128)(2,1)} %copy-done.3, ...), custom_call_target="tpu_custom_call" | custom-call | flops 1 | bytes 1 | tf_op jit(solution)/shard_map/pallas_call | solution.py:96
  294.0 3.1 shard_map.613.refs_1_.refs_2_
  299.0 15.5 %shard_map.614 = (bf16[1024,1024]{1,0:T(8,128)(2,1)S(1)}, bf16[1024,1024]{1,0:T(8,128)(2,1)S(1)}, bf16[1024,1024]{1,0:T(8,128)(2,1)}) custom-call(s32[1]{0:T(128)} %bitcast.refs_0_, bf16[1024,2048]{1,0:T(8,128)(2,1)} %shard_map.613.refs_1_.refs_2_, bf16[1024,1024]{1,0:T(8,128)(2,1)} %shard_map.605.refs_1_.refs_2_.refs_3_, bf16[1024,1024]{1,0:T(8,128)(2,1)} %copy-done.3, ...), custom_call_target="tpu_custom_call" | custom-call | flops 1 | bytes 1 | tf_op jit(solution)/shard_map/pallas_call | solution.py:96
  317.2 13.9 %shard_map.615 = (bf16[1024,1024]{1,0:T(8,128)(2,1)S(1)}, bf16[1024,1024]{1,0:T(8,128)(2,1)S(1)}) custom-call(s32[8]{0:T(128)S(1)} %pad_add_fusion.3.refs_0_, bf16[1024,2048]{1,0:T(8,128)(2,1)} %shard_map.598.refs_5_.refs_1_, bf16[1024,2048]{1,0:T(8,128)(2,1)} %collective-permute-done.11.refs_6_.refs_2_.refs_1_, bf16[1024,1024]{1,0:T(8,128)(2,1)} %copy-done.16, ...), custom_call_target="tpu_custom_call" | custom-call | flops 1 | bytes 1 | tf_op jit(solution)/shard_map/pallas_call | solution.py:96
  332.6 13.1 %collective-permute-done.17.refs_3_ = bf16[1024,1024]{1,0:T(8,128)(2,1)S(1)} collective-permute-done((bf16[1024,1024]{1,0:T(8,128)(2,1)}, bf16[1024,1024]{1,0:T(8,128)(2,1)S(1)}, u32[]{:S(2)}, u32[]{:S(2)}) %collective-permute-start.17) | collective-permute-done | bytes 2097184 | tf_op jit(solution)/shard_map/ppermute | solution.py:682
  347.1 9.5 %shard_map.616 = (bf16[1024,1024]{1,0:T(8,128)(2,1)S(1)}, bf16[1024,1024]{1,0:T(8,128)(2,1)S(1)}) custom-call(s32[1]{0:T(128)} %bitcast.refs_0_, bf16[1024,2048]{1,0:T(8,128)(2,1)} %collective-permute-done.11.refs_6_.refs_2_.refs_1_, bf16[1024,1024]{1,0:T(8,128)(2,1)} %shard_map.611.refs_6_.refs_2_, bf16[1024,1024]{1,0:T(8,128)(2,1)} %copy-done.91, ...), custom_call_target="tpu_custom_call" | custom-call | flops 1 | bytes 1 | tf_op jit(solution)/shard_map/pallas_call | solution.py:96
  359.2 9.5 %shard_map.617 = (bf16[1024,1024]{1,0:T(8,128)(2,1)S(1)}, bf16[1024,1024]{1,0:T(8,128)(2,1)S(1)}) custom-call(s32[1]{0:T(128)} %bitcast.refs_0_, bf16[1024,2048]{1,0:T(8,128)(2,1)} %shard_map.598.refs_5_.refs_1_, bf16[1024,1024]{1,0:T(8,128)(2,1)} %shard_map.611.refs_6_.refs_2_, bf16[1024,1024]{1,0:T(8,128)(2,1)} %copy-done.91, ...), custom_call_target="tpu_custom_call" | custom-call | flops 1 | bytes 1 | tf_op jit(solution)/shard_map/pallas_call | solution.py:96
  371.4 14.8 %shard_map.618 = (bf16[1024,1024]{1,0:T(8,128)(2,1)}, bf16[1024,1024]{1,0:T(8,128)(2,1)S(1)}) custom-call(s32[8]{0:T(128)S(1)} %pad_add_fusion.3.refs_0_, bf16[1024,2048]{1,0:T(8,128)(2,1)} %shard_map.608.refs_1_, bf16[1024,2048]{1,0:T(8,128)(2,1)} %shard_map.613.refs_1_.refs_2_, bf16[1024,1024]{1,0:T(8,128)(2,1)} %copy-done.37, bf16[1024,1024]{1,0:T(8,128)(2,1)} %copy-done.25), custom_call_target="tpu_custom_call" | custom-call | flops 1 | bytes 1 | tf_op jit(solution)/shard_map/pallas_call | solution.py:96
  394.6 4.9 all-to-all-start.5
  399.5 14.8 %shard_map.619 = (bf16[1024,1024]{1,0:T(8,128)(2,1)}, bf16[1024,1024]{1,0:T(8,128)(2,1)S(1)}) custom-call(s32[8]{0:T(128)S(1)} %pad_add_fusion.3.refs_0_, bf16[1024,2048]{1,0:T(8,128)(2,1)} %shard_map.608.refs_1_, bf16[1024,2048]{1,0:T(8,128)(2,1)} %shard_map.613.refs_1_.refs_2_, bf16[1024,1024]{1,0:T(8,128)(2,1)} %copy-done.46, ...), custom_call_target="tpu_custom_call" | custom-call | flops 1 | bytes 1 | tf_op jit(solution)/shard_map/pallas_call | solution.py:96
  415.6 15.5 %shard_map.620 = (bf16[256,2048]{1,0:T(8,128)(2,1)}, bf16[256,2048]{1,0:T(8,128)(2,1)S(1)}, bf16[256,2048]{1,0:T(8,128)(2,1)S(1)}, bf16[256,2048]{1,0:T(8,128)(2,1)S(1)}) custom-call(s32[1]{0:T(128)} %bitcast.refs_0_, bf16[1024,1024]{1,0:T(8,128)(2,1)} %copy-done.25, bf16[1024,1024]{1,0:T(8,128)(2,1)} %copy-done.55, ...), custom_call_target="tpu_custom_call" | custom-call | flops 1 | bytes 1 | tf_op jit(solution)/shard_map/pallas_call | solution.py:96
  431.7 3.6 collective-permute-done.22.refs_8_.refs_0_
  435.4 14.7 %shard_map.621 = (bf16[256,2048]{1,0:T(8,128)(2,1)S(1)}, bf16[256,2048]{1,0:T(8,128)(2,1)S(1)}, bf16[256,2048]{1,0:T(8,128)(2,1)S(1)}, bf16[256,2048]{1,0:T(8,128)(2,1)S(1)}) custom-call(s32[1]{0:T(128)} %bitcast.refs_0_, bf16[1024,1024]{1,0:T(8,128)(2,1)} %copy-done.37, bf16[1024,1024]{1,0:T(8,128)(2,1)} %copy-done.46, ...), custom_call_target="tpu_custom_call" | custom-call | flops 1 | bytes 1 | tf_op jit(solution)/shard_map/pallas_call | solution.py:96
  456.2 8.7 %shard_map.624.refs_4_.refs_0_.refs_2_ = bf16[1024,2048]{1,0:T(8,128)(2,1)} custom-call(s32[1]{0:T(128)} %bitcast.refs_0_, bf16[1024,1024]{1,0:T(8,128)(2,1)S(1)} %copy-done.36, bf16[1024,1024]{1,0:T(8,128)(2,1)} %shard_map.611.refs_6_.refs_2_, bf16[1024,1024]{1,0:T(8,128)(2,1)} %copy-done.91, bf16[256,2048]{1,0:T(8,128)(2,1)} %shard_map.622.refs_4_, ...), custom_call_target="tpu_custom_call" | custom-call | flops 1 | bytes 1 | tf_op jit(solution)/shard_map/pallas_call | solution.py:96
  465.6 8.5 %shard_map.625.refs_3_.refs_0_.refs_1_ = bf16[1024,2048]{1,0:T(8,128)(2,1)} custom-call(s32[1]{0:T(128)} %bitcast.refs_0_, bf16[1024,1024]{1,0:T(8,128)(2,1)S(1)} %copy-done.17, bf16[1024,1024]{1,0:T(8,128)(2,1)} %shard_map.611.refs_6_.refs_2_, bf16[1024,1024]{1,0:T(8,128)(2,1)} %copy-done.91, bf16[1024,2048]{1,0:T(8,128)(2,1)} %shard_map.624.refs_4_.refs_0_.refs_2_), custom_call_target="tpu_custom_call" | custom-call | flops 1 | bytes 1 | tf_op jit(solution)/shard_map/pallas_call | solution.py:96
  486.1 5.2 all-to-all-start.6
  491.3 7.2 collective-permute-done.32.refs_7_.refs_0_
  499.7 5.6 shard_map.629
  506.8 21.0 %collective-permute-done.33.refs_2_ = bf16[256,2048]{1,0:T(8,128)(2,1)S(1)} collective-permute-done((bf16[256,2048]{1,0:T(8,128)(2,1)S(1)}, bf16[256,2048]{1,0:T(8,128)(2,1)S(1)}, u32[]{:S(2)}, u32[]{:S(2)}) %collective-permute-start.33) | collective-permute-done | bytes 1048608 | tf_op jit(solution)/shard_map/ppermute | solution.py:682
  530.4 3.1 shard_map.630.refs_1_.refs_2_
  533.5 5.9 all-to-all-done.6
  545.1 3.6 all-to-all-start.7
  550.0 7.4 shard_map.631
  558.6 14.4 %shard_map.633 = (bf16[1024,512]{1,0:T(8,128)(2,1)S(1)}, bf16[1024,256]{1,0:T(8,128)(2,1)S(1)}, bf16[1024,256]{1,0:T(8,128)(2,1)S(1)}) custom-call(s32[1]{0:T(128)} %bitcast.refs_0_, bf16[1024,2048]{1,0:T(8,128)(2,1)} %shard_map.630.refs_1_.refs_2_, bf16[1024,512]{1,0:T(8,128)(2,1)S(1)} %bitcast.57, bf16[1024,512]{1,0:T(8,128)(2,1)S(1)} %copy-done.60, ...), custom_call_target="tpu_custom_call" | custom-call | flops 1 | bytes 1 | tf_op jit(solution)/shard_map/pallas_call | solution.py:96
  574.6 10.6 %shard_map.636 = (bf16[1024,1024]{1,0:T(8,128)(2,1)}, bf16[1024,1024]{1,0:T(8,128)(2,1)S(1)}) custom-call(s32[8]{0:T(128)S(1)} %pad_add_fusion.3.refs_0_, bf16[1024,2048]{1,0:T(8,128)(2,1)} %shard_map.591.refs_1_, bf16[1024,1024]{1,0:T(8,128)(2,1)} %copy-done.92), custom_call_target="tpu_custom_call" | custom-call | flops 1 | bytes 1 | tf_op jit(solution)/shard_map/pallas_call | solution.py:96
  588.3 10.7 %shard_map.637 = (bf16[256,2048]{1,0:T(8,128)(2,1)}, bf16[256,2048]{1,0:T(8,128)(2,1)}, bf16[256,2048]{1,0:T(8,128)(2,1)S(1)}, bf16[256,2048]{1,0:T(8,128)(2,1)S(1)}) custom-call(s32[1]{0:T(128)} %bitcast.refs_0_, bf16[1024,1024]{1,0:T(8,128)(2,1)} %copy-done.92, bf16[1024,1024]{1,0:T(8,128)(2,1)} %bitcast.45, ...), custom_call_target="tpu_custom_call" | custom-call | flops 1 | bytes 1 | tf_op jit(solution)/shard_map/pallas_call | solution.py:96
  608.5 5.0 all-to-all-start.8
  613.6 4.3 shard_map.634
  619.9 13.6 %collective-permute-done.41.refs_3_.refs_0_ = bf16[1024,1024]{1,0:T(8,128)(2,1)} collective-permute-done((bf16[1024,1024]{1,0:T(8,128)(2,1)}, bf16[1024,1024]{1,0:T(8,128)(2,1)}, u32[]{:S(2)}, u32[]{:S(2)}) %collective-permute-start.41) | collective-permute-done | bytes 2097184 | tf_op jit(solution)/shard_map/ppermute | solution.py:682
  633.5 4.9 all-to-all-done.8
  642.8 4.6 all-to-all-start.9
  648.0 20.6 %collective-permute-done.36.refs_2_.refs_3_ = bf16[512,2048]{1,0:T(8,128)(2,1)} collective-permute-done((bf16[512,2048]{1,0:T(8,128)(2,1)}, bf16[512,2048]{1,0:T(8,128)(2,1)}, u32[]{:S(2)}, u32[]{:S(2)}) %collective-permute-start.36) | collective-permute-done | bytes 2097184 | tf_op jit(solution)/shard_map/ppermute | solution.py:682
  679.4 7.2 collective-permute-done.42.refs_2_
  686.6 4.9 shard_map.643
  691.4 6.4 collective-permute-done.38.refs_4_
  697.8 4.0 shard_map.644.refs_1_
  717.5 3.4 collective-permute-done.46
  721.2 3.5 collective-permute-done.47
  727.9 7.0 add_multiply_fusion.1
  735.0 4.0 add_multiply_fusion.2
  744.1 3.8 add_multiply_fusion
  (370 shorter events, 169.0 us)
Async XLA Ops:
  6.1 54.6 %all-to-all-start = ((bf16[4,256,1024]{2,1,0:T(8,128)(2,1)}), bf16[4,256,1024]{2,1,0:T(8,128)(2,1)S(1)}, u32[]{:S(2)}, u32[]{:S(2)}) async-start(bf16[4,256,1024]{2,1,0:T(8,128)(2,1)} %bitcast.60), calls=%async_computation | async-start | bytes 4194304 | tf_op jit(solution)/shard_map/all_to_all | solution.py:700
  12.5 49.8 %copy-start.68 = (f32[256,512]{1,0:T(8,128)S(1)}, f32[256,512]{1,0:T(8,128)}, u32[]{:S(2)}) copy-start(f32[256,512]{1,0:T(8,128)} %refs_0_.10) | copy-start | bytes 1572868
  12.5 51.7 %collective-permute-start = (bf16[256,2048]{1,0:T(8,128)(2,1)}, bf16[256,2048]{1,0:T(8,128)(2,1)}, u32[]{:S(2)}, u32[]{:S(2)}) collective-permute-start(bf16[256,2048]{1,0:T(8,128)(2,1)} %shard_map.589.refs_1_.refs_3_), channel_id=1, source_target_pairs={{0,2},{1,3},{2,0},{3,1},{4,6},{5,7},{6,4},{7,5},{8,10},{9,11},{10,... | collective-permute-start | bytes 3145736 | tf_op jit(solution)/shard_map/ppermute | solution.py:682
  16.9 54.2 %collective-permute-start.1 = (bf16[256,2048]{1,0:T(8,128)(2,1)}, bf16[256,2048]{1,0:T(8,128)(2,1)}, u32[]{:S(2)}, u32[]{:S(2)}) collective-permute-start(bf16[256,2048]{1,0:T(8,128)(2,1)} %broadcast_select_fusion.refs_1_.refs_5_), channel_id=1, source_target_pairs={{0,8},{1,9},{2,10},{3,11},{4,12},{5,13},{6,14},{7,15},{8,0},{9,1},... | collective-permute-start | bytes 3145736 | tf_op jit(solution)/shard_map/ppermute | solution.py:682
  60.8 46.6 %collective-permute-start.4 = (bf16[1024,1024]{1,0:T(8,128)(2,1)S(1)}, bf16[1024,1024]{1,0:T(8,128)(2,1)}, u32[]{:S(2)}, u32[]{:S(2)}) collective-permute-start(bf16[1024,1024]{1,0:T(8,128)(2,1)S(1)} %bitcast.42), channel_id=1, source_target_pairs={{0,4},{1,5},{2,6},{3,7},{4,0},{5,1},{6,2},{7,3},{8,12},{9,13},{10,... | collective-permute-start | bytes 6291464 | tf_op jit(solution)/shard_map/ppermute | solution.py:682
  66.0 28.4 %all-to-all-start.1 = ((bf16[4,256,512]{2,1,0:T(8,128)(2,1)}), bf16[4,256,512]{2,1,0:T(8,128)(2,1)S(1)}, u32[]{:S(2)}, u32[]{:S(2)}) async-start(bf16[4,256,512]{2,1,0:T(8,128)(2,1)} %bitcast.64), calls=%async_computation.1 | async-start | bytes 2097152 | tf_op jit(solution)/shard_map/all_to_all | solution.py:700
  69.5 8.4 %collective-permute-start.2 = (bf16[256,2048]{1,0:T(8,128)(2,1)}, bf16[256,2048]{1,0:T(8,128)(2,1)}, u32[]{:S(2)}, u32[]{:S(2)}) collective-permute-start(bf16[256,2048]{1,0:T(8,128)(2,1)} %shard_map.589.refs_1_.refs_3_), channel_id=1, source_target_pairs={{0,1},{1,0},{2,3},{3,2},{4,5},{5,4},{6,7},{7,6},{8,9},{9,8},{10,11... | collective-permute-start | bytes 3145736 | tf_op jit(solution)/shard_map/ppermute | solution.py:682
  71.1 6.8 collective-permute-start.3
  71.1 48.4 %collective-permute-start.6 = (bf16[256,2048]{1,0:T(8,128)(2,1)}, bf16[256,2048]{1,0:T(8,128)(2,1)}, u32[]{:S(2)}, u32[]{:S(2)}) collective-permute-start(bf16[256,2048]{1,0:T(8,128)(2,1)} %broadcast_select_fusion.refs_1_.refs_5_), channel_id=1, source_target_pairs={{0,2},{1,3},{2,0},{3,1},{4,6},{5,7},{6,4},{7,5},{8,10},{9,11},{10,... | collective-permute-start | bytes 3145736 | tf_op jit(solution)/shard_map/ppermute | solution.py:682
  72.6 46.9 %collective-permute-start.7 = (bf16[256,2048]{1,0:T(8,128)(2,1)}, bf16[256,2048]{1,0:T(8,128)(2,1)}, u32[]{:S(2)}, u32[]{:S(2)}) collective-permute-start(bf16[256,2048]{1,0:T(8,128)(2,1)} %collective-permute-done.1.refs_1_.refs_3_), channel_id=1, source_target_pairs={{0,2},{1,3},{2,0},{3,1},{4,6},{5,7},{6,4},{7,5},{8,10},{9,11},{10,... | collective-permute-start | bytes 3145736 | tf_op jit(solution)/shard_map/ppermute | solution.py:682
  94.4 30.5 %copy-start.14 = (bf16[4,256,512]{2,1,0:T(8,128)(2,1)}, bf16[4,256,512]{2,1,0:T(8,128)(2,1)S(1)}, u32[]{:S(2)}) copy-start(bf16[4,256,512]{2,1,0:T(8,128)(2,1)S(1)} %all-to-all-done.1) | copy-start | bytes 3145732
  97.7 65.6 %all-to-all-start.2 = ((bf16[4,256,1024]{2,1,0:T(8,128)(2,1)}), bf16[4,256,1024]{2,1,0:T(8,128)(2,1)}, u32[]{:S(2)}, u32[]{:S(2)}) async-start(bf16[4,256,1024]{2,1,0:T(8,128)(2,1)} %bitcast.61), calls=%async_computation.2 | async-start | bytes 4194304 | tf_op jit(solution)/shard_map/all_to_all | solution.py:700
  124.9 63.8 %collective-permute-start.11 = (bf16[1024,2048]{1,0:T(8,128)(2,1)}, bf16[1024,2048]{1,0:T(8,128)(2,1)}, u32[]{:S(2)}, u32[]{:S(2)}) collective-permute-start(bf16[1024,2048]{1,0:T(8,128)(2,1)} %shard_map.598.refs_5_.refs_1_), channel_id=1, source_target_pairs={{0,1},{1,0},{2,3},{3,2},{4,5},{5,4},{6,7},{7,6},{8,9},{9,8},{10,11... | collective-permute-start | bytes 12582920 | tf_op jit(solution)/shard_map/ppermute | solution.py:682
  124.9 25.7 %collective-permute-start.5 = (bf16[1024,512]{1,0:T(8,128)(2,1)S(1)}, bf16[1024,512]{1,0:T(8,128)(2,1)S(1)}, u32[]{:S(2)}, u32[]{:S(2)}) collective-permute-start(bf16[1024,512]{1,0:T(8,128)(2,1)S(1)} %bitcast.55), channel_id=1, source_target_pairs={{0,4},{1,5},{2,6},{3,7},{4,0},{5,1},{6,2},{7,3},{8,12},{9,13},{10,... | collective-permute-start | bytes 3145736 | tf_op jit(solution)/shard_map/ppermute | solution.py:682
  134.4 23.5 %copy-start.33 = (bf16[1024,512]{1,0:T(8,128)(2,1)}, bf16[1024,512]{1,0:T(8,128)(2,1)S(1)}, u32[]{:S(2)}) copy-start(bf16[1024,512]{1,0:T(8,128)(2,1)S(1)} %shard_map.597.refs_1_.refs_2_) | copy-start | bytes 3145732
  158.8 4.1 collective-permute-start.9
  158.8 16.1 %collective-permute-start.8 = (bf16[256,2048]{1,0:T(8,128)(2,1)}, bf16[256,2048]{1,0:T(8,128)(2,1)}, u32[]{:S(2)}, u32[]{:S(2)}) collective-permute-start(bf16[256,2048]{1,0:T(8,128)(2,1)} %get-tuple-element.96), channel_id=1, source_target_pairs={{0,1},{1,0},{2,3},{3,2},{4,5},{5,4},{6,7},{7,6},{8,9},{9,8},{10,11... | collective-permute-start | bytes 3145736 | tf_op jit(solution)/shard_map/ppermute | solution.py:682
  163.3 25.4 %collective-permute-start.10 = (bf16[256,2048]{1,0:T(8,128)(2,1)S(1)}, bf16[256,2048]{1,0:T(8,128)(2,1)}, u32[]{:S(2)}, u32[]{:S(2)}) collective-permute-start(bf16[256,2048]{1,0:T(8,128)(2,1)S(1)} %shard_map.600.refs_1_), channel_id=1, source_target_pairs={{0,2},{1,3},{2,0},{3,1},{4,6},{5,7},{6,4},{7,5},{8,10},{9,11},{10,... | collective-permute-start | bytes 3145736 | tf_op jit(solution)/shard_map/ppermute | solution.py:682
  166.2 55.7 %all-to-all-start.3 = ((bf16[4,256,1024]{2,1,0:T(8,128)(2,1)}), bf16[4,256,1024]{2,1,0:T(8,128)(2,1)S(1)}, u32[]{:S(2)}, u32[]{:S(2)}) async-start(bf16[4,256,1024]{2,1,0:T(8,128)(2,1)} %bitcast.41), calls=%async_computation.3 | async-start | bytes 4194304 | tf_op jit(solution)/shard_map/all_to_all | solution.py:700
  171.6 17.1 %copy-start.90 = (f32[2048]{0:T(1024)S(1)}, f32[2048]{0:T(1024)}, u32[]{:S(2)}) copy-start(f32[2048]{0:T(1024)} %param.41) | copy-start | bytes 24580
  173.2 47.4 %collective-permute-start.15 = (bf16[1024,1024]{1,0:T(8,128)(2,1)}, bf16[1024,1024]{1,0:T(8,128)(2,1)S(1)}, u32[]{:S(2)}, u32[]{:S(2)}) collective-permute-start(bf16[1024,1024]{1,0:T(8,128)(2,1)} %shard_map.605.refs_1_.refs_2_.refs_3_), channel_id=1, source_target_pairs={{0,4},{1,5},{2,6},{3,7},{4,0},{5,1},{6,2},{7,3},{8,12},{9,13},{10,... | collective-permute-start | bytes 6291464 | tf_op jit(solution)/shard_map/ppermute | solution.py:682
  192.9 24.8 %collective-permute-start.12 = (bf16[256,2048]{1,0:T(8,128)(2,1)}, bf16[256,2048]{1,0:T(8,128)(2,1)}, u32[]{:S(2)}, u32[]{:S(2)}) collective-permute-start(bf16[256,2048]{1,0:T(8,128)(2,1)} %get-tuple-element.100.refs_1_), channel_id=1, source_target_pairs={{0,2},{1,9},{2,0},{3,11},{4,6},{5,13},{6,4},{7,15},{8,10},{9,1},{1... | collective-permute-start | bytes 3145736 | tf_op jit(solution)/shard_map/ppermute | solution.py:682
  194.4 34.3 %collective-permute-start.13 = (bf16[256,2048]{1,0:T(8,128)(2,1)}, bf16[256,2048]{1,0:T(8,128)(2,1)}, u32[]{:S(2)}, u32[]{:S(2)}) collective-permute-start(bf16[256,2048]{1,0:T(8,128)(2,1)} %get-tuple-element.100.refs_1_), channel_id=1, source_target_pairs={{0,8},{1,3},{2,10},{3,1},{4,12},{5,7},{6,14},{7,5},{8,0},{9,11},{1... | collective-permute-start | bytes 3145736 | tf_op jit(solution)/shard_map/ppermute | solution.py:682
  217.7 22.2 %collective-permute-start.14 = (bf16[256,2048]{1,0:T(8,128)(2,1)}, bf16[256,2048]{1,0:T(8,128)(2,1)S(1)}, u32[]{:S(2)}, u32[]{:S(2)}) collective-permute-start(bf16[256,2048]{1,0:T(8,128)(2,1)} %collective-permute-done.12.refs_1_.refs_2_), channel_id=1, source_target_pairs={{0,8},{1,3},{2,10},{3,1},{4,12},{5,7},{6,14},{7,5},{8,0},{9,11},{1... | collective-permute-start | bytes 3145736 | tf_op jit(solution)/shard_map/ppermute | solution.py:682
  223.5 42.1 %collective-permute-start.16 = (bf16[1024,1024]{1,0:T(8,128)(2,1)S(1)}, bf16[1024,1024]{1,0:T(8,128)(2,1)}, u32[]{:S(2)}, u32[]{:S(2)}) collective-permute-start(bf16[1024,1024]{1,0:T(8,128)(2,1)S(1)} %shard_map.607.refs_4_.refs_1_.refs_5_), channel_id=1, source_target_pairs={{0,4},{1,5},{2,6},{3,7},{4,0},{5,1},{6,2},{7,3},{8,12},{9,13},{10,... | collective-permute-start | bytes 6291464 | tf_op jit(solution)/shard_map/ppermute | solution.py:682
  241.1 56.0 %all-to-all-start.4 = ((bf16[4,256,1024]{2,1,0:T(8,128)(2,1)}), bf16[4,256,1024]{2,1,0:T(8,128)(2,1)}, u32[]{:S(2)}, u32[]{:S(2)}) async-start(bf16[4,256,1024]{2,1,0:T(8,128)(2,1)} %bitcast.52), calls=%async_computation.4 | async-start | bytes 4194304 | tf_op jit(solution)/shard_map/all_to_all | solution.py:700
  245.8 48.2 %collective-permute-start.18 = (bf16[256,2048]{1,0:T(8,128)(2,1)}, bf16[256,2048]{1,0:T(8,128)(2,1)S(1)}, u32[]{:S(2)}, u32[]{:S(2)}) collective-permute-start(bf16[256,2048]{1,0:T(8,128)(2,1)} %get-tuple-element.100.refs_1_), channel_id=1, source_target_pairs={{0,1},{1,0},{2,3},{3,2},{4,5},{5,4},{6,7},{7,6},{8,9},{9,8},{10,11... | collective-permute-start | bytes 3145736 | tf_op jit(solution)/shard_map/ppermute | solution.py:682
  246.9 47.1 %collective-permute-start.20 = (bf16[256,2048]{1,0:T(8,128)(2,1)}, bf16[256,2048]{1,0:T(8,128)(2,1)S(1)}, u32[]{:S(2)}, u32[]{:S(2)}) collective-permute-start(bf16[256,2048]{1,0:T(8,128)(2,1)} %collective-permute-done.13.refs_3_), channel_id=1, source_target_pairs={{0,1},{1,0},{2,3},{3,2},{4,5},{5,4},{6,7},{7,6},{8,9},{9,8},{10,11... | collective-permute-start | bytes 3145736 | tf_op jit(solution)/shard_map/ppermute | solution.py:682
  270.5 23.5 %collective-permute-start.19 = (bf16[256,2048]{1,0:T(8,128)(2,1)}, bf16[256,2048]{1,0:T(8,128)(2,1)S(1)}, u32[]{:S(2)}, u32[]{:S(2)}) collective-permute-start(bf16[256,2048]{1,0:T(8,128)(2,1)} %collective-permute-done.12.refs_1_.refs_2_), channel_id=1, source_target_pairs={{0,1},{1,0},{2,3},{3,2},{4,5},{5,4},{6,7},{7,6},{8,9},{9,8},{10,11... | collective-permute-start | bytes 3145736 | tf_op jit(solution)/shard_map/ppermute | solution.py:682
  277.1 16.9 %collective-permute-start.21 = (bf16[256,2048]{1,0:T(8,128)(2,1)S(1)}, bf16[256,2048]{1,0:T(8,128)(2,1)S(1)}, u32[]{:S(2)}, u32[]{:S(2)}) collective-permute-start(bf16[256,2048]{1,0:T(8,128)(2,1)S(1)} %shard_map.612), channel_id=1, source_target_pairs={{0,1},{1,0},{2,3},{3,2},{4,5},{5,4},{6,7},{7,6},{8,9},{9,8},{10,11... | collective-permute-start | bytes 3145736 | tf_op jit(solution)/shard_map/ppermute | solution.py:682
  297.1 48.6 %collective-permute-start.17 = (bf16[1024,1024]{1,0:T(8,128)(2,1)}, bf16[1024,1024]{1,0:T(8,128)(2,1)S(1)}, u32[]{:S(2)}, u32[]{:S(2)}) collective-permute-start(bf16[1024,1024]{1,0:T(8,128)(2,1)} %shard_map.611.refs_6_.refs_2_), channel_id=1, source_target_pairs={{0,4},{1,5},{2,6},{3,7},{4,0},{5,1},{6,2},{7,3},{8,12},{9,13},{10,... | collective-permute-start | bytes 6291464 | tf_op jit(solution)/shard_map/ppermute | solution.py:682
  332.4 58.4 %collective-permute-start.27 = (bf16[1024,1024]{1,0:T(8,128)(2,1)S(1)}, bf16[1024,1024]{1,0:T(8,128)(2,1)S(1)}, u32[]{:S(2)}, u32[]{:S(2)}) collective-permute-start(bf16[1024,1024]{1,0:T(8,128)(2,1)S(1)} %get-tuple-element.122), channel_id=1, source_target_pairs={{0,4},{1,5},{2,6},{3,7},{4,0},{5,1},{6,2},{7,3},{8,12},{9,13},{10,... | collective-permute-start | bytes 6291464 | tf_op jit(solution)/shard_map/ppermute | solution.py:682
  387.6 47.7 %collective-permute-start.22 = (bf16[1024,1024]{1,0:T(8,128)(2,1)}, bf16[1024,1024]{1,0:T(8,128)(2,1)}, u32[]{:S(2)}, u32[]{:S(2)}) collective-permute-start(bf16[1024,1024]{1,0:T(8,128)(2,1)} %get-tuple-element.115), channel_id=1, source_target_pairs={{0,4},{1,5},{2,6},{3,7},{4,0},{5,1},{6,2},{7,3},{8,12},{9,13},{10,... | collective-permute-start | bytes 6291464 | tf_op jit(solution)/shard_map/ppermute | solution.py:682
  394.6 80.5 %all-to-all-start.5 = ((bf16[4,256,1024]{2,1,0:T(8,128)(2,1)}), bf16[4,256,1024]{2,1,0:T(8,128)(2,1)S(1)}, u32[]{:S(2)}, u32[]{:S(2)}) async-start(bf16[4,256,1024]{2,1,0:T(8,128)(2,1)} %bitcast.66), calls=%async_computation.5 | async-start | bytes 4194304 | tf_op jit(solution)/shard_map/all_to_all | solution.py:700
  431.1 19.9 %collective-permute-start.24 = (bf16[256,2048]{1,0:T(8,128)(2,1)S(1)}, bf16[256,2048]{1,0:T(8,128)(2,1)S(1)}, u32[]{:S(2)}, u32[]{:S(2)}) collective-permute-start(bf16[256,2048]{1,0:T(8,128)(2,1)S(1)} %get-tuple-element.119), channel_id=1, source_target_pairs={{0,1},{1,0},{2,3},{3,2},{4,5},{5,4},{6,7},{7,6},{8,9},{9,8},{10,11... | collective-permute-start | bytes 3145736 | tf_op jit(solution)/shard_map/ppermute | solution.py:682
  431.1 23.4 %collective-permute-start.23 = (bf16[256,2048]{1,0:T(8,128)(2,1)S(1)}, bf16[256,2048]{1,0:T(8,128)(2,1)S(1)}, u32[]{:S(2)}, u32[]{:S(2)}) collective-permute-start(bf16[256,2048]{1,0:T(8,128)(2,1)S(1)} %get-tuple-element.117), channel_id=1, source_target_pairs={{0,1},{1,0},{2,3},{3,2},{4,5},{5,4},{6,7},{7,6},{8,9},{9,8},{10,11... | collective-permute-start | bytes 3145736 | tf_op jit(solution)/shard_map/ppermute | solution.py:682
  431.6 42.5 %collective-permute-start.25 = (bf16[256,2048]{1,0:T(8,128)(2,1)S(1)}, bf16[256,2048]{1,0:T(8,128)(2,1)S(1)}, u32[]{:S(2)}, u32[]{:S(2)}) collective-permute-start(bf16[256,2048]{1,0:T(8,128)(2,1)S(1)} %get-tuple-element.121), channel_id=1, source_target_pairs={{0,1},{1,0},{2,3},{3,2},{4,5},{5,4},{6,7},{7,6},{8,9},{9,8},{10,11... | collective-permute-start | bytes 3145736 | tf_op jit(solution)/shard_map/ppermute | solution.py:682
  451.3 23.8 %collective-permute-start.26 = (bf16[256,2048]{1,0:T(8,128)(2,1)S(1)}, bf16[256,2048]{1,0:T(8,128)(2,1)}, u32[]{:S(2)}, u32[]{:S(2)}) collective-permute-start(bf16[256,2048]{1,0:T(8,128)(2,1)S(1)} %shard_map.623.refs_5_), channel_id=1, source_target_pairs={{0,8},{1,3},{2,10},{3,1},{4,12},{5,7},{6,14},{7,5},{8,0},{9,11},{1... | collective-permute-start | bytes 3145736 | tf_op jit(solution)/shard_map/ppermute | solution.py:682
  452.8 45.7 %collective-permute-start.32 = (bf16[1024,1024]{1,0:T(8,128)(2,1)}, bf16[1024,1024]{1,0:T(8,128)(2,1)}, u32[]{:S(2)}, u32[]{:S(2)}) collective-permute-start(bf16[1024,1024]{1,0:T(8,128)(2,1)} %get-tuple-element.124), channel_id=1, source_target_pairs={{0,4},{1,5},{2,6},{3,7},{4,0},{5,1},{6,2},{7,3},{8,12},{9,13},{10,... | collective-permute-start | bytes 6291464 | tf_op jit(solution)/shard_map/ppermute | solution.py:682
  456.2 35.1 %collective-permute-start.29 = (bf16[256,2048]{1,0:T(8,128)(2,1)}, bf16[256,2048]{1,0:T(8,128)(2,1)}, u32[]{:S(2)}, u32[]{:S(2)}) collective-permute-start(bf16[256,2048]{1,0:T(8,128)(2,1)} %get-tuple-element.114.refs_7_), channel_id=1, source_target_pairs={{0,1},{1,0},{2,3},{3,2},{4,5},{5,4},{6,7},{7,6},{8,9},{9,8},{10,11... | collective-permute-start | bytes 3145736 | tf_op jit(solution)/shard_map/ppermute | solution.py:682
  464.9 33.6 %collective-permute-start.30 = (bf16[256,2048]{1,0:T(8,128)(2,1)}, bf16[256,2048]{1,0:T(8,128)(2,1)}, u32[]{:S(2)}, u32[]{:S(2)}) collective-permute-start(bf16[256,2048]{1,0:T(8,128)(2,1)} %shard_map.622.refs_4_), channel_id=1, source_target_pairs={{0,8},{1,3},{2,10},{3,1},{4,12},{5,7},{6,14},{7,5},{8,0},{9,11},{1... | collective-permute-start | bytes 3145736 | tf_op jit(solution)/shard_map/ppermute | solution.py:682
  481.1 17.4 %collective-permute-start.31 = (bf16[256,2048]{1,0:T(8,128)(2,1)S(1)}, bf16[256,2048]{1,0:T(8,128)(2,1)}, u32[]{:S(2)}, u32[]{:S(2)}) collective-permute-start(bf16[256,2048]{1,0:T(8,128)(2,1)S(1)} %shard_map.627.refs_1_), channel_id=1, source_target_pairs={{0,2},{1,9},{2,0},{3,11},{4,6},{5,13},{6,4},{7,15},{8,10},{9,1},{1... | collective-permute-start | bytes 3145736 | tf_op jit(solution)/shard_map/ppermute | solution.py:682
  486.1 53.3 %all-to-all-start.6 = ((bf16[4,256,1024]{2,1,0:T(8,128)(2,1)}), bf16[4,256,1024]{2,1,0:T(8,128)(2,1)S(1)}, u32[]{:S(2)}, u32[]{:S(2)}) async-start(bf16[4,256,1024]{2,1,0:T(8,128)(2,1)} %bitcast.68), calls=%async_computation.6 | async-start | bytes 4194304 | tf_op jit(solution)/shard_map/all_to_all | solution.py:700
  505.3 22.4 %collective-permute-start.33 = (bf16[256,2048]{1,0:T(8,128)(2,1)S(1)}, bf16[256,2048]{1,0:T(8,128)(2,1)S(1)}, u32[]{:S(2)}, u32[]{:S(2)}) collective-permute-start(bf16[256,2048]{1,0:T(8,128)(2,1)S(1)} %get-tuple-element.125.refs_1_), channel_id=1, source_target_pairs={{0,2},{1,3},{2,0},{3,1},{4,6},{5,7},{6,4},{7,5},{8,10},{9,11},{10,... | collective-permute-start | bytes 3145736 | tf_op jit(solution)/shard_map/ppermute | solution.py:682
  506.8 21.0 %collective-permute-start.34 = (bf16[256,2048]{1,0:T(8,128)(2,1)S(1)}, bf16[256,2048]{1,0:T(8,128)(2,1)S(1)}, u32[]{:S(2)}, u32[]{:S(2)}) collective-permute-start(bf16[256,2048]{1,0:T(8,128)(2,1)S(1)} %get-tuple-element.125.refs_1_), channel_id=1, source_target_pairs={{0,1},{1,0},{2,3},{3,2},{4,5},{5,4},{6,7},{7,6},{8,9},{9,8},{10,11... | collective-permute-start | bytes 3145736 | tf_op jit(solution)/shard_map/ppermute | solution.py:682
  527.8 2.7 collective-permute-start.35
  545.1 56.8 %all-to-all-start.7 = ((bf16[4,256,1024]{2,1,0:T(8,128)(2,1)}), bf16[4,256,1024]{2,1,0:T(8,128)(2,1)S(1)}, u32[]{:S(2)}, u32[]{:S(2)}) async-start(bf16[4,256,1024]{2,1,0:T(8,128)(2,1)} %bitcast.67), calls=%async_computation.7 | async-start | bytes 4194304 | tf_op jit(solution)/shard_map/all_to_all | solution.py:700
  548.8 64.8 %collective-permute-start.28 = (bf16[1024,2048]{1,0:T(8,128)(2,1)}, bf16[1024,2048]{1,0:T(8,128)(2,1)}, u32[]{:S(2)}, u32[]{:S(2)}) collective-permute-start(bf16[1024,2048]{1,0:T(8,128)(2,1)} %shard_map.628), channel_id=1, source_target_pairs={{0,1},{1,0},{2,3},{3,2},{4,5},{5,4},{6,7},{7,6},{8,9},{9,8},{10,11... | collective-permute-start | bytes 12582920 | tf_op jit(solution)/shard_map/ppermute | solution.py:682
  558.3 30.0 %collective-permute-start.37 = (bf16[1024,512]{1,0:T(8,128)(2,1)S(1)}, bf16[1024,512]{1,0:T(8,128)(2,1)S(1)}, u32[]{:S(2)}, u32[]{:S(2)}) collective-permute-start(bf16[1024,512]{1,0:T(8,128)(2,1)S(1)} %get-tuple-element.128), channel_id=1, source_target_pairs={{0,4},{1,5},{2,6},{3,7},{4,0},{5,1},{6,2},{7,3},{8,12},{9,13},{10,... | collective-permute-start | bytes 3145736 | tf_op jit(solution)/shard_map/ppermute | solution.py:682
  586.5 47.0 %collective-permute-start.41 = (bf16[1024,1024]{1,0:T(8,128)(2,1)}, bf16[1024,1024]{1,0:T(8,128)(2,1)}, u32[]{:S(2)}, u32[]{:S(2)}) collective-permute-start(bf16[1024,1024]{1,0:T(8,128)(2,1)} %get-tuple-element.136), channel_id=1, source_target_pairs={{0,4},{1,5},{2,6},{3,7},{4,0},{5,1},{6,2},{7,3},{8,12},{9,13},{10,... | collective-permute-start | bytes 6291464 | tf_op jit(solution)/shard_map/ppermute | solution.py:682
  608.5 29.9 %all-to-all-start.8 = ((bf16[4,256,512]{2,1,0:T(8,128)(2,1)}), bf16[4,256,512]{2,1,0:T(8,128)(2,1)S(1)}, u32[]{:S(2)}, u32[]{:S(2)}) async-start(bf16[4,256,512]{2,1,0:T(8,128)(2,1)} %bitcast.26), calls=%async_computation.8 | async-start | bytes 2097152 | tf_op jit(solution)/shard_map/all_to_all | solution.py:700
  617.9 50.7 %collective-permute-start.36 = (bf16[512,2048]{1,0:T(8,128)(2,1)}, bf16[512,2048]{1,0:T(8,128)(2,1)}, u32[]{:S(2)}, u32[]{:S(2)}) collective-permute-start(bf16[512,2048]{1,0:T(8,128)(2,1)} %shard_map.634), channel_id=1, source_target_pairs={{0,8},{1,3},{2,10},{3,1},{4,12},{5,7},{6,14},{7,5},{8,0},{9,11},{1... | collective-permute-start | bytes 6291464 | tf_op jit(solution)/shard_map/ppermute | solution.py:682
  642.8 60.0 %all-to-all-start.9 = ((bf16[4,256,1024]{2,1,0:T(8,128)(2,1)}), bf16[4,256,1024]{2,1,0:T(8,128)(2,1)}, u32[]{:S(2)}, u32[]{:S(2)}) async-start(bf16[4,256,1024]{2,1,0:T(8,128)(2,1)} %bitcast.65), calls=%async_computation.9 | async-start | bytes 4194304 | tf_op jit(solution)/shard_map/all_to_all | solution.py:700
  647.4 23.9 %collective-permute-start.40 = (bf16[256,2048]{1,0:T(8,128)(2,1)}, bf16[256,2048]{1,0:T(8,128)(2,1)S(1)}, u32[]{:S(2)}, u32[]{:S(2)}) collective-permute-start(bf16[256,2048]{1,0:T(8,128)(2,1)} %get-tuple-element.135), channel_id=1, source_target_pairs={{0,1},{1,0},{2,3},{3,2},{4,5},{5,4},{6,7},{7,6},{8,9},{9,8},{10,11... | collective-permute-start | bytes 3145736 | tf_op jit(solution)/shard_map/ppermute | solution.py:682
  647.5 23.8 %copy-start.85 = (bf16[256,2048]{1,0:T(8,128)(2,1)S(1)}, bf16[256,2048]{1,0:T(8,128)(2,1)}, u32[]{:S(2)}) copy-start(bf16[256,2048]{1,0:T(8,128)(2,1)} %copy-done.84) | copy-start | bytes 3145732
  647.5 31.9 %collective-permute-start.39 = (bf16[256,2048]{1,0:T(8,128)(2,1)}, bf16[256,2048]{1,0:T(8,128)(2,1)S(1)}, u32[]{:S(2)}, u32[]{:S(2)}) collective-permute-start(bf16[256,2048]{1,0:T(8,128)(2,1)} %get-tuple-element.133), channel_id=1, source_target_pairs={{0,1},{1,0},{2,3},{3,2},{4,5},{5,4},{6,7},{7,6},{8,9},{9,8},{10,11... | collective-permute-start | bytes 3145736 | tf_op jit(solution)/shard_map/ppermute | solution.py:682
  671.7 14.9 %collective-permute-start.42 = (bf16[256,2048]{1,0:T(8,128)(2,1)S(1)}, bf16[256,2048]{1,0:T(8,128)(2,1)S(1)}, u32[]{:S(2)}, u32[]{:S(2)}) collective-permute-start(bf16[256,2048]{1,0:T(8,128)(2,1)S(1)} %shard_map.640.refs_1_), channel_id=1, source_target_pairs={{0,2},{1,3},{2,0},{3,1},{4,6},{5,7},{6,4},{7,5},{8,10},{9,11},{10,... | collective-permute-start | bytes 3145736 | tf_op jit(solution)/shard_map/ppermute | solution.py:682
  672.9 24.8 %collective-permute-start.38 = (bf16[256,2048]{1,0:T(8,128)(2,1)S(1)}, bf16[256,2048]{1,0:T(8,128)(2,1)S(1)}, u32[]{:S(2)}, u32[]{:S(2)}) collective-permute-start(bf16[256,2048]{1,0:T(8,128)(2,1)S(1)} %shard_map.639.refs_2_), channel_id=1, source_target_pairs={{0,2},{1,9},{2,0},{3,11},{4,6},{5,13},{6,4},{7,15},{8,10},{9,1},{1... | collective-permute-start | bytes 3145736 | tf_op jit(solution)/shard_map/ppermute | solution.py:682
  701.8 26.1 %copy-start.45 = (f32[256,2048]{1,0:T(8,128)S(1)}, f32[256,2048]{1,0:T(8,128)}, u32[]{:S(2)}) copy-start(f32[256,2048]{1,0:T(8,128)} %refs_0_.11) | copy-start | bytes 6291460
  706.5 2.2 collective-permute-start.43
  708.6 3.8 collective-permute-start.44
  712.4 4.7 collective-permute-start.45
  717.1 3.8 collective-permute-start.46
  720.9 3.8 collective-permute-start.47
  (106 other events, 374.3 us)
